TPU v7x, 256 devices: a whole 4x4x8 slice. The times are simulated.
256 devices in a mesh: bump: 4 (over y), nx: 16 (over x_lo, z), ny: 4 (over x_hi, core).
Axes of the slice: x: 4 (x_hi: 2, x_lo: 2; x = x_hi * 2 + x_lo), y: 4, z: 8, core: 2. Of those that a mesh axis runs over, the one named last changes fastest.
Arguments:
- payoff: float32 [2097152], P(('nx', 'ny')), may hold values from -6 to 6
- positions: float32 [2097152], P(('nx', 'ny')), may hold values from -20 to 20
- tables: float32 [8, 5, 2097152], P('bump', None, ('nx', 'ny')), may hold values from 0.02 to 1, as said below
- offsets: int32 [8, 8192], P(None, ('nx', 'ny')), may hold values from -1 to 1
- vol_curve: float32 [8], replicated, may hold values from 0.5 to 1.2
- bucket: int32 [64], P('bump'), may hold values from 0 to 7
- bump_size: float32 [64], P('bump'), may hold values from 0.1 to 0.4
Outputs:
- bumped_values: float32 [64, 2097152], P('bump', ('nx', 'ny'))
- vega: float32 [64], P('bump')
Inputs may be any that keep to these rules, and one draw needn't show every extreme that they name: `tables`: component 0 lies in [0.9, 1], components 1 and 3 in [0.1, 0.2], components 2 and 4 in [0.02, 0.06].
All inputs are finite; a program needn't handle non-finite values.
Results may differ from a plain program's by a relative error of at most 0.0003.
Values sent between devices are 32-bit elements; how exact they have to be, the bound alone decides.
No kernel may reach another device: no remote copies, remote signals or barrier semaphores. Data moves between devices by JAX's collectives and lax.ppermute only.
A program may use at most 64 MiB of HBM per device.

v0:
```python
import jax
import jax.numpy as jnp
from jax import lax
from jax.sharding import PartitionSpec as P


def from_root(array, axis, root):
    return lax.dynamic_index_in_dim(lax.all_gather(array, axis), root, 0, keepdims=False)


def with_halo(array, sides, width):
    edges = {}
    for axis, dim in sides:
        peers, length = (lax.axis_size(axis), array.shape[dim])
        up = [(i, (i + 1) % peers) for i in range(peers)]
        last = lax.slice_in_dim(array, length - width, length, axis=dim)
        initial = lax.slice_in_dim(array, 0, width, axis=dim)
        edges[dim] = (
            lax.ppermute(last, axis, up),
            lax.ppermute(initial, axis, [(b, a) for a, b in up]),
        )
    done = []
    for _, dim in sides:
        low, high = edges[dim]
        around = [(width, width) if d in done else (0, 0) for d in range(array.ndim)]
        array = jnp.concatenate([jnp.pad(low, around), array, jnp.pad(high, around)], axis=dim)
        done.append(dim)
    return array


def copy_for_each(array, axis):
    copies = jnp.broadcast_to(array, (lax.axis_size(axis), *array.shape))
    return lax.all_to_all(copies, axis, split_axis=0, concat_axis=0, tiled=True)


def taken_together(array, axis):
    return copy_for_each(array, axis).sum(axis=0)


def advance(padded, table, branch_nodes, variance):
    count = padded.shape[-1] - 4

    def shifted(shift_by):
        return padded[..., 2 + shift_by : 2 + shift_by + count]

    upward = table[1] + variance * table[2]
    downward = table[3] + variance * table[4]
    middle = 1.0 - upward - downward
    low_case = upward * shifted(0) + middle * shifted(-1) + downward * shifted(-2)
    even_case = upward * shifted(1) + middle * shifted(0) + downward * shifted(-1)
    high_case = upward * shifted(2) + middle * shifted(1) + downward * shifted(0)
    mixed = jnp.where(
        branch_nodes == -1, low_case, jnp.where(branch_nodes == 0, even_case, high_case)
    )
    return table[0] * mixed


def on_device(payoff, positions, tables, offsets, vol_curve, bucket, bump_size):
    step_count = vol_curve.shape[0]
    local_steps = tables.shape[0]
    node_count = payoff.shape[0]
    block_count = offsets.shape[1]
    block_len = node_count // block_count
    step_ids = jnp.arange(step_count, dtype=jnp.int32)
    sigma_bumps = vol_curve[None, :] + bump_size[:, None] * (
        bucket[:, None] == step_ids[None, :]
    ).astype(jnp.float32)
    sigma_rows = jnp.concatenate([vol_curve[None, :], sigma_bumps], axis=0)
    variance_rows = sigma_rows * sigma_rows
    values = jnp.broadcast_to(payoff[None, :], (sigma_rows.shape[0], node_count))
    for step in reversed(range(step_count)):
        table = from_root(tables[step % local_steps], "bump", step // local_steps)
        padded = with_halo(values, ((("nx", "ny"), 1),), 2)
        branch_nodes = jnp.broadcast_to(offsets[step][:, None], (block_count, block_len)).reshape(
            node_count
        )
        values = advance(padded, table, branch_nodes[None, :], variance_rows[:, step : step + 1])
    base_values = values[0]
    bumped_values = values[1:]
    partial_sums = jnp.sum(positions[None, :] * (bumped_values - base_values[None, :]), axis=1)
    totals = taken_together(partial_sums, ("nx", "ny"))
    return (bumped_values, totals / bump_size)


def solution(mesh):
    in_specs = (
        P(("nx", "ny")),
        P(("nx", "ny")),
        P("bump", None, ("nx", "ny")),
        P(None, ("nx", "ny")),
        P(),
        P("bump"),
        P("bump"),
    )
    out_specs = (P("bump", ("nx", "ny")), P("bump"))
    return jax.shard_map(
        on_device, mesh=mesh, in_specs=in_specs, out_specs=out_specs, check_vma=False
    )
```

profile of v0, /device:TPU:1, one launch (start us, length us, event | category | flops | bytes accessed | tf_op | source)
XLA Modules:
  0.0 258.6 jit_solution(16836493279003777501)
XLA Ops:
  7.2 3.0 %fusion.89 = (f32[1,5,32768]{2,0,1:T(1,128)S(1)}, f32[1,5,32768]{2,0,1:T(1,128)S(1)}) fusion(f32[2,5,32768]{2,0,1:T(2,128)} %param.9), kind=kLoop, calls=%fused_computation.165 | loop fusion | bytes 2621440 | tf_op jit(solution)/shard_map/slice | solution.py:72
  10.2 1.4 copy.22
  11.8 3.3 %collective-permute-start.1 = (f32[17,2]{1,0:T(8,128)S(1)}, f32[17,2]{1,0:T(8,128)S(1)}, u32[]{:S(2)}, u32[]{:S(2)}) collective-permute-start(f32[17,2]{1,0:T(8,128)S(1)} %broadcast_in_dim.181), channel_id=1, source_target_pairs={{1,0},{2,1},{3,2},{4,3},{5,4},{6,5},{7,6},{8,7},{9,8},{10,9},{11,1... | collective-permute-start | bytes 416 | tf_op jit(solution)/shard_map/ppermute | solution.py:20
  15.0 1.0 collective-permute-start
  16.0 1.4 copy.21
  17.7 0.6 slice_bitcast_fusion.7
  18.3 0.6 compare_bitcast_fusion.15
  19.0 0.6 eq.255
  19.7 0.6 eq.303
  20.4 0.6 eq.300
  21.2 0.6 eq.297
  21.9 0.6 eq.294
  22.6 0.6 eq.291
  23.3 0.6 eq.288
  24.1 0.6 eq.285
  24.8 0.6 eq.282
  25.5 0.6 eq.273
  26.2 0.6 eq.279
  26.9 0.6 eq.276
  27.6 38.9 %all-gather.5.cloned.1.call-done = f32[4,5,32768]{2,1,0:T(8,128)} async-done(((f32[1,5,32768]{2,1,0:T(8,128)}), f32[4,5,32768]{2,1,0:T(8,128)}) %all-gather.5.cloned.1.call-update) | async-done | bytes 2621456 | tf_op jit(solution)/shard_map/all_gather | solution.py:8
  66.4 10.7 %fusion.81 = (f32[1,1,32768]{2,1,0:T(1,128)S(1)}, f32[1,1,32768]{2,1,0:T(1,128)S(1)}, f32[1,1,32768]{2,1,0:T(1,128)S(1)}, f32[1,1,32768]{2,1,0:T(1,128)}, f32[1,...) fusion(f32[4,5,32768]{2,1,0:T(8,128)} %all-gather.5.cloned.1.ca, ...), kind=kLoop, calls=%fused_computation.157 | loop fusion | bytes 4980736 | tf_op jit(solution)/shard_map/slice | solution.py:55
  77.2 0.6 copy-done.17
  77.8 0.2 broadcast_in_dim.177
  78.0 6.2 %fusion.77 = f32[17,32768]{1,0:T(8,128)S(1)} fusion(f32[17,2]{1,0:T(8,128)S(1)} %collective-permute-done.1, f32[17,32768]{1,0:T(8,128)S(1)} %broadcast_in_dim.177, f32[17,2]{1,0:T(8,128)} %copy-done.17, f32[32768]{0:T(1024)S(1)} %bitcast.118, f32[32768]{0:T(1024)S(1)} %bitcast.119, f32[32768]{0:T(1024)S(1)} %bitcast.120, f32[17]{0:T(128)S(1)} %copy-done.26, ...), kind=kLoop, calls=%fused_computation.124 | loop fusion | flops 15597568 | bytes 5177684 | tf_op jit(solution)/shard_map/mul | solution.py:55
  84.2 0.7 fusion.88
  84.9 3.3 %collective-permute-start.2 = (f32[17,2]{1,0:T(8,128)}, f32[17,2]{1,0:T(8,128)}, u32[]{:S(2)}, u32[]{:S(2)}) collective-permute-start(f32[17,2]{1,0:T(8,128)} %get-tuple-element.54), channel_id=1, source_target_pairs={{0,1},{1,2},{2,3},{3,4},{4,5},{5,6},{6,7},{7,8},{8,9},{9,10},{10,1... | collective-permute-start | bytes 416 | tf_op jit(solution)/shard_map/ppermute | solution.py:19
  88.2 31.3 %all-gather.3.cloned.1.call-done = f32[4,5,32768]{2,1,0:T(8,128)} async-done(((f32[1,5,32768]{2,1,0:T(8,128)}), f32[4,5,32768]{2,1,0:T(8,128)}) %all-gather.3.cloned.1.call-update) | async-done | bytes 2621456 | tf_op jit(solution)/shard_map/all_gather | solution.py:8
  119.5 10.7 %fusion.80 = (f32[1,1,32768]{2,1,0:T(1,128)}, f32[1,1,32768]{2,1,0:T(1,128)}, f32[1,1,32768]{2,1,0:T(1,128)}, f32[1,1,32768]{2,1,0:T(1,128)}, f32[1,1,32768]{2,1...) fusion(f32[4,5,32768]{2,1,0:T(8,128)} %all-gather.3.cloned.1.ca, ...), kind=kLoop, calls=%fused_computation.156 | loop fusion | bytes 4980736 | tf_op jit(solution)/shard_map/slice | solution.py:55
  130.3 6.3 %fusion.69 = f32[17,32768]{1,0:T(8,128)S(1)} fusion(f32[17,2]{1,0:T(8,128)} %collective-permute-done.3, f32[17,32768]{1,0:T(8,128)S(1)} %fusion.77, f32[17,2]{1,0:T(8,128)} %collective-permute-done.2, f32[32768]{0:T(1024)S(1)} %bitcast.123, f32[32768]{0:T(1024)S(1)} %bitcast.124, f32[32768]{0:T(1024)S(1)} %bitcast.125, f32[17]{0:T(128)} %get-tuple-element.78, ...), kind=kLoop, calls=%fused_computation.114 | loop fusion | flops 15597568 | bytes 5177684 | tf_op jit(solution)/shard_map/mul | solution.py:55
  136.6 1.6 copy-done
  138.3 3.3 %collective-permute-start.4 = (f32[17,2]{1,0:T(8,128)S(1)}, f32[17,2]{1,0:T(8,128)S(1)}, u32[]{:S(2)}, u32[]{:S(2)}) collective-permute-start(f32[17,2]{1,0:T(8,128)S(1)} %get-tuple-element.52), channel_id=1, source_target_pairs={{0,1},{1,2},{2,3},{3,4},{4,5},{5,6},{6,7},{7,8},{8,9},{9,10},{10,1... | collective-permute-start | bytes 416 | tf_op jit(solution)/shard_map/ppermute | solution.py:19
  141.6 0.6 eq.270
  142.4 3.8 %collective-permute-done.5 = f32[17,2]{1,0:T(8,128)S(1)} collective-permute-done((f32[17,2]{1,0:T(8,128)S(1)}, f32[17,2]{1,0:T(8,128)S(1)}, u32[]{:S(2)}, u32[]{:S(2)}) %collective-permute-start.5) | collective-permute-done | bytes 168 | tf_op jit(solution)/shard_map/ppermute | solution.py:20
  146.2 0.6 copy-done.18
  146.8 10.1 %fusion.61 = f32[17,32768]{1,0:T(8,128)S(1)} fusion(f32[17,2]{1,0:T(8,128)} %copy-done.18, f32[17,32768]{1,0:T(8,128)} %copy-done, f32[17,2]{1,0:T(8,128)S(1)} %collective-permute-done.4, f32[32768]{0:T(1024)} %bitcast.108, f32[32768]{0:T(1024)} %bitcast.109, f32[32768]{0:T(1024)} %bitcast.110, f32[17]{0:T(128)} %get-tuple-element.79, f32[32768]{0:T(1024)} %bitcast.111, ...), kind=kLoop, calls=%fused_computation.104 | loop fusion | flops 15597568 | bytes 5177684 | tf_op jit(solution)/shard_map/mul | solution.py:55
  156.8 0.7 fusion.86
  157.5 0.5 collective-permute-start.7
  158.0 0.7 broadcast_in_dim.167
  158.7 1.4 eq.267
  160.1 2.5 collective-permute-done.7
  162.6 6.4 %fusion.53 = f32[17,32768]{1,0:T(8,128)S(1)} fusion(f32[17,2]{1,0:T(8,128)} %collective-permute-done.7, f32[17,32768]{1,0:T(8,128)S(1)} %fusion.61, f32[17,2]{1,0:T(8,128)} %collective-permute-done.6, f32[32768]{0:T(1024)} %bitcast.113, f32[32768]{0:T(1024)} %bitcast.114, f32[32768]{0:T(1024)} %bitcast.115, f32[17]{0:T(128)} %get-tuple-element.80, ...), kind=kLoop, calls=%fused_computation.94 | loop fusion | flops 15597568 | bytes 5177684 | tf_op jit(solution)/shard_map/mul | solution.py:55
  169.0 1.6 copy-done.1
  170.7 0.3 collective-permute-start.8
  171.0 1.3 collective-permute-start.9
  172.4 0.6 eq.264
  173.1 2.6 %collective-permute-done.9 = f32[17,2]{1,0:T(8,128)S(1)} collective-permute-done((f32[17,2]{1,0:T(8,128)S(1)}, f32[17,2]{1,0:T(8,128)S(1)}, u32[]{:S(2)}, u32[]{:S(2)}) %collective-permute-start.9) | collective-permute-done | bytes 168 | tf_op jit(solution)/shard_map/ppermute | solution.py:20
  175.7 0.6 copy-done.19
  176.3 10.0 %fusion.45 = f32[17,32768]{1,0:T(8,128)S(1)} fusion(f32[17,2]{1,0:T(8,128)} %copy-done.19, f32[17,32768]{1,0:T(8,128)} %copy-done.1, f32[17,2]{1,0:T(8,128)S(1)} %collective-permute-done.8, f32[32768]{0:T(1024)} %bitcast.98, f32[32768]{0:T(1024)} %bitcast.99, f32[32768]{0:T(1024)} %bitcast.100, f32[17]{0:T(128)} %get-tuple-element.81, f32[32768]{0:T(1024)} %bitcast.101, ...), kind=kLoop, calls=%fused_computation.84 | loop fusion | flops 15597568 | bytes 5177684 | tf_op jit(solution)/shard_map/mul | solution.py:55
  186.2 0.7 fusion.84
  187.0 2.9 %collective-permute-start.11 = (f32[17,2]{1,0:T(8,128)S(1)}, f32[17,2]{1,0:T(8,128)}, u32[]{:S(2)}, u32[]{:S(2)}) collective-permute-start(f32[17,2]{1,0:T(8,128)S(1)} %get-tuple-element.47), channel_id=1, source_target_pairs={{1,0},{2,1},{3,2},{4,3},{5,4},{6,5},{7,6},{8,7},{9,8},{10,9},{11,1... | collective-permute-start | bytes 416 | tf_op jit(solution)/shard_map/ppermute | solution.py:20
  189.8 0.7 broadcast_in_dim.163
  190.5 1.4 eq.261
  191.9 0.8 collective-permute-done.11
  192.8 6.5 %fusion.37 = f32[17,32768]{1,0:T(8,128)S(1)} fusion(f32[17,2]{1,0:T(8,128)} %collective-permute-done.11, f32[17,32768]{1,0:T(8,128)S(1)} %fusion.45, f32[17,2]{1,0:T(8,128)} %collective-permute-done.10, f32[32768]{0:T(1024)} %bitcast.103, f32[32768]{0:T(1024)} %bitcast.104, f32[32768]{0:T(1024)} %bitcast.105, f32[17]{0:T(128)} %get-tuple-element.82, ...), kind=kLoop, calls=%fused_computation.74 | loop fusion | flops 15597568 | bytes 5177684 | tf_op jit(solution)/shard_map/mul | solution.py:55
  199.3 0.6 collective-permute-start.12
  200.0 3.7 %collective-permute-start.13 = (f32[17,2]{1,0:T(8,128)S(1)}, f32[17,2]{1,0:T(8,128)S(1)}, u32[]{:S(2)}, u32[]{:S(2)}) collective-permute-start(f32[17,2]{1,0:T(8,128)S(1)} %get-tuple-element.45), channel_id=1, source_target_pairs={{1,0},{2,1},{3,2},{4,3},{5,4},{6,5},{7,6},{8,7},{9,8},{10,9},{11,1... | collective-permute-start | bytes 416 | tf_op jit(solution)/shard_map/ppermute | solution.py:20
  203.7 1.4 slice.580
  205.2 5.4 %fusion.29 = f32[17,32768]{1,0:T(8,128)S(1)} fusion(f32[17,2]{1,0:T(8,128)S(1)} %collective-permute-done.13, f32[17,32768]{1,0:T(8,128)S(1)} %fusion.37, f32[17,2]{1,0:T(8,128)S(1)} %collective-permute-done.12, f32[32768]{0:T(1024)S(1)} %bitcast.91, f32[32768]{0:T(1024)S(1)} %bitcast.92, f32[32768]{0:T(1024)S(1)} %bitcast.93, f32[17]{0:T(128)S(1)} %copy-done.21, ...), kind=kLoop, calls=%fused_computation.64 | loop fusion | flops 15597568 | bytes 5177684 | tf_op jit(solution)/shard_map/mul | solution.py:55
  210.7 5.1 %collective-permute-start.15 = (f32[17,2]{1,0:T(8,128)S(1)}, f32[17,2]{1,0:T(8,128)S(1)}, u32[]{:S(2)}, u32[]{:S(2)}) collective-permute-start(f32[17,2]{1,0:T(8,128)S(1)} %get-tuple-element.43), channel_id=1, source_target_pairs={{1,0},{2,1},{3,2},{4,3},{5,4},{6,5},{7,6},{8,7},{9,8},{10,9},{11,1... | collective-permute-start | bytes 416 | tf_op jit(solution)/shard_map/ppermute | solution.py:20
  215.7 1.4 slice.577
  217.2 5.4 %fusion.21 = f32[17,32768]{1,0:T(8,128)S(1)} fusion(f32[17,2]{1,0:T(8,128)S(1)} %collective-permute-done.15, f32[17,32768]{1,0:T(8,128)S(1)} %fusion.29, f32[17,2]{1,0:T(8,128)S(1)} %collective-permute-done.14, f32[32768]{0:T(1024)S(1)} %bitcast.95, f32[32768]{0:T(1024)S(1)} %bitcast.96, f32[32768]{0:T(1024)S(1)} %bitcast.97, f32[17]{0:T(128)S(1)} %get-tuple-element.76, ...), kind=kLoop, calls=%fused_computation.54 | loop fusion | flops 15597568 | bytes 5177684 | tf_op jit(solution)/shard_map/mul | solution.py:55
  222.7 1.8 multiply_reduce_fusion
  224.6 26.6 %all_to_all.6 = f32[64,1,16]{2,1,0:T(1,128)S(1)} all-to-all(f32[64,1,16]{2,1,0:T(1,128)S(1)} %broadcast_in_dim.196), channel_id=1, replica_groups=mesh['bump'=4,'nx'=16,'ny'=4] {'nx','ny'}, dimensions={0} | all-to-all | bytes 8192 | tf_op jit(solution)/shard_map/all_to_all | solution.py:33
  251.3 0.5 div.3
  (105 shorter events, 2.4 us)
Async XLA Ops:
  7.2 4.5 %copy-start.7 = (f32[32768]{0:T(1024)S(1)}, f32[32768]{0:T(1024)}, u32[]{:S(2)}) copy-start(f32[32768]{0:T(1024)} %param.7) | copy-start | bytes 393220
  7.2 59.3 %all-gather.5.cloned.1.call-start = ((), (), s32[]{:S(2)}) async-start(), calls=%async_computation.2 | async-start | bytes 5242880 | tf_op jit(solution)/shard_map/all_gather | solution.py:8
  10.2 7.2 %copy-start.27 = (f32[8]{0:T(128)S(1)}, f32[8]{0:T(128)}, u32[]{:S(2)}) copy-start(f32[8]{0:T(128)} %param.11) | copy-start | bytes 100
  10.2 7.3 %copy-start.28 = (s32[16]{0:T(128)S(1)}, s32[16]{0:T(128)}, u32[]{:S(2)}) copy-start(s32[16]{0:T(128)} %param.12) | copy-start | bytes 196
  10.2 7.3 %copy-start.29 = (f32[16]{0:T(128)S(1)}, f32[16]{0:T(128)}, u32[]{:S(2)}) copy-start(f32[16]{0:T(128)} %param.13) | copy-start | bytes 196
  10.2 8.1 %copy-start.20 = (s32[8,128]{1,0:T(8,128)S(1)}, s32[8,128]{1,0:T(8,128)}, u32[]{:S(2)}) copy-start(s32[8,128]{1,0:T(8,128)} %param.10) | copy-start | bytes 12292
  11.6 107.8 %all-gather.3.cloned.1.call-start = ((), (), s32[]{:S(2)}) async-start(), calls=%async_computation.1 | async-start | bytes 5242880 | tf_op jit(solution)/shard_map/all_gather | solution.py:8
  11.8 65.4 %collective-permute-start.1 = (f32[17,2]{1,0:T(8,128)S(1)}, f32[17,2]{1,0:T(8,128)S(1)}, u32[]{:S(2)}, u32[]{:S(2)}) collective-permute-start(f32[17,2]{1,0:T(8,128)S(1)} %broadcast_in_dim.181), channel_id=1, source_target_pairs={{1,0},{2,1},{3,2},{4,3},{5,4},{6,5},{7,6},{8,7},{9,8},{10,9},{11,1... | collective-permute-start | bytes 416 | tf_op jit(solution)/shard_map/ppermute | solution.py:20
  15.0 62.1 %collective-permute-start = (f32[17,2]{1,0:T(8,128)S(1)}, f32[17,2]{1,0:T(8,128)S(1)}, u32[]{:S(2)}, u32[]{:S(2)}) collective-permute-start(f32[17,2]{1,0:T(8,128)S(1)} %broadcast_in_dim.178), channel_id=1, source_target_pairs={{0,1},{1,2},{2,3},{3,4},{4,5},{5,6},{6,7},{7,8},{8,9},{9,10},{10,1... | collective-permute-start | bytes 416 | tf_op jit(solution)/shard_map/ppermute | solution.py:19
  66.4 11.5 %copy-start.14 = (pred[32768]{0:T(1024)(128)(4,1)S(1)}, pred[32768]{0:T(1024)(128)(4,1)}, u32[]{:S(2)}) copy-start(pred[32768]{0:T(1024)(128)(4,1)} %eq.282) | copy-start | bytes 98308
  66.4 11.6 %copy-start.15 = (pred[32768]{0:T(1024)(128)(4,1)S(1)}, pred[32768]{0:T(1024)(128)(4,1)}, u32[]{:S(2)}) copy-start(pred[32768]{0:T(1024)(128)(4,1)} %eq.279) | copy-start | bytes 98308
  66.4 11.6 %copy-start.26 = (f32[17]{0:T(128)S(1)}, f32[17]{0:T(128)}, u32[]{:S(2)}) copy-start(f32[17]{0:T(128)} %get-tuple-element.77) | copy-start | bytes 208
  77.2 0.6 copy-start.17
  84.9 45.3 %collective-permute-start.2 = (f32[17,2]{1,0:T(8,128)}, f32[17,2]{1,0:T(8,128)}, u32[]{:S(2)}, u32[]{:S(2)}) collective-permute-start(f32[17,2]{1,0:T(8,128)} %get-tuple-element.54), channel_id=1, source_target_pairs={{0,1},{1,2},{2,3},{3,4},{4,5},{5,6},{6,7},{7,8},{8,9},{9,10},{10,1... | collective-permute-start | bytes 416 | tf_op jit(solution)/shard_map/ppermute | solution.py:19
  88.2 42.1 %collective-permute-start.3 = (f32[17,2]{1,0:T(8,128)S(1)}, f32[17,2]{1,0:T(8,128)}, u32[]{:S(2)}, u32[]{:S(2)}) collective-permute-start(f32[17,2]{1,0:T(8,128)S(1)} %get-tuple-element.55), channel_id=1, source_target_pairs={{1,0},{2,1},{3,2},{4,3},{5,4},{6,5},{7,6},{8,7},{9,8},{10,9},{11,1... | collective-permute-start | bytes 416 | tf_op jit(solution)/shard_map/ppermute | solution.py:20
  119.5 10.7 %copy-start.11 = (pred[32768]{0:T(1024)(128)(4,1)S(1)}, pred[32768]{0:T(1024)(128)(4,1)}, u32[]{:S(2)}) copy-start(pred[32768]{0:T(1024)(128)(4,1)} %eq.285) | copy-start | bytes 98308
  119.5 10.8 %copy-start.12 = (pred[32768]{0:T(1024)(128)(4,1)S(1)}, pred[32768]{0:T(1024)(128)(4,1)}, u32[]{:S(2)}) copy-start(pred[32768]{0:T(1024)(128)(4,1)} %eq.276) | copy-start | bytes 98308
  130.2 11.3 %copy-start.25 = (pred[128]{0:T(512)(128)(4,1)S(1)}, pred[128]{0:T(512)(128)(4,1)}, u32[]{:S(2)}) copy-start(pred[128]{0:T(512)(128)(4,1)} %get-tuple-element.70) | copy-start | bytes 388
  136.6 1.6 copy-start
  138.3 4.1 %collective-permute-start.4 = (f32[17,2]{1,0:T(8,128)S(1)}, f32[17,2]{1,0:T(8,128)S(1)}, u32[]{:S(2)}, u32[]{:S(2)}) collective-permute-start(f32[17,2]{1,0:T(8,128)S(1)} %get-tuple-element.52), channel_id=1, source_target_pairs={{0,1},{1,2},{2,3},{3,4},{4,5},{5,6},{6,7},{7,8},{8,9},{9,10},{10,1... | collective-permute-start | bytes 416 | tf_op jit(solution)/shard_map/ppermute | solution.py:19
  141.5 4.6 %collective-permute-start.5 = (f32[17,2]{1,0:T(8,128)S(1)}, f32[17,2]{1,0:T(8,128)S(1)}, u32[]{:S(2)}, u32[]{:S(2)}) collective-permute-start(f32[17,2]{1,0:T(8,128)S(1)} %get-tuple-element.53), channel_id=1, source_target_pairs={{1,0},{2,1},{3,2},{4,3},{5,4},{6,5},{7,6},{8,7},{9,8},{10,9},{11,1... | collective-permute-start | bytes 416 | tf_op jit(solution)/shard_map/ppermute | solution.py:20
  146.2 0.6 copy-start.18
  146.8 11.3 %copy-start.24 = (pred[128]{0:T(512)(128)(4,1)S(1)}, pred[128]{0:T(512)(128)(4,1)}, u32[]{:S(2)}) copy-start(pred[128]{0:T(512)(128)(4,1)} %get-tuple-element.71) | copy-start | bytes 388
  157.5 2.6 %collective-permute-start.6 = (f32[17,2]{1,0:T(8,128)}, f32[17,2]{1,0:T(8,128)}, u32[]{:S(2)}, u32[]{:S(2)}) collective-permute-start(f32[17,2]{1,0:T(8,128)} %get-tuple-element.50), channel_id=1, source_target_pairs={{0,1},{1,2},{2,3},{3,4},{4,5},{5,6},{6,7},{7,8},{8,9},{9,10},{10,1... | collective-permute-start | bytes 416 | tf_op jit(solution)/shard_map/ppermute | solution.py:19
  157.5 5.0 %collective-permute-start.7 = (f32[17,2]{1,0:T(8,128)S(1)}, f32[17,2]{1,0:T(8,128)}, u32[]{:S(2)}, u32[]{:S(2)}) collective-permute-start(f32[17,2]{1,0:T(8,128)S(1)} %get-tuple-element.51), channel_id=1, source_target_pairs={{1,0},{2,1},{3,2},{4,3},{5,4},{6,5},{7,6},{8,7},{9,8},{10,9},{11,1... | collective-permute-start | bytes 416 | tf_op jit(solution)/shard_map/ppermute | solution.py:20
  162.6 9.8 %copy-start.23 = (pred[128]{0:T(512)(128)(4,1)S(1)}, pred[128]{0:T(512)(128)(4,1)}, u32[]{:S(2)}) copy-start(pred[128]{0:T(512)(128)(4,1)} %get-tuple-element.72) | copy-start | bytes 388
  169.0 1.6 copy-start.1
  170.7 2.4 collective-permute-start.8
  171.0 4.6 %collective-permute-start.9 = (f32[17,2]{1,0:T(8,128)S(1)}, f32[17,2]{1,0:T(8,128)S(1)}, u32[]{:S(2)}, u32[]{:S(2)}) collective-permute-start(f32[17,2]{1,0:T(8,128)S(1)} %get-tuple-element.49), channel_id=1, source_target_pairs={{1,0},{2,1},{3,2},{4,3},{5,4},{6,5},{7,6},{8,7},{9,8},{10,9},{11,1... | collective-permute-start | bytes 416 | tf_op jit(solution)/shard_map/ppermute | solution.py:20
  175.7 0.6 copy-start.19
  176.3 13.6 %copy-start.22 = (pred[128]{0:T(512)(128)(4,1)S(1)}, pred[128]{0:T(512)(128)(4,1)}, u32[]{:S(2)}) copy-start(pred[128]{0:T(512)(128)(4,1)} %get-tuple-element.73) | copy-start | bytes 388
  186.9 5.0 %collective-permute-start.10 = (f32[17,2]{1,0:T(8,128)}, f32[17,2]{1,0:T(8,128)}, u32[]{:S(2)}, u32[]{:S(2)}) collective-permute-start(f32[17,2]{1,0:T(8,128)} %get-tuple-element.46), channel_id=1, source_target_pairs={{0,1},{1,2},{2,3},{3,4},{4,5},{5,6},{6,7},{7,8},{8,9},{9,10},{10,1... | collective-permute-start | bytes 416 | tf_op jit(solution)/shard_map/ppermute | solution.py:19
  187.0 5.8 %collective-permute-start.11 = (f32[17,2]{1,0:T(8,128)S(1)}, f32[17,2]{1,0:T(8,128)}, u32[]{:S(2)}, u32[]{:S(2)}) collective-permute-start(f32[17,2]{1,0:T(8,128)S(1)} %get-tuple-element.47), channel_id=1, source_target_pairs={{1,0},{2,1},{3,2},{4,3},{5,4},{6,5},{7,6},{8,7},{9,8},{10,9},{11,1... | collective-permute-start | bytes 416 | tf_op jit(solution)/shard_map/ppermute | solution.py:20
  192.8 12.3 %copy-start.2 = (f32[1,1,32768]{2,1,0:T(1,128)S(1)}, f32[1,1,32768]{2,1,0:T(1,128)}, u32[]{:S(2)}) copy-start(f32[1,1,32768]{2,1,0:T(1,128)} %get-tuple-element.41) | copy-start | bytes 393220
  192.8 12.3 %copy-start.10 = (pred[32768]{0:T(1024)(128)(4,1)S(1)}, pred[32768]{0:T(1024)(128)(4,1)}, u32[]{:S(2)}) copy-start(pred[32768]{0:T(1024)(128)(4,1)} %eq.300) | copy-start | bytes 98308
  192.8 12.3 %copy-start.13 = (pred[32768]{0:T(1024)(128)(4,1)S(1)}, pred[32768]{0:T(1024)(128)(4,1)}, u32[]{:S(2)}) copy-start(pred[32768]{0:T(1024)(128)(4,1)} %eq.261) | copy-start | bytes 98308
  192.8 12.3 %copy-start.21 = (f32[17]{0:T(128)S(1)}, f32[17]{0:T(128)}, u32[]{:S(2)}) copy-start(f32[17]{0:T(128)} %get-tuple-element.83) | copy-start | bytes 208
  199.3 5.7 %collective-permute-start.12 = (f32[17,2]{1,0:T(8,128)S(1)}, f32[17,2]{1,0:T(8,128)S(1)}, u32[]{:S(2)}, u32[]{:S(2)}) collective-permute-start(f32[17,2]{1,0:T(8,128)S(1)} %get-tuple-element.44), channel_id=1, source_target_pairs={{0,1},{1,2},{2,3},{3,4},{4,5},{5,6},{6,7},{7,8},{8,9},{9,10},{10,1... | collective-permute-start | bytes 416 | tf_op jit(solution)/shard_map/ppermute | solution.py:19
  200.0 5.1 %collective-permute-start.13 = (f32[17,2]{1,0:T(8,128)S(1)}, f32[17,2]{1,0:T(8,128)S(1)}, u32[]{:S(2)}, u32[]{:S(2)}) collective-permute-start(f32[17,2]{1,0:T(8,128)S(1)} %get-tuple-element.45), channel_id=1, source_target_pairs={{1,0},{2,1},{3,2},{4,3},{5,4},{6,5},{7,6},{8,7},{9,8},{10,9},{11,1... | collective-permute-start | bytes 416 | tf_op jit(solution)/shard_map/ppermute | solution.py:20
  205.1 12.0 %copy-start.3 = (f32[1,1,32768]{2,1,0:T(1,128)S(1)}, f32[1,1,32768]{2,1,0:T(1,128)}, u32[]{:S(2)}) copy-start(f32[1,1,32768]{2,1,0:T(1,128)} %get-tuple-element.4) | copy-start | bytes 393220
  205.1 12.0 %copy-start.4 = (f32[1,1,32768]{2,1,0:T(1,128)S(1)}, f32[1,1,32768]{2,1,0:T(1,128)}, u32[]{:S(2)}) copy-start(f32[1,1,32768]{2,1,0:T(1,128)} %get-tuple-element.5) | copy-start | bytes 393220
  205.1 12.0 %copy-start.5 = (f32[1,1,32768]{2,1,0:T(1,128)S(1)}, f32[1,1,32768]{2,1,0:T(1,128)}, u32[]{:S(2)}) copy-start(f32[1,1,32768]{2,1,0:T(1,128)} %get-tuple-element.6) | copy-start | bytes 393220
  205.1 12.0 %copy-start.6 = (f32[1,1,32768]{2,1,0:T(1,128)S(1)}, f32[1,1,32768]{2,1,0:T(1,128)}, u32[]{:S(2)}) copy-start(f32[1,1,32768]{2,1,0:T(1,128)} %get-tuple-element.22) | copy-start | bytes 393220
  205.1 12.0 %copy-start.8 = (pred[32768]{0:T(1024)(128)(4,1)S(1)}, pred[32768]{0:T(1024)(128)(4,1)}, u32[]{:S(2)}) copy-start(pred[32768]{0:T(1024)(128)(4,1)} %eq.255) | copy-start | bytes 98308
  205.1 12.0 %copy-start.9 = (pred[32768]{0:T(1024)(128)(4,1)S(1)}, pred[32768]{0:T(1024)(128)(4,1)}, u32[]{:S(2)}) copy-start(pred[32768]{0:T(1024)(128)(4,1)} %eq.303) | copy-start | bytes 98308
  210.7 6.5 %collective-permute-start.14 = (f32[17,2]{1,0:T(8,128)S(1)}, f32[17,2]{1,0:T(8,128)S(1)}, u32[]{:S(2)}, u32[]{:S(2)}) collective-permute-start(f32[17,2]{1,0:T(8,128)S(1)} %get-tuple-element.42), channel_id=1, source_target_pairs={{0,1},{1,2},{2,3},{3,4},{4,5},{5,6},{6,7},{7,8},{8,9},{9,10},{10,1... | collective-permute-start | bytes 416 | tf_op jit(solution)/shard_map/ppermute | solution.py:19
  210.7 6.4 %collective-permute-start.15 = (f32[17,2]{1,0:T(8,128)S(1)}, f32[17,2]{1,0:T(8,128)S(1)}, u32[]{:S(2)}, u32[]{:S(2)}) collective-permute-start(f32[17,2]{1,0:T(8,128)S(1)} %get-tuple-element.43), channel_id=1, source_target_pairs={{1,0},{2,1},{3,2},{4,3},{5,4},{6,5},{7,6},{8,7},{9,8},{10,9},{11,1... | collective-permute-start | bytes 416 | tf_op jit(solution)/shard_map/ppermute | solution.py:20
  217.2 5.5 %copy-start.16 = (f32[32768]{0:T(1024)S(1)}, f32[32768]{0:T(1024)}, u32[]{:S(2)}) copy-start(f32[32768]{0:T(1024)} %param.8) | copy-start | bytes 393220
  222.6 28.6 %copy-start.30 = (f32[16]{0:T(128)S(1)}, f32[16]{0:T(128)}, u32[]{:S(2)}) copy-start(f32[16]{0:T(128)} %param.13) | copy-start | bytes 196
Sparse Core Ops, SparseCore 0:
  11.8 54.6 all-gather.4
  68.2 51.1 all-gather.2
where the time goes:
time: 259 us
  waiting for transfers between devices  80.1 us (31%)
  other arithmetic  59.5 us (23%)
  local copies, waits for them, and re-layouts  52.6 us (20%)
  blocking collectives  26.6 us (10%)
  starting transfers between devices  25.3 us (10%)
  between operations  14.6 us (6%)
    all_gather x2, waiting for transfers between devices, from_root(): lax.all_gather(array, axis)  70.2 us
    mul x8, other arithmetic, advance(): return table[0] * mixed  56.3 us
    all_to_all x1, blocking collectives, copy_for_each(): return lax.all_to_all(copies, axis, split_axis=0, concat_axis=0, tiled=True)  26.6 us
    slice x2, local copies, waits for them, and re-layouts, advance(): return table[0] * mixed  21.4 us
    ppermute x8, starting transfers between devices, with_halo(): lax.ppermute(initial, axis, [(b, a) for a, b in up])  16.7 us
    ppermute x8, waiting for transfers between devices, with_halo(): lax.ppermute(initial, axis, [(b, a) for a, b in up])  9.71 us
    ppermute x8, starting transfers between devices, with_halo(): lax.ppermute(last, axis, up)  8.56 us
    unnamed x64, local copies, waits for them, and re-layouts  7.89 us
  transfers between devices with their start and end apart: 18, of which 7 were waited for; matrix products, arithmetic and copies ran while one was open for 19% of the time, Pallas kernels for 0%

commit v1 on v0

v1 whole, which is shorter than its diff:
```python
import jax
import jax.numpy as jnp
from jax import lax
from jax.experimental import pallas as pl
from jax.experimental.pallas import tpu as pltpu
from jax.sharding import PartitionSpec as P

NODE_AXES = ("nx", "ny")
LANES = 128
ROWS_PER_STEP = 5
STEPS = 8
WORKERS = 4
LOCAL_STEPS = STEPS // WORKERS
LOCAL_ROWS = LOCAL_STEPS * ROWS_PER_STEP
CURVES = 16
VMEM_LIMIT = 48 * 1024 * 1024

ROWS = 256
CHUNK = ROWS // WORKERS
PADDED = CHUNK + 8
PAIRS = LOCAL_STEPS * ROWS
CHUNK_PAIRS = LOCAL_STEPS * CHUNK
PADDED_PAIRS = LOCAL_STEPS * PADDED
TABLE_ROWS = LOCAL_ROWS * CHUNK
GHOST_ROWS = 24
MESSAGE = TABLE_ROWS + GHOST_ROWS
HALO = 24
VALUES = (STEPS + 1) * CHUNK

EXPAND_COST = pl.CostEstimate(flops=100_000_000, bytes_accessed=100_000_000, transcendentals=0)

VMEM = pltpu.MemorySpace.VMEM
SMEM = pltpu.MemorySpace.SMEM


def params(limit=VMEM_LIMIT):
    return pltpu.CompilerParams(vmem_limit_bytes=limit)


def vmem():
    return pl.BlockSpec(memory_space=VMEM)


def smem():
    return pl.BlockSpec(memory_space=SMEM)


def anywhere():
    return pl.BlockSpec(memory_space=pl.ANY)


def in_hbm(array):
    return pltpu.with_memory_space_constraint(array, pltpu.HBM)


def hbm():
    return pl.BlockSpec(memory_space=pltpu.HBM)


def edges_kernel(tables, payoff, offsets, first, last, held, held_payoff, held_offsets, sem):
    copies = [pltpu.make_async_copy(offsets, held_offsets, sem.at[2, 0])]
    for side, pair, row in ((0, 0, 0), (1, PAIRS - 8, ROWS - 8)):
        copies.append(
            pltpu.make_async_copy(tables.at[:, pl.ds(pair, 8), :], held.at[side], sem.at[0, side])
        )
        copies.append(
            pltpu.make_async_copy(
                payoff.at[pl.ds(row, 8), :], held_payoff.at[side], sem.at[1, side]
            )
        )
    for copy in copies:
        copy.start()
    for copy in copies:
        copy.wait()
    for side, out, row, lane in ((0, first, 0, 0), (1, last, 7, LANES - 1)):
        pair = row * (8 - LOCAL_STEPS) // 7
        for i in range(ROWS_PER_STEP):
            out[i * LOCAL_STEPS : (i + 1) * LOCAL_STEPS, :] = held[
                side, i, pair : pair + LOCAL_STEPS, :
            ]
        out[LOCAL_ROWS : 2 * STEPS, :] = jnp.broadcast_to(
            held_payoff[side, row : row + 1, :], (2 * STEPS - LOCAL_ROWS, LANES)
        )
        out[2 * STEPS : HALO, :] = jnp.broadcast_to(
            held_offsets[:, lane : lane + 1].astype(jnp.float32), (STEPS, LANES)
        )


def edges(tables, payoff_rows, offsets):
    shape = jax.ShapeDtypeStruct((HALO, LANES), jnp.float32)
    return pl.pallas_call(
        edges_kernel,
        out_shape=(shape, shape),
        in_specs=[hbm(), hbm(), hbm()],
        out_specs=(vmem(), vmem()),
        scratch_shapes=[
            pltpu.VMEM((2, ROWS_PER_STEP, 8, LANES), jnp.float32),
            pltpu.VMEM((2, 8, LANES), jnp.float32),
            pltpu.VMEM((STEPS, LANES), jnp.int32),
            pltpu.SemaphoreType.DMA((3, 2)),
        ],
        compiler_params=params(),
        name="edges",
    )(*(in_hbm(array) for array in (tables, payoff_rows, offsets)))


def load_kernel(tables, payoff, positions, held, held_payoff, held_positions, sem):
    copies = [
        pltpu.make_async_copy(source, target, sem.at[i])
        for i, (source, target) in enumerate(
            ((tables, held), (payoff, held_payoff), (positions, held_positions))
        )
    ]
    for copy in copies:
        copy.start()
    for copy in copies:
        copy.wait()


def load(*arrays):
    return pl.pallas_call(
        load_kernel,
        out_shape=tuple(jax.ShapeDtypeStruct(array.shape, array.dtype) for array in arrays),
        in_specs=[hbm()] * len(arrays),
        out_specs=(vmem(),) * len(arrays),
        scratch_shapes=[pltpu.SemaphoreType.DMA((len(arrays),))],
        compiler_params=params(),
        cost_estimate=pl.CostEstimate(flops=0, bytes_accessed=6_000_000, transcendentals=0),
        name="load",
    )(*(in_hbm(array) for array in arrays))


def pack_kernel(tables, before, after, own, plus1, plus2, plus3):
    me = lax.axis_index("bump")
    for k, out in ((1, plus1), (3, plus3), (2, plus2), (0, own)):
        chunk = lax.rem(me + k, WORKERS)
        below = lax.rem(chunk + WORKERS - 1, WORKERS)
        above = lax.rem(chunk + 1, WORKERS)
        start = pl.multiple_of(chunk * CHUNK_PAIRS, CHUNK_PAIRS)
        low = pl.multiple_of(below * CHUNK_PAIRS + CHUNK_PAIRS - 8, 8)
        high = pl.multiple_of(above * CHUNK_PAIRS, CHUNK_PAIRS)
        for i in range(ROWS_PER_STEP):
            out[i * CHUNK_PAIRS : (i + 1) * CHUNK_PAIRS, :] = tables[i, pl.ds(start, CHUNK_PAIRS), :]
            two = slice(i * LOCAL_STEPS, (i + 1) * LOCAL_STEPS)
            row = TABLE_ROWS + i * LOCAL_STEPS
            out[row : row + LOCAL_STEPS, :] = jnp.where(
                chunk == 0, before[two, :], tables[i, pl.ds(low, 8), :][8 - LOCAL_STEPS :]
            )
            row += LOCAL_ROWS
            out[row : row + LOCAL_STEPS, :] = jnp.where(
                chunk == WORKERS - 1, after[two, :], tables[i, pl.ds(high, 8), :][:LOCAL_STEPS]
            )
        out[TABLE_ROWS + 2 * LOCAL_ROWS :, :] = jnp.zeros(
            (GHOST_ROWS - 2 * LOCAL_ROWS, LANES), jnp.float32
        )


def pack(tables, before, after):
    shape = jax.ShapeDtypeStruct((MESSAGE, LANES), jnp.float32)
    return pl.pallas_call(
        pack_kernel,
        out_shape=(shape,) * WORKERS,
        in_specs=[vmem()] * 3,
        out_specs=(vmem(),) * WORKERS,
        compiler_params=params(),
        name="pack",
    )(tables, before, after)


def shifted(values, by, lane):
    if by == 0:
        return values
    turned = pltpu.roll(values, (-by) % LANES, 1)
    if by > 0:
        return jnp.where(lane < LANES - by, turned, pltpu.roll(turned, PADDED - 1, 0))
    return jnp.where(lane >= -by, turned, pltpu.roll(turned, 1, 0))


def spread(low, even, down, middle, up):
    zero = jnp.zeros_like(up)
    return (
        jnp.where(low, down, zero),
        jnp.where(low, middle, jnp.where(even, down, zero)),
        jnp.where(low, up, jnp.where(even, middle, down)),
        jnp.where(low, zero, jnp.where(even, up, middle)),
        jnp.where(even, zero, up),
    )


def weigh(weights, reach):
    total = weights[0] * reach[0]
    for weight, value in zip(weights[1:], reach[1:]):
        total = total + weight * value
    return total


def roll_kernel(
    own,
    from_m1,
    from_m2,
    from_p1,
    payoff,
    positions,
    offsets,
    before,
    after,
    vol,
    out,
    sums,
    table,
    steps_k,
    nodes_k,
):
    me = lax.axis_index("bump")
    sources = (own, from_m1, from_m2, from_p1)
    turns = (0, WORKERS - 1, WORKERS - 2, 1)
    turned = jnp.transpose(offsets[...].astype(jnp.float32))
    steps_k[8 : 8 + ROWS, :] = jnp.repeat(turned, ROWS // LANES, axis=0)
    steps_k[0:8, :] = jnp.transpose(before[2 * STEPS : HALO, 0:8])
    steps_k[8 + ROWS :, :] = jnp.transpose(after[2 * STEPS : HALO, 0:8])
    start = pl.multiple_of(me * CHUNK, CHUNK)
    part = jnp.concatenate(
        [
            steps_k[pl.ds(start + 8, CHUNK + 1), :],
            jnp.zeros((PADDED - CHUNK - 2, STEPS), jnp.float32),
            steps_k[pl.ds(start + 7, 1), :],
        ]
    )
    for s in range(STEPS):
        nodes_k[s] = jnp.broadcast_to(part[:, s : s + 1], (PADDED, LANES))
    above = payoff[pl.ds(pl.multiple_of(jnp.minimum(start + CHUNK, ROWS - 8), 8), 8), :]
    below = payoff[pl.ds(pl.multiple_of(jnp.maximum(start - 8, 0), 8), 8), :]
    values = jnp.concatenate(
        [
            payoff[pl.ds(start, CHUNK), :],
            jnp.where(me == WORKERS - 1, after[LOCAL_ROWS : LOCAL_ROWS + 1, :], above[0:1, :]),
            jnp.zeros((PADDED - CHUNK - 2, LANES), jnp.float32),
            jnp.where(me == 0, before[LOCAL_ROWS : LOCAL_ROWS + 1, :], below[7:8, :]),
        ]
    )
    gap = jnp.zeros((PADDED_PAIRS - CHUNK_PAIRS - 2 * LOCAL_STEPS, LANES), jnp.float32)
    for k in range(WORKERS):
        owner = lax.rem(me + turns[k], WORKERS)
        source = sources[k]
        for i in range(ROWS_PER_STEP):
            table[owner, i, :CHUNK_PAIRS, :] = source[i * CHUNK_PAIRS : (i + 1) * CHUNK_PAIRS, :]
            low = TABLE_ROWS + i * LOCAL_STEPS
            high = low + LOCAL_ROWS
            table[owner, i, CHUNK_PAIRS:, :] = jnp.concatenate(
                [source[high : high + LOCAL_STEPS, :], gap, source[low : low + LOCAL_STEPS, :]]
            )

    def rows(s, i):
        return table[s // LOCAL_STEPS, i, pl.ds(s % LOCAL_STEPS, PADDED, stride=LOCAL_STEPS), :]

    lane = lax.broadcasted_iota(jnp.int32, (PADDED, LANES), 1)
    slopes = {}
    for s in reversed(range(STEPS)):
        variance = vol[s] * vol[s]
        discount = rows(s, 0)
        up_slope = discount * rows(s, 2)
        down_slope = discount * rows(s, 4)
        up = discount * rows(s, 1) + variance * up_slope
        down = discount * rows(s, 3) + variance * down_slope
        low, even = nodes_k[s] < -0.5, nodes_k[s] < 0.5
        weights = spread(low, even, down, discount - up - down, up)
        slope_weights = spread(low, even, down_slope, -(up_slope + down_slope), up_slope)
        for q in list(slopes):
            reach = [shifted(slopes[q], m, lane) for m in range(-2, 3)]
            slopes[q] = weigh(weights, reach)
        reach = [shifted(values, m, lane) for m in range(-2, 3)]
        slopes[s] = weigh(slope_weights, reach)
        values = weigh(weights, reach)
    out[0:CHUNK, :] = values[0:CHUNK]
    weight = positions[pl.ds(start, CHUNK), :]
    for s in range(STEPS):
        slope = slopes[s][0:CHUNK]
        out[(s + 1) * CHUNK : (s + 2) * CHUNK, :] = slope
        sums[s : s + 1, :] = jnp.sum(weight * slope, axis=0, keepdims=True)


def share_kernel(own, from_m1, from_m2, from_p1, out):
    added = own[...] + from_m1[...] + from_m2[...] + from_p1[...]
    totals = jnp.sum(added, axis=1, keepdims=True)
    lane = lax.broadcasted_iota(jnp.int32, (STEPS, LANES), 1)
    step = lax.broadcasted_iota(jnp.int32, (STEPS, LANES), 0)
    row = jnp.sum(jnp.where(lane == step, totals, 0.0), axis=0, keepdims=True)
    out[...] = jnp.broadcast_to(row, out.shape)


def share(parts, peers):
    return pl.pallas_call(
        share_kernel,
        out_shape=jax.ShapeDtypeStruct((peers, LANES), jnp.float32),
        in_specs=[vmem()] * WORKERS,
        out_specs=vmem(),
        compiler_params=params(),
        name="share",
    )(*parts)


def roll_back(messages, payoff, positions, offsets, before, after, vol):
    return pl.pallas_call(
        roll_kernel,
        out_shape=(
            jax.ShapeDtypeStruct((VALUES, LANES), jnp.float32),
            jax.ShapeDtypeStruct((STEPS, LANES), jnp.float32),
        ),
        in_specs=[vmem()] * (WORKERS + 5) + [smem()],
        out_specs=(vmem(), vmem()),
        scratch_shapes=[
            pltpu.VMEM((WORKERS, ROWS_PER_STEP, PADDED_PAIRS, LANES), jnp.float32),
            pltpu.VMEM((ROWS + 16, STEPS), jnp.float32),
            pltpu.VMEM((STEPS, PADDED, LANES), jnp.float32),
        ],
        compiler_params=params(),
        name="roll_back",
    )(*messages, payoff, positions, offsets, before, after, vol)


def expand_kernel(
    own, from_m1, from_m2, from_p1, vol, bucket, bump, out, rate, built, done
):
    me = lax.axis_index("bump")
    sources = (own, from_m1, from_m2, from_p1)
    turns = (0, WORKERS - 1, WORKERS - 2, 1)
    for b in range(CURVES):
        rate[b] = 2.0 * vol[bucket[b]] + bump[b]
    stores = []
    for k in range(WORKERS):
        chunk = lax.rem(me + turns[k], WORKERS)
        base = sources[k][0:CHUNK, :]
        for b in range(CURVES):
            gain = bump[b] * rate[b]
            at = pl.multiple_of((bucket[b] + 1) * CHUNK, CHUNK)
            slope = sources[k][pl.ds(at, CHUNK), :]
            built[b // 8, k, pl.ds(b % 8, CHUNK, stride=8), :] = base + gain * slope
        for tile in range(CURVES // 8):
            stores.append(
                pltpu.make_async_copy(
                    built.at[tile, k],
                    out.at[tile, pl.ds(pl.multiple_of(chunk * CHUNK * 8, CHUNK * 8), CHUNK * 8), :],
                    done.at[tile, k],
                )
            )
            stores[-1].start()
    for store in stores:
        store.wait()


def expand(parts, vol, bucket, bump):
    tiles = CURVES // 8
    laid, rate = pl.pallas_call(
        expand_kernel,
        out_shape=(
            jax.ShapeDtypeStruct((tiles, ROWS * 8, LANES), jnp.float32),
            jax.ShapeDtypeStruct((CURVES,), jnp.float32),
        ),
        in_specs=[vmem()] * WORKERS + [smem()] * 3,
        out_specs=(anywhere(), smem()),
        scratch_shapes=[
            pltpu.VMEM((tiles, WORKERS, CHUNK * 8, LANES), jnp.float32),
            pltpu.SemaphoreType.DMA((tiles, WORKERS)),
        ],
        compiler_params=params(),
        cost_estimate=EXPAND_COST,
        name="expand",
    )(*parts, vol, bucket, bump)
    curves = laid.reshape(tiles, ROWS, 8, LANES).transpose(0, 2, 1, 3)
    return curves.reshape(CURVES, ROWS * LANES), rate


def vega_kernel(shared, bucket, rate, vega):
    totals = jnp.sum(shared[...], axis=0, keepdims=True)
    lane = lax.broadcasted_iota(jnp.int32, (1, LANES), 1)
    for b in range(CURVES):
        vega[b] = rate[b] * jnp.sum(jnp.where(lane == bucket[b], totals, 0.0))


def vegas(shared, bucket, rate):
    return pl.pallas_call(
        vega_kernel,
        out_shape=jax.ShapeDtypeStruct((CURVES,), jnp.float32),
        in_specs=[vmem(), smem(), smem()],
        out_specs=smem(),
        compiler_params=params(),
        name="vegas",
    )(shared, bucket, rate)


def rotated(by):
    return [(i, (i + by) % WORKERS) for i in range(WORKERS)]


def exchanged(array, axis):
    return (array,) + tuple(lax.ppermute(array, axis, rotated(by)) for by in (1, 2, -1))


def on_device(payoff, positions, tables, offsets, vol_curve, bucket, bump_size):
    groups = lax.axis_size(NODE_AXES)
    up = [(i, (i + 1) % groups) for i in range(groups)]
    payoff_rows = payoff.reshape(ROWS, LANES)
    tables = tables.transpose(1, 0, 2).reshape(ROWS_PER_STEP, LOCAL_STEPS, ROWS, LANES)
    tables = tables.transpose(0, 2, 1, 3).reshape(ROWS_PER_STEP, PAIRS, LANES)
    first, last = edges(tables, payoff_rows, offsets)
    before = lax.ppermute(last, NODE_AXES, up)
    after = lax.ppermute(first, NODE_AXES, [(b, a) for a, b in up])
    held, payoff_rows, position_rows = load(tables, payoff_rows, positions.reshape(ROWS, LANES))
    messages = pack(held, before, after)
    received = (
        messages[0],
        lax.ppermute(messages[1], "bump", rotated(1)),
        lax.ppermute(messages[2], "bump", rotated(2)),
        lax.ppermute(messages[3], "bump", rotated(-1)),
    )
    arrays, sums = roll_back(
        received, payoff_rows, position_rows, offsets, before, after, vol_curve
    )
    inner, outer = "ny", ("bump", "nx")
    arrays, *sums = lax.optimization_barrier((arrays, *exchanged(sums, inner)))
    peers = lax.axis_size(outer)
    sums = share(sums, peers)
    bumped_values, rate = expand(exchanged(arrays, "bump"), vol_curve, bucket, bump_size)
    shared = lax.all_to_all(
        sums.reshape(peers, 1, LANES), outer, split_axis=0, concat_axis=0, tiled=True
    )
    return (bumped_values, vegas(shared.reshape(peers, LANES), bucket, rate))


def solution(mesh):
    in_specs = (
        P(("nx", "ny")),
        P(("nx", "ny")),
        P("bump", None, ("nx", "ny")),
        P(None, ("nx", "ny")),
        P(),
        P("bump"),
        P("bump"),
    )
    out_specs = (P("bump", ("nx", "ny")), P("bump"))
    return jax.shard_map(
        on_device, mesh=mesh, in_specs=in_specs, out_specs=out_specs, check_vma=False
    )
```

time: 259 us -> 66.2 us (0.26)
  other arithmetic: 59.5 us -> 0 us
  waiting for transfers between devices: 80.1 us -> 27.4 us
  local copies, waits for them, and re-layouts: 52.6 us -> 0.01 us
  blocking collectives: 26.6 us -> 0 us
  between operations: 14.6 us -> 0.7 us
  Pallas kernels: 0 us -> 9.63 us
  starting transfers between devices: 25.3 us -> 28.2 us
    all_gather x2 -> x0, waiting for transfers between devices: 70.2 us -> none  [from_root(): lax.all_gather(array, axis)]
    mul x9 -> x0, other arithmetic: 56.4 us -> none  [the longest x8 56.3 us: advance(): return table[0] * mixed]
    slice x14 -> x0, local copies, waits for them, and re-layouts: 29.6 us -> none  [the longest x2 21.4 us: advance(): return table[0] * mixed]
    all_to_all x1 -> x0, blocking collectives: 26.6 us -> none  [copy_for_each(): return lax.all_to_all(copies, axis, split_axis=0, concat_axis=0, tiled=True)]
    ppermute x16 -> x11, waiting for transfers between devices: 9.82 us -> 21.6 us  [the longest x1 8.4 us: on_device(): lax.ppermute(messages[2], 'bump', rotated(2))]
    eq x16 -> x0, local copies, waits for them, and re-layouts: 11.6 us -> none  [the longest x8 6.57 us: advance(): branch_nodes == -1]
    pallas_call x0 -> x7, Pallas kernels: none -> 9.63 us  [the longest x1 2.67 us: roll_back(): pl.pallas_call(roll_kernel, out_shape=(jax.ShapeDtypeStruct((VALUES, LANE...]
    all_to_all x0 -> x1, starting transfers between devices: none -> 9.62 us  [on_device(): lax.all_to_all(sums.reshape(peers, 1, LANES), outer, split_axis=0, concat...]
  transfers between devices with their start and end apart: 18 -> 12, of which waited for: 7 -> 9; matrix products, arithmetic and copies ran while one was open for 19% -> 0% of each run, Pallas kernels for 0% -> 7%
where the time goes in v1:
time: 66.2 us; the launch traced here: 66 us
  starting transfers between devices  28.2 us (43%)
  waiting for transfers between devices  27.4 us (41%)
  Pallas kernels  9.63 us (15%)
  between operations  0.7 us (1%)
    all_to_all x1, starting transfers between devices, on_device(): lax.all_to_all(sums.reshape(peers, 1, LANES), outer, split_axis=0, concat...  9.62 us
    ppermute x6, starting transfers between devices, exchanged(): lax.ppermute(array, axis, rotated(by))  9.32 us
    ppermute x1, waiting for transfers between devices, on_device(): lax.ppermute(messages[2], 'bump', rotated(2))  8.4 us
    all_to_all x1, waiting for transfers between devices, on_device(): lax.all_to_all(sums.reshape(peers, 1, LANES), outer, split_axis=0, concat...  5.8 us
    ppermute x6, waiting for transfers between devices, exchanged(): lax.ppermute(array, axis, rotated(by))  5.29 us
    ppermute x1, starting transfers between devices, on_device(): before = lax.ppermute(last, NODE_AXES, up)  4.21 us
    ppermute x1, waiting for transfers between devices, on_device(): lax.ppermute(messages[1], 'bump', rotated(1))  4.03 us
    ppermute x1, waiting for transfers between devices, on_device(): after = lax.ppermute(first, NODE_AXES, [(b, a) for a, b in up])  3.21 us
  transfers between devices with their start and end apart: 12, of which 9 were waited for; matrix products, arithmetic and copies ran while one was open for 0% of the time, Pallas kernels for 7%

profile of v1, /device:TPU:1, one launch (start us, length us, event | category | flops | bytes accessed | tf_op | source)
XLA Modules:
  0.0 66.0 jit_solution(17898368766180826569)
XLA Ops:
  0.6 0.9 %edges.1 = (f32[24,128]{1,0:T(8,128)S(1)}, f32[24,128]{1,0:T(8,128)S(1)}) custom-call(f32[5,512,128]{2,1,0:T(8,128)} %bitcast.19, f32[256,128]{1,0:T(8,128)} %bitcast.21, s32[8,128]{1,0:T(8,128)} %offsets.3), custom_call_target="tpu_custom_call" | custom-call | tf_op jit(solution)/shard_map/edges/pallas_call | solution.py:91
  1.5 4.2 %collective-permute-start = (f32[24,128]{1,0:T(8,128)S(1)}, f32[24,128]{1,0:T(8,128)S(1)}, u32[]{:S(2)}, u32[]{:S(2)}) collective-permute-start(f32[24,128]{1,0:T(8,128)S(1)} %get-tuple-element.21), channel_id=1, source_target_pairs={{0,1},{1,2},{2,3},{3,4},{4,5},{5,6},{6,7},{7,8},{8,9},{9,10},{10,1... | collective-permute-start | bytes 36872 | tf_op jit(solution)/shard_map/ppermute | solution.py:406
  5.8 0.0 collective-permute-start.1
  5.8 0.0 copy-start
  5.8 0.0 copy-start.1
  5.8 1.4 %load.1 = (f32[5,512,128]{2,1,0:T(8,128)S(1)}, f32[256,128]{1,0:T(8,128)S(1)}, f32[256,128]{1,0:T(8,128)S(1)}) custom-call(f32[5,512,128]{2,1,0:T(8,128)} %bitcast.20, f32[256,128]{1,0:T(8,128)} %bitcast.22, f32[256,128]{1,0:T(8,128)} %bitcast.23), custom_call_target="tpu_custom_call" | custom-call | bytes 6000000 | tf_op jit(solution)/shard_map/load/pallas_call | solution.py:121
  7.2 0.0 collective-permute-done.before
  7.2 3.2 %collective-permute-done.1.after = f32[24,128]{1,0:T(8,128)S(1)} collective-permute-done((f32[24,128]{1,0:T(8,128)S(1)}, f32[24,128]{1,0:T(8,128)S(1)}, u32[]{:S(2)}, u32[]{:S(2)}) %collective-permute-start.1) | collective-permute-done | bytes 12320 | tf_op jit(solution)/shard_map/ppermute | solution.py:407
  10.4 0.0 copy-start.2
  10.4 0.0 copy-start.3
  10.4 0.1 pack.1
  10.5 1.4 %collective-permute-start.2 = (f32[664,128]{1,0:T(8,128)S(1)}, f32[664,128]{1,0:T(8,128)S(1)}, u32[]{:S(2)}, u32[]{:S(2)}) collective-permute-start(f32[664,128]{1,0:T(8,128)S(1)} %get-tuple-element.24), channel_id=1, source_target_pairs={{0,64},{64,128},{128,192},{192,0},{1,65},{65,129},{129,193},{193,1... | collective-permute-start | bytes 1019912 | tf_op jit(solution)/shard_map/ppermute | solution.py:412
  11.9 2.6 %collective-permute-start.3 = (f32[664,128]{1,0:T(8,128)S(1)}, f32[664,128]{1,0:T(8,128)S(1)}, u32[]{:S(2)}, u32[]{:S(2)}) collective-permute-start(f32[664,128]{1,0:T(8,128)S(1)} %get-tuple-element.25), channel_id=1, source_target_pairs={{0,128},{64,192},{128,0},{192,64},{1,129},{65,193},{129,1},{193,65... | collective-permute-start | bytes 1019912 | tf_op jit(solution)/shard_map/ppermute | solution.py:413
  14.5 1.1 %collective-permute-start.4 = (f32[664,128]{1,0:T(8,128)S(1)}, f32[664,128]{1,0:T(8,128)S(1)}, u32[]{:S(2)}, u32[]{:S(2)}) collective-permute-start(f32[664,128]{1,0:T(8,128)S(1)} %get-tuple-element.26), channel_id=1, source_target_pairs={{0,192},{64,0},{128,64},{192,128},{1,193},{65,1},{129,65},{193,129... | collective-permute-start | bytes 1019912 | tf_op jit(solution)/shard_map/ppermute | solution.py:414
  15.6 4.0 %collective-permute-done.2.from_m1 = f32[664,128]{1,0:T(8,128)S(1)} collective-permute-done((f32[664,128]{1,0:T(8,128)S(1)}, f32[664,128]{1,0:T(8,128)S(1)}, u32[]{:S(2)}, u32[]{:S(2)}) %collective-permute-start.2) | collective-permute-done | bytes 340000 | tf_op jit(solution)/shard_map/ppermute | solution.py:412
  19.6 8.4 %collective-permute-done.3.from_m2 = f32[664,128]{1,0:T(8,128)S(1)} collective-permute-done((f32[664,128]{1,0:T(8,128)S(1)}, f32[664,128]{1,0:T(8,128)S(1)}, u32[]{:S(2)}, u32[]{:S(2)}) %collective-permute-start.3) | collective-permute-done | bytes 340000 | tf_op jit(solution)/shard_map/ppermute | solution.py:413
  28.0 0.7 %collective-permute-done.4.from_p1 = f32[664,128]{1,0:T(8,128)S(1)} collective-permute-done((f32[664,128]{1,0:T(8,128)S(1)}, f32[664,128]{1,0:T(8,128)S(1)}, u32[]{:S(2)}, u32[]{:S(2)}) %collective-permute-start.4) | collective-permute-done | bytes 340000 | tf_op jit(solution)/shard_map/ppermute | solution.py:414
  28.7 0.0 copy-done
  28.7 0.0 copy-done.1
  28.7 2.7 %roll_back.1 = (f32[576,128]{1,0:T(8,128)S(1)}, f32[8,128]{1,0:T(8,128)S(1)}) custom-call(f32[664,128]{1,0:T(8,128)S(1)} %get-tuple-element.23.own, f32[664,128]{1,0:T(8,128)S(1)} %collective-permute-done.2.from_m1, f32[664,128]{1,0:T(8,128)S(1)} %collective-permute-done.3.from_m2, f32[664,128]{1,0:T(8,128)S(1)} %collective-permute-done.4.from_p1, ...), custom_call_target="tpu_custom_call" | custom-call | tf_op jit(solution)/shard_map/roll_back/pallas_call | solution.py:303
  31.4 1.1 %collective-permute-start.5 = (f32[8,128]{1,0:T(8,128)S(1)}, f32[8,128]{1,0:T(8,128)S(1)}, u32[]{:S(2)}, u32[]{:S(2)}) collective-permute-start(f32[8,128]{1,0:T(8,128)S(1)} %get-tuple-element.33.own), channel_id=1, source_target_pairs={{0,1},{1,2},{2,3},{3,0},{4,5},{5,6},{6,7},{7,4},{8,9},{9,10},{10,1... | collective-permute-start | bytes 12296 | tf_op jit(solution)/shard_map/ppermute | solution.py:396
  32.5 3.8 %collective-permute-start.6 = (f32[8,128]{1,0:T(8,128)S(1)}, f32[8,128]{1,0:T(8,128)S(1)}, u32[]{:S(2)}, u32[]{:S(2)}) collective-permute-start(f32[8,128]{1,0:T(8,128)S(1)} %get-tuple-element.33.own), channel_id=1, source_target_pairs={{0,2},{1,3},{2,0},{3,1},{4,6},{5,7},{6,4},{7,5},{8,10},{9,11},{10,... | collective-permute-start | bytes 12296 | tf_op jit(solution)/shard_map/ppermute | solution.py:396
  36.3 0.0 collective-permute-start.7
  36.3 0.0 collective-permute-done.5.from_m1
  36.3 1.3 %collective-permute-done.6.from_m2 = f32[8,128]{1,0:T(8,128)S(1)} collective-permute-done((f32[8,128]{1,0:T(8,128)S(1)}, f32[8,128]{1,0:T(8,128)S(1)}, u32[]{:S(2)}, u32[]{:S(2)}) %collective-permute-start.6) | collective-permute-done | bytes 4128 | tf_op jit(solution)/shard_map/ppermute | solution.py:396
  37.6 3.3 %collective-permute-done.7.from_p1 = f32[8,128]{1,0:T(8,128)S(1)} collective-permute-done((f32[8,128]{1,0:T(8,128)S(1)}, f32[8,128]{1,0:T(8,128)S(1)}, u32[]{:S(2)}, u32[]{:S(2)}) %collective-permute-start.7) | collective-permute-done | bytes 4128 | tf_op jit(solution)/shard_map/ppermute | solution.py:396
  40.9 1.0 %collective-permute-start.8 = (f32[576,128]{1,0:T(8,128)S(1)}, f32[576,128]{1,0:T(8,128)S(1)}, u32[]{:S(2)}, u32[]{:S(2)}) collective-permute-start(f32[576,128]{1,0:T(8,128)S(1)} %get-tuple-element.31.own), channel_id=1, source_target_pairs={{0,64},{64,128},{128,192},{192,0},{1,65},{65,129},{129,193},{193,1... | collective-permute-start | bytes 884744 | tf_op jit(solution)/shard_map/ppermute | solution.py:396
  41.8 2.1 %collective-permute-start.9 = (f32[576,128]{1,0:T(8,128)S(1)}, f32[576,128]{1,0:T(8,128)S(1)}, u32[]{:S(2)}, u32[]{:S(2)}) collective-permute-start(f32[576,128]{1,0:T(8,128)S(1)} %get-tuple-element.31.own), channel_id=1, source_target_pairs={{0,128},{64,192},{128,0},{192,64},{1,129},{65,193},{129,1},{193,65... | collective-permute-start | bytes 884744 | tf_op jit(solution)/shard_map/ppermute | solution.py:396
  43.9 1.3 %collective-permute-start.10 = (f32[576,128]{1,0:T(8,128)S(1)}, f32[576,128]{1,0:T(8,128)S(1)}, u32[]{:S(2)}, u32[]{:S(2)}) collective-permute-start(f32[576,128]{1,0:T(8,128)S(1)} %get-tuple-element.31.own), channel_id=1, source_target_pairs={{0,192},{64,0},{128,64},{192,128},{1,193},{65,1},{129,65},{193,129... | collective-permute-start | bytes 884744 | tf_op jit(solution)/shard_map/ppermute | solution.py:396
  45.2 0.7 %share.1 = f32[64,128]{1,0:T(8,128)} custom-call(f32[8,128]{1,0:T(8,128)S(1)} %get-tuple-element.33.own, f32[8,128]{1,0:T(8,128)S(1)} %collective-permute-done.5.from_m1, f32[8,128]{1,0:T(8,128)S(1)} %collective-permute-done.6.from_m2, f32[8,128]{1,0:T(8,128)S(1)} %collective-permute-done.7.from_p1), custom_call_target="tpu_custom_call" | custom-call | tf_op jit(solution)/shard_map/share/pallas_call | solution.py:292
  45.9 9.6 %all-to-all-start = ((f32[64,1,128]{2,1,0:T(1,128)}), f32[64,1,128]{2,1,0:T(1,128)S(1)}, u32[]{:S(2)}, u32[]{:S(2)}) async-start(f32[64,1,128]{2,1,0:T(1,128)} %bitcast.13), calls=%async_computation | async-start | bytes 65536 | tf_op jit(solution)/shard_map/all_to_all | solution.py:424
  55.5 0.0 collective-permute-done.8.from_m1
  55.5 0.3 collective-permute-done.9.from_m2
  55.8 0.5 collective-permute-done.10.from_p1
  56.3 0.0 copy-done.2
  56.3 0.0 copy-done.3
  56.3 2.7 %expand.1 = (f32[2,2048,128]{2,1,0:T(8,128)}, f32[16]{0:T(128)S(1)}) custom-call(f32[576,128]{1,0:T(8,128)S(1)} %get-tuple-element.31.own, f32[576,128]{1,0:T(8,128)S(1)} %collective-permute-done.8.from_m1, f32[576,128]{1,0:T(8,128)S(1)} %collective-permute-done.9.from_m2, f32[576,128]{1,0:T(8,128)S(1)} %collective-permute-done.10.from_p1, f32[8]{0:T(128)S(1)} %copy-done.1, ...), custom_call_target="tpu_custom_call" | custom-call | flops 100000000 | bytes 100000000 | tf_op jit(solution)/shard_map/expand/pallas_call | solution.py:353
  59.0 5.8 %all-to-all-done = f32[64,1,128]{2,1,0:T(1,128)S(1)} async-done(((f32[64,1,128]{2,1,0:T(1,128)}), f32[64,1,128]{2,1,0:T(1,128)S(1)}, u32[]{:S(2)}, u32[]{:S(2)}) %all-to-all-start) | async-done | bytes 32800 | tf_op jit(solution)/shard_map/all_to_all | solution.py:424
  64.8 1.2 %vegas.1 = f32[16]{0:T(128)} custom-call(f32[64,128]{1,0:T(8,128)S(1)} %bitcast.18, s32[16]{0:T(128)S(1)} %copy-done.2, f32[16]{0:T(128)S(1)} %get-tuple-element.37.rate), custom_call_target="tpu_custom_call" | custom-call | tf_op jit(solution)/shard_map/vegas/pallas_call | solution.py:381
Async XLA Ops:
  1.5 5.6 %collective-permute-start = (f32[24,128]{1,0:T(8,128)S(1)}, f32[24,128]{1,0:T(8,128)S(1)}, u32[]{:S(2)}, u32[]{:S(2)}) collective-permute-start(f32[24,128]{1,0:T(8,128)S(1)} %get-tuple-element.21), channel_id=1, source_target_pairs={{0,1},{1,2},{2,3},{3,4},{4,5},{5,6},{6,7},{7,8},{8,9},{9,10},{10,1... | collective-permute-start | bytes 36872 | tf_op jit(solution)/shard_map/ppermute | solution.py:406
  5.8 4.6 %collective-permute-start.1 = (f32[24,128]{1,0:T(8,128)S(1)}, f32[24,128]{1,0:T(8,128)S(1)}, u32[]{:S(2)}, u32[]{:S(2)}) collective-permute-start(f32[24,128]{1,0:T(8,128)S(1)} %get-tuple-element.22), channel_id=1, source_target_pairs={{1,0},{2,1},{3,2},{4,3},{5,4},{6,5},{7,6},{8,7},{9,8},{10,9},{11,1... | collective-permute-start | bytes 36872 | tf_op jit(solution)/shard_map/ppermute | solution.py:407
  5.8 22.9 %copy-start = (s32[8,128]{1,0:T(8,128)S(1)}, s32[8,128]{1,0:T(8,128)}, u32[]{:S(2)}) copy-start(s32[8,128]{1,0:T(8,128)} %offsets.3) | copy-start | bytes 12292
  5.8 22.9 %copy-start.1 = (f32[8]{0:T(128)S(1)}, f32[8]{0:T(128)}, u32[]{:S(2)}) copy-start(f32[8]{0:T(128)} %vol.3) | copy-start | bytes 100
  10.4 45.9 %copy-start.2 = (s32[16]{0:T(128)S(1)}, s32[16]{0:T(128)}, u32[]{:S(2)}) copy-start(s32[16]{0:T(128)} %bucket.3) | copy-start | bytes 196
  10.4 45.9 %copy-start.3 = (f32[16]{0:T(128)S(1)}, f32[16]{0:T(128)}, u32[]{:S(2)}) copy-start(f32[16]{0:T(128)} %bump.1) | copy-start | bytes 196
  10.5 9.1 %collective-permute-start.2 = (f32[664,128]{1,0:T(8,128)S(1)}, f32[664,128]{1,0:T(8,128)S(1)}, u32[]{:S(2)}, u32[]{:S(2)}) collective-permute-start(f32[664,128]{1,0:T(8,128)S(1)} %get-tuple-element.24), channel_id=1, source_target_pairs={{0,64},{64,128},{128,192},{192,0},{1,65},{65,129},{129,193},{193,1... | collective-permute-start | bytes 1019912 | tf_op jit(solution)/shard_map/ppermute | solution.py:412
  11.9 16.1 %collective-permute-start.3 = (f32[664,128]{1,0:T(8,128)S(1)}, f32[664,128]{1,0:T(8,128)S(1)}, u32[]{:S(2)}, u32[]{:S(2)}) collective-permute-start(f32[664,128]{1,0:T(8,128)S(1)} %get-tuple-element.25), channel_id=1, source_target_pairs={{0,128},{64,192},{128,0},{192,64},{1,129},{65,193},{129,1},{193,65... | collective-permute-start | bytes 1019912 | tf_op jit(solution)/shard_map/ppermute | solution.py:413
  14.5 14.2 %collective-permute-start.4 = (f32[664,128]{1,0:T(8,128)S(1)}, f32[664,128]{1,0:T(8,128)S(1)}, u32[]{:S(2)}, u32[]{:S(2)}) collective-permute-start(f32[664,128]{1,0:T(8,128)S(1)} %get-tuple-element.26), channel_id=1, source_target_pairs={{0,192},{64,0},{128,64},{192,128},{1,193},{65,1},{129,65},{193,129... | collective-permute-start | bytes 1019912 | tf_op jit(solution)/shard_map/ppermute | solution.py:414
  31.4 5.0 %collective-permute-start.5 = (f32[8,128]{1,0:T(8,128)S(1)}, f32[8,128]{1,0:T(8,128)S(1)}, u32[]{:S(2)}, u32[]{:S(2)}) collective-permute-start(f32[8,128]{1,0:T(8,128)S(1)} %get-tuple-element.33.own), channel_id=1, source_target_pairs={{0,1},{1,2},{2,3},{3,0},{4,5},{5,6},{6,7},{7,4},{8,9},{9,10},{10,1... | collective-permute-start | bytes 12296 | tf_op jit(solution)/shard_map/ppermute | solution.py:396
  32.5 5.1 %collective-permute-start.6 = (f32[8,128]{1,0:T(8,128)S(1)}, f32[8,128]{1,0:T(8,128)S(1)}, u32[]{:S(2)}, u32[]{:S(2)}) collective-permute-start(f32[8,128]{1,0:T(8,128)S(1)} %get-tuple-element.33.own), channel_id=1, source_target_pairs={{0,2},{1,3},{2,0},{3,1},{4,6},{5,7},{6,4},{7,5},{8,10},{9,11},{10,... | collective-permute-start | bytes 12296 | tf_op jit(solution)/shard_map/ppermute | solution.py:396
  36.3 4.5 %collective-permute-start.7 = (f32[8,128]{1,0:T(8,128)S(1)}, f32[8,128]{1,0:T(8,128)S(1)}, u32[]{:S(2)}, u32[]{:S(2)}) collective-permute-start(f32[8,128]{1,0:T(8,128)S(1)} %get-tuple-element.33.own), channel_id=1, source_target_pairs={{0,3},{1,0},{2,1},{3,2},{4,7},{5,4},{6,5},{7,6},{8,11},{9,8},{10,9... | collective-permute-start | bytes 12296 | tf_op jit(solution)/shard_map/ppermute | solution.py:396
  40.9 14.7 %collective-permute-start.8 = (f32[576,128]{1,0:T(8,128)S(1)}, f32[576,128]{1,0:T(8,128)S(1)}, u32[]{:S(2)}, u32[]{:S(2)}) collective-permute-start(f32[576,128]{1,0:T(8,128)S(1)} %get-tuple-element.31.own), channel_id=1, source_target_pairs={{0,64},{64,128},{128,192},{192,0},{1,65},{65,129},{129,193},{193,1... | collective-permute-start | bytes 884744 | tf_op jit(solution)/shard_map/ppermute | solution.py:396
  41.8 14.0 %collective-permute-start.9 = (f32[576,128]{1,0:T(8,128)S(1)}, f32[576,128]{1,0:T(8,128)S(1)}, u32[]{:S(2)}, u32[]{:S(2)}) collective-permute-start(f32[576,128]{1,0:T(8,128)S(1)} %get-tuple-element.31.own), channel_id=1, source_target_pairs={{0,128},{64,192},{128,0},{192,64},{1,129},{65,193},{129,1},{193,65... | collective-permute-start | bytes 884744 | tf_op jit(solution)/shard_map/ppermute | solution.py:396
  43.9 12.4 %collective-permute-start.10 = (f32[576,128]{1,0:T(8,128)S(1)}, f32[576,128]{1,0:T(8,128)S(1)}, u32[]{:S(2)}, u32[]{:S(2)}) collective-permute-start(f32[576,128]{1,0:T(8,128)S(1)} %get-tuple-element.31.own), channel_id=1, source_target_pairs={{0,192},{64,0},{128,64},{192,128},{1,193},{65,1},{129,65},{193,129... | collective-permute-start | bytes 884744 | tf_op jit(solution)/shard_map/ppermute | solution.py:396
  45.9 18.9 %all-to-all-start = ((f32[64,1,128]{2,1,0:T(1,128)}), f32[64,1,128]{2,1,0:T(1,128)S(1)}, u32[]{:S(2)}, u32[]{:S(2)}) async-start(f32[64,1,128]{2,1,0:T(1,128)} %bitcast.13), calls=%async_computation | async-start | bytes 65536 | tf_op jit(solution)/shard_map/all_to_all | solution.py:424

commit v2 on v1

--- a/solution.py
+++ b/solution.py
@@ -57,7 +57,16 @@
     return pl.BlockSpec(memory_space=pltpu.HBM)
 
 
-def edges_kernel(tables, payoff, offsets, first, last, held, held_payoff, held_offsets, sem):
+def on_even_group():
+    return lax.rem(lax.axis_index("ny"), 2) == 0
+
+
+def halos(one, two):
+    even = on_even_group()
+    return jnp.where(even, two[...], one[...]), jnp.where(even, one[...], two[...])
+
+
+def edges_kernel(tables, payoff, offsets, one, two, held, held_payoff, held_offsets, ends, sem):
     copies = [pltpu.make_async_copy(offsets, held_offsets, sem.at[2, 0])]
     for side, pair, row in ((0, 0, 0), (1, PAIRS - 8, ROWS - 8)):
         copies.append(
@@ -72,7 +81,8 @@
         copy.start()
     for copy in copies:
         copy.wait()
-    for side, out, row, lane in ((0, first, 0, 0), (1, last, 7, LANES - 1)):
+    for side, row, lane in ((0, 0, 0), (1, 7, LANES - 1)):
+        out = ends.at[side]
         pair = row * (8 - LOCAL_STEPS) // 7
         for i in range(ROWS_PER_STEP):
             out[i * LOCAL_STEPS : (i + 1) * LOCAL_STEPS, :] = held[
@@ -84,6 +94,8 @@
         out[2 * STEPS : HALO, :] = jnp.broadcast_to(
             held_offsets[:, lane : lane + 1].astype(jnp.float32), (STEPS, LANES)
         )
+    one[...] = jnp.where(on_even_group(), ends[1], ends[0])
+    two[...] = jnp.where(on_even_group(), ends[0], ends[1])
 
 
 def edges(tables, payoff_rows, offsets):
@@ -97,6 +109,7 @@
             pltpu.VMEM((2, ROWS_PER_STEP, 8, LANES), jnp.float32),
             pltpu.VMEM((2, 8, LANES), jnp.float32),
             pltpu.VMEM((STEPS, LANES), jnp.int32),
+            pltpu.VMEM((2, HALO, LANES), jnp.float32),
             pltpu.SemaphoreType.DMA((3, 2)),
         ],
         compiler_params=params(),
@@ -130,8 +143,9 @@
     )(*(in_hbm(array) for array in arrays))
 
 
-def pack_kernel(tables, before, after, own, plus1, plus2, plus3):
+def pack_kernel(tables, one, two, own, plus1, plus2, plus3):
     me = lax.axis_index("bump")
+    before, after = halos(one, two)
     for k, out in ((1, plus1), (3, plus3), (2, plus2), (0, own)):
         chunk = lax.rem(me + k, WORKERS)
         below = lax.rem(chunk + WORKERS - 1, WORKERS)
@@ -141,21 +155,21 @@
         high = pl.multiple_of(above * CHUNK_PAIRS, CHUNK_PAIRS)
         for i in range(ROWS_PER_STEP):
             out[i * CHUNK_PAIRS : (i + 1) * CHUNK_PAIRS, :] = tables[i, pl.ds(start, CHUNK_PAIRS), :]
-            two = slice(i * LOCAL_STEPS, (i + 1) * LOCAL_STEPS)
+            at = slice(i * LOCAL_STEPS, (i + 1) * LOCAL_STEPS)
             row = TABLE_ROWS + i * LOCAL_STEPS
             out[row : row + LOCAL_STEPS, :] = jnp.where(
-                chunk == 0, before[two, :], tables[i, pl.ds(low, 8), :][8 - LOCAL_STEPS :]
+                chunk == 0, before[at, :], tables[i, pl.ds(low, 8), :][8 - LOCAL_STEPS :]
             )
             row += LOCAL_ROWS
             out[row : row + LOCAL_STEPS, :] = jnp.where(
-                chunk == WORKERS - 1, after[two, :], tables[i, pl.ds(high, 8), :][:LOCAL_STEPS]
+                chunk == WORKERS - 1, after[at, :], tables[i, pl.ds(high, 8), :][:LOCAL_STEPS]
             )
         out[TABLE_ROWS + 2 * LOCAL_ROWS :, :] = jnp.zeros(
             (GHOST_ROWS - 2 * LOCAL_ROWS, LANES), jnp.float32
         )
 
 
-def pack(tables, before, after):
+def pack(tables, one, two):
     shape = jax.ShapeDtypeStruct((MESSAGE, LANES), jnp.float32)
     return pl.pallas_call(
         pack_kernel,
@@ -164,7 +178,7 @@
         out_specs=(vmem(),) * WORKERS,
         compiler_params=params(),
         name="pack",
-    )(tables, before, after)
+    )(tables, one, two)
 
 
 def shifted(values, by, lane):
@@ -202,8 +216,8 @@
     payoff,
     positions,
     offsets,
-    before,
-    after,
+    one,
+    two,
     vol,
     out,
     sums,
@@ -212,6 +226,7 @@
     nodes_k,
 ):
     me = lax.axis_index("bump")
+    before, after = halos(one, two)
     sources = (own, from_m1, from_m2, from_p1)
     turns = (0, WORKERS - 1, WORKERS - 2, 1)
     turned = jnp.transpose(offsets[...].astype(jnp.float32))
@@ -273,38 +288,22 @@
         values = weigh(weights, reach)
     out[0:CHUNK, :] = values[0:CHUNK]
     weight = positions[pl.ds(start, CHUNK), :]
+    lane8 = lax.broadcasted_iota(jnp.int32, (8, LANES), 1)
+    held = jnp.zeros((8, LANES), jnp.float32)
     for s in range(STEPS):
         slope = slopes[s][0:CHUNK]
         out[(s + 1) * CHUNK : (s + 2) * CHUNK, :] = slope
-        sums[s : s + 1, :] = jnp.sum(weight * slope, axis=0, keepdims=True)
-
-
-def share_kernel(own, from_m1, from_m2, from_p1, out):
-    added = own[...] + from_m1[...] + from_m2[...] + from_p1[...]
-    totals = jnp.sum(added, axis=1, keepdims=True)
-    lane = lax.broadcasted_iota(jnp.int32, (STEPS, LANES), 1)
-    step = lax.broadcasted_iota(jnp.int32, (STEPS, LANES), 0)
-    row = jnp.sum(jnp.where(lane == step, totals, 0.0), axis=0, keepdims=True)
-    out[...] = jnp.broadcast_to(row, out.shape)
-
-
-def share(parts, peers):
-    return pl.pallas_call(
-        share_kernel,
-        out_shape=jax.ShapeDtypeStruct((peers, LANES), jnp.float32),
-        in_specs=[vmem()] * WORKERS,
-        out_specs=vmem(),
-        compiler_params=params(),
-        name="share",
-    )(*parts)
-
-
-def roll_back(messages, payoff, positions, offsets, before, after, vol):
+        total = jnp.sum(jnp.sum(weight * slope, axis=0, keepdims=True), axis=1, keepdims=True)
+        held = jnp.where(lane8 == s, total, held)
+    sums[...] = jnp.broadcast_to(held[0:1, :], sums.shape)
+
+
+def roll_back(messages, payoff, positions, offsets, one, two, vol, groups):
     return pl.pallas_call(
         roll_kernel,
         out_shape=(
             jax.ShapeDtypeStruct((VALUES, LANES), jnp.float32),
-            jax.ShapeDtypeStruct((STEPS, LANES), jnp.float32),
+            jax.ShapeDtypeStruct((groups, LANES), jnp.float32),
         ),
         in_specs=[vmem()] * (WORKERS + 5) + [smem()],
         out_specs=(vmem(), vmem()),
@@ -315,35 +314,34 @@
         ],
         compiler_params=params(),
         name="roll_back",
-    )(*messages, payoff, positions, offsets, before, after, vol)
-
-
-def expand_kernel(
-    own, from_m1, from_m2, from_p1, vol, bucket, bump, out, rate, built, done
-):
+    )(*messages, payoff, positions, offsets, one, two, vol)
+
+
+def build(source, tile_rows, rate, bucket, bump):
+    base = source[0:CHUNK, :]
+    for b in range(CURVES):
+        gain = bump[b] * rate[b]
+        slope = source[pl.ds(pl.multiple_of((bucket[b] + 1) * CHUNK, CHUNK), CHUNK), :]
+        tile_rows[b // 8, pl.ds(b % 8, CHUNK, stride=8), :] = base + gain * slope
+
+
+def write(built, out, chunk, sems):
+    stores = []
+    for tile in range(CURVES // 8):
+        rows = pl.ds(pl.multiple_of(chunk * CHUNK * 8, CHUNK * 8), CHUNK * 8)
+        stores.append(pltpu.make_async_copy(built.at[tile], out.at[tile, rows, :], sems.at[tile]))
+        stores[-1].start()
+    return stores
+
+
+def expand_kernel(own, from_m1, from_m2, from_p1, vol, bucket, bump, out, rate, built, done):
     me = lax.axis_index("bump")
-    sources = (own, from_m1, from_m2, from_p1)
-    turns = (0, WORKERS - 1, WORKERS - 2, 1)
     for b in range(CURVES):
         rate[b] = 2.0 * vol[bucket[b]] + bump[b]
     stores = []
-    for k in range(WORKERS):
-        chunk = lax.rem(me + turns[k], WORKERS)
-        base = sources[k][0:CHUNK, :]
-        for b in range(CURVES):
-            gain = bump[b] * rate[b]
-            at = pl.multiple_of((bucket[b] + 1) * CHUNK, CHUNK)
-            slope = sources[k][pl.ds(at, CHUNK), :]
-            built[b // 8, k, pl.ds(b % 8, CHUNK, stride=8), :] = base + gain * slope
-        for tile in range(CURVES // 8):
-            stores.append(
-                pltpu.make_async_copy(
-                    built.at[tile, k],
-                    out.at[tile, pl.ds(pl.multiple_of(chunk * CHUNK * 8, CHUNK * 8), CHUNK * 8), :],
-                    done.at[tile, k],
-                )
-            )
-            stores[-1].start()
+    for k, (source, turn) in enumerate(((own, 0), (from_m1, 3), (from_m2, 2), (from_p1, 1))):
+        build(source, built.at[k], rate, bucket, bump)
+        stores += write(built.at[k], out, lax.rem(me + turn, WORKERS), done.at[k])
     for store in stores:
         store.wait()
 
@@ -359,8 +357,8 @@
         in_specs=[vmem()] * WORKERS + [smem()] * 3,
         out_specs=(anywhere(), smem()),
         scratch_shapes=[
-            pltpu.VMEM((tiles, WORKERS, CHUNK * 8, LANES), jnp.float32),
-            pltpu.SemaphoreType.DMA((tiles, WORKERS)),
+            pltpu.VMEM((WORKERS, tiles, CHUNK * 8, LANES), jnp.float32),
+            pltpu.SemaphoreType.DMA((WORKERS, tiles)),
         ],
         compiler_params=params(),
         cost_estimate=EXPAND_COST,
@@ -370,22 +368,48 @@
     return curves.reshape(CURVES, ROWS * LANES), rate
 
 
-def vega_kernel(shared, bucket, rate, vega):
-    totals = jnp.sum(shared[...], axis=0, keepdims=True)
-    lane = lax.broadcasted_iota(jnp.int32, (1, LANES), 1)
-    for b in range(CURVES):
-        vega[b] = rate[b] * jnp.sum(jnp.where(lane == bucket[b], totals, 0.0))
-
-
-def vegas(shared, bucket, rate):
+def total_kernel(shared, out):
+    out[...] = jnp.broadcast_to(jnp.sum(shared[...], axis=0, keepdims=True), out.shape)
+
+
+def total(shared):
+    return pl.pallas_call(
+        total_kernel,
+        out_shape=jax.ShapeDtypeStruct((8, LANES), jnp.float32),
+        in_specs=[vmem()],
+        out_specs=vmem(),
+        compiler_params=params(),
+        name="total",
+    )(shared)
+
+
+def vega_kernel(own, from_m1, from_m2, from_p1, bucket, rate, vega):
+    totals = own[...] + from_m1[...] + from_m2[...] + from_p1[...]
+    lane = lax.broadcasted_iota(jnp.int32, (8, LANES), 1)
+    row = lax.broadcasted_iota(jnp.int32, (8, LANES), 0)
+    line = jnp.zeros((1, LANES), jnp.float32)
+    for tile in range(CURVES // 8):
+        picked = jnp.zeros((8, LANES), jnp.float32)
+        for r in range(8):
+            b = tile * 8 + r
+            hit = jnp.logical_and(row == r, lane == bucket[b])
+            picked = jnp.where(hit, rate[b] * totals, picked)
+        entry = jnp.sum(picked, axis=1, keepdims=True)
+        line += jnp.sum(
+            jnp.where(lane == row + tile * 8, entry, 0.0), axis=0, keepdims=True
+        )
+    vega[...] = line[:, :CURVES]
+
+
+def vegas(parts, bucket, rate):
     return pl.pallas_call(
         vega_kernel,
-        out_shape=jax.ShapeDtypeStruct((CURVES,), jnp.float32),
-        in_specs=[vmem(), smem(), smem()],
-        out_specs=smem(),
+        out_shape=jax.ShapeDtypeStruct((1, CURVES), jnp.float32),
+        in_specs=[vmem()] * WORKERS + [smem(), smem()],
+        out_specs=vmem(),
         compiler_params=params(),
         name="vegas",
-    )(shared, bucket, rate)
+    )(*parts, bucket, rate).reshape(CURVES)
 
 
 def rotated(by):
@@ -398,15 +422,16 @@
 
 def on_device(payoff, positions, tables, offsets, vol_curve, bucket, bump_size):
     groups = lax.axis_size(NODE_AXES)
-    up = [(i, (i + 1) % groups) for i in range(groups)]
+    with_next = [(i, i ^ 1) for i in range(groups)]
+    with_last = [(i, (i + (1 if i % 2 else groups - 1)) % groups) for i in range(groups)]
     payoff_rows = payoff.reshape(ROWS, LANES)
     tables = tables.transpose(1, 0, 2).reshape(ROWS_PER_STEP, LOCAL_STEPS, ROWS, LANES)
     tables = tables.transpose(0, 2, 1, 3).reshape(ROWS_PER_STEP, PAIRS, LANES)
-    first, last = edges(tables, payoff_rows, offsets)
-    before = lax.ppermute(last, NODE_AXES, up)
-    after = lax.ppermute(first, NODE_AXES, [(b, a) for a, b in up])
+    one, two = edges(tables, payoff_rows, offsets)
+    one = lax.ppermute(one, NODE_AXES, with_next)
+    two = lax.ppermute(two, NODE_AXES, with_last)
     held, payoff_rows, position_rows = load(tables, payoff_rows, positions.reshape(ROWS, LANES))
-    messages = pack(held, before, after)
+    messages = pack(held, one, two)
     received = (
         messages[0],
         lax.ppermute(messages[1], "bump", rotated(1)),
@@ -414,17 +439,15 @@
         lax.ppermute(messages[3], "bump", rotated(-1)),
     )
     arrays, sums = roll_back(
-        received, payoff_rows, position_rows, offsets, before, after, vol_curve
-    )
-    inner, outer = "ny", ("bump", "nx")
-    arrays, *sums = lax.optimization_barrier((arrays, *exchanged(sums, inner)))
-    peers = lax.axis_size(outer)
-    sums = share(sums, peers)
+        received, payoff_rows, position_rows, offsets, one, two, vol_curve, groups
+    )
     bumped_values, rate = expand(exchanged(arrays, "bump"), vol_curve, bucket, bump_size)
     shared = lax.all_to_all(
-        sums.reshape(peers, 1, LANES), outer, split_axis=0, concat_axis=0, tiled=True
-    )
-    return (bumped_values, vegas(shared.reshape(peers, LANES), bucket, rate))
+        sums.reshape(groups, 1, LANES), NODE_AXES, split_axis=0, concat_axis=0, tiled=True
+    )
+    shared, rate = lax.optimization_barrier((shared, rate))
+    totals = exchanged(total(shared.reshape(groups, LANES)), "bump")
+    return (bumped_values, vegas(totals, bucket, rate))
 
 
 def solution(mesh):

time: 66.2 us -> 65.1 us (0.983)
  waiting for transfers between devices: 27.4 us -> 25.6 us
  starting transfers between devices: 28.2 us -> 29 us
    ppermute x1, waiting for transfers between devices: 8.4 us -> 1.75 us  [on_device(): lax.ppermute(messages[2], 'bump', rotated(2))]
    all_to_all x1, starting transfers between devices: 9.62 us -> 14.2 us  [on_device(): lax.all_to_all(sums.reshape(groups, 1, LANES), NODE_AXES, split_axis=0, c...]
    ppermute x1, waiting for transfers between devices: 0.69 us -> 4.18 us  [on_device(): lax.ppermute(messages[3], 'bump', rotated(-1))]
    ppermute x1, waiting for transfers between devices: 4.03 us -> 7.26 us  [on_device(): lax.ppermute(messages[1], 'bump', rotated(1))]
    ppermute x6, starting transfers between devices: 9.32 us -> 7.13 us  [exchanged(): lax.ppermute(array, axis, rotated(by))]
    ppermute x1, starting transfers between devices: 1.37 us -> 0.08 us  [on_device(): lax.ppermute(messages[1], 'bump', rotated(1))]
    ppermute x2, waiting for transfers between devices: 3.21 us -> 2.22 us  [the longest x1 2.22 us: on_device(): two = lax.ppermute(two, NODE_AXES, with_last)]
    pallas_call x2, Pallas kernels: 1.9 us -> 1.17 us  [the longest x1 1.15 us: vegas(): pl.pallas_call(vega_kernel, out_shape=jax.ShapeDtypeStruct((1, CURVES), j...]
  transfers between devices with their start and end apart: 12 -> 12, of which waited for: 9 -> 9; matrix products, arithmetic and copies ran while one was open for 0% -> 0% of each run, Pallas kernels for 7% -> 6%
where the time goes in v2:
time: 65.1 us; the launch traced here: 64.9 us
  starting transfers between devices  29 us (45%)
  waiting for transfers between devices  25.6 us (39%)
  Pallas kernels  9.6 us (15%)
  between operations  0.71 us (1%)
    all_to_all x1, starting transfers between devices, on_device(): lax.all_to_all(sums.reshape(groups, 1, LANES), NODE_AXES, split_axis=0, c...  14.2 us
    ppermute x1, waiting for transfers between devices, on_device(): lax.ppermute(messages[1], 'bump', rotated(1))  7.26 us
    ppermute x6, starting transfers between devices, exchanged(): lax.ppermute(array, axis, rotated(by))  7.13 us
    all_to_all x1, waiting for transfers between devices, on_device(): lax.all_to_all(sums.reshape(groups, 1, LANES), NODE_AXES, split_axis=0, c...  5.2 us
    ppermute x6, waiting for transfers between devices, exchanged(): lax.ppermute(array, axis, rotated(by))  4.94 us
    ppermute x1, waiting for transfers between devices, on_device(): lax.ppermute(messages[3], 'bump', rotated(-1))  4.18 us
    pallas_call x1, Pallas kernels, roll_back(): pl.pallas_call(roll_kernel, out_shape=(jax.ShapeDtypeStruct((VALUES, LANE...  3.38 us
    ppermute x1, starting transfers between devices, on_device(): one = lax.ppermute(one, NODE_AXES, with_next)  3.33 us
  transfers between devices with their start and end apart: 12, of which 9 were waited for; matrix products, arithmetic and copies ran while one was open for 0% of the time, Pallas kernels for 6%

profile of v2, /device:TPU:1, one launch (start us, length us, event | category | flops | bytes accessed | tf_op | source)
XLA Modules:
  0.0 64.9 jit_solution(12596929669176556050)
XLA Ops:
  0.6 0.9 %edges.1 = (f32[24,128]{1,0:T(8,128)S(1)}, f32[24,128]{1,0:T(8,128)S(1)}) custom-call(f32[5,512,128]{2,1,0:T(8,128)} %bitcast.20, f32[256,128]{1,0:T(8,128)} %bitcast.22, s32[8,128]{1,0:T(8,128)} %offsets.3), custom_call_target="tpu_custom_call" | custom-call | tf_op jit(solution)/shard_map/edges/pallas_call | solution.py:103
  1.5 3.3 %collective-permute-start = (f32[24,128]{1,0:T(8,128)S(1)}, f32[24,128]{1,0:T(8,128)S(1)}, u32[]{:S(2)}, u32[]{:S(2)}) collective-permute-start(f32[24,128]{1,0:T(8,128)S(1)} %get-tuple-element.18), channel_id=1, source_target_pairs={{0,1},{1,0},{2,3},{3,2},{4,5},{5,4},{6,7},{7,6},{8,9},{9,8},{10,11... | collective-permute-start | bytes 36872 | tf_op jit(solution)/shard_map/ppermute | solution.py:431
  4.9 1.0 %collective-permute-start.1 = (f32[24,128]{1,0:T(8,128)S(1)}, f32[24,128]{1,0:T(8,128)S(1)}, u32[]{:S(2)}, u32[]{:S(2)}) collective-permute-start(f32[24,128]{1,0:T(8,128)S(1)} %get-tuple-element.19), channel_id=1, source_target_pairs={{0,63},{1,2},{2,1},{3,4},{4,3},{5,6},{6,5},{7,8},{8,7},{9,10},{10,... | collective-permute-start | bytes 36872 | tf_op jit(solution)/shard_map/ppermute | solution.py:432
  5.9 0.0 copy-start
  5.9 0.0 copy-start.1
  5.9 1.4 %load.1 = (f32[5,512,128]{2,1,0:T(8,128)S(1)}, f32[256,128]{1,0:T(8,128)S(1)}, f32[256,128]{1,0:T(8,128)S(1)}) custom-call(f32[5,512,128]{2,1,0:T(8,128)} %bitcast.21, f32[256,128]{1,0:T(8,128)} %bitcast.23, f32[256,128]{1,0:T(8,128)} %bitcast.24), custom_call_target="tpu_custom_call" | custom-call | bytes 6000000 | tf_op jit(solution)/shard_map/load/pallas_call | solution.py:134
  7.3 0.0 collective-permute-done.one
  7.3 2.2 %collective-permute-done.1.two = f32[24,128]{1,0:T(8,128)S(1)} collective-permute-done((f32[24,128]{1,0:T(8,128)S(1)}, f32[24,128]{1,0:T(8,128)S(1)}, u32[]{:S(2)}, u32[]{:S(2)}) %collective-permute-start.1) | collective-permute-done | bytes 12320 | tf_op jit(solution)/shard_map/ppermute | solution.py:432
  9.5 0.0 copy-start.2
  9.5 0.0 copy-start.3
  9.5 0.1 pack.1
  9.6 0.1 collective-permute-start.2
  9.7 2.2 %collective-permute-start.3 = (f32[664,128]{1,0:T(8,128)S(1)}, f32[664,128]{1,0:T(8,128)S(1)}, u32[]{:S(2)}, u32[]{:S(2)}) collective-permute-start(f32[664,128]{1,0:T(8,128)S(1)} %get-tuple-element.22), channel_id=1, source_target_pairs={{0,128},{64,192},{128,0},{192,64},{1,129},{65,193},{129,1},{193,65... | collective-permute-start | bytes 1019912 | tf_op jit(solution)/shard_map/ppermute | solution.py:438
  11.9 1.1 %collective-permute-start.4 = (f32[664,128]{1,0:T(8,128)S(1)}, f32[664,128]{1,0:T(8,128)S(1)}, u32[]{:S(2)}, u32[]{:S(2)}) collective-permute-start(f32[664,128]{1,0:T(8,128)S(1)} %get-tuple-element.23), channel_id=1, source_target_pairs={{0,192},{64,0},{128,64},{192,128},{1,193},{65,1},{129,65},{193,129... | collective-permute-start | bytes 1019912 | tf_op jit(solution)/shard_map/ppermute | solution.py:439
  12.9 7.3 %collective-permute-done.2.from_m1 = f32[664,128]{1,0:T(8,128)S(1)} collective-permute-done((f32[664,128]{1,0:T(8,128)S(1)}, f32[664,128]{1,0:T(8,128)S(1)}, u32[]{:S(2)}, u32[]{:S(2)}) %collective-permute-start.2) | collective-permute-done | bytes 340000 | tf_op jit(solution)/shard_map/ppermute | solution.py:437
  20.2 1.8 %collective-permute-done.3.from_m2 = f32[664,128]{1,0:T(8,128)S(1)} collective-permute-done((f32[664,128]{1,0:T(8,128)S(1)}, f32[664,128]{1,0:T(8,128)S(1)}, u32[]{:S(2)}, u32[]{:S(2)}) %collective-permute-start.3) | collective-permute-done | bytes 340000 | tf_op jit(solution)/shard_map/ppermute | solution.py:438
  21.9 4.2 %collective-permute-done.4.from_p1 = f32[664,128]{1,0:T(8,128)S(1)} collective-permute-done((f32[664,128]{1,0:T(8,128)S(1)}, f32[664,128]{1,0:T(8,128)S(1)}, u32[]{:S(2)}, u32[]{:S(2)}) %collective-permute-start.4) | collective-permute-done | bytes 340000 | tf_op jit(solution)/shard_map/ppermute | solution.py:439
  26.1 0.0 copy-done
  26.1 0.0 copy-done.1
  26.1 3.4 %roll_back.1 = (f32[576,128]{1,0:T(8,128)S(1)}, f32[64,128]{1,0:T(8,128)}) custom-call(f32[664,128]{1,0:T(8,128)S(1)} %get-tuple-element.20.own, f32[664,128]{1,0:T(8,128)S(1)} %collective-permute-done.2.from_m1, f32[664,128]{1,0:T(8,128)S(1)} %collective-permute-done.3.from_m2, f32[664,128]{1,0:T(8,128)S(1)} %collective-permute-done.4.from_p1, ...), custom_call_target="tpu_custom_call" | custom-call | tf_op jit(solution)/shard_map/roll_back/pallas_call | solution.py:302
  29.5 3.4 %collective-permute-start.7 = (f32[576,128]{1,0:T(8,128)S(1)}, f32[576,128]{1,0:T(8,128)S(1)}, u32[]{:S(2)}, u32[]{:S(2)}) collective-permute-start(f32[576,128]{1,0:T(8,128)S(1)} %get-tuple-element.26.own), channel_id=1, source_target_pairs={{0,192},{64,0},{128,64},{192,128},{1,193},{65,1},{129,65},{193,129... | collective-permute-start | bytes 884744 | tf_op jit(solution)/shard_map/ppermute | solution.py:420
  32.9 0.0 collective-permute-start.6
  32.9 0.6 collective-permute-start.5
  33.5 14.2 %all-to-all-start = ((f32[64,1,128]{2,1,0:T(1,128)}), f32[64,1,128]{2,1,0:T(1,128)S(1)}, u32[]{:S(2)}, u32[]{:S(2)}) async-start(f32[64,1,128]{2,1,0:T(1,128)} %bitcast.13), calls=%async_computation | async-start | bytes 65536 | tf_op jit(solution)/shard_map/all_to_all | solution.py:445
  47.7 0.0 collective-permute-done.7.from_p1
  47.7 0.0 collective-permute-done.6.from_m2
  47.7 1.3 %collective-permute-done.5.from_m1 = f32[576,128]{1,0:T(8,128)S(1)} collective-permute-done((f32[576,128]{1,0:T(8,128)S(1)}, f32[576,128]{1,0:T(8,128)S(1)}, u32[]{:S(2)}, u32[]{:S(2)}) %collective-permute-start.5) | collective-permute-done | bytes 294944 | tf_op jit(solution)/shard_map/ppermute | solution.py:420
  49.0 0.0 copy-done.2
  49.0 0.0 copy-done.3
  49.0 2.7 %expand.1 = (f32[2,2048,128]{2,1,0:T(8,128)}, f32[16]{0:T(128)S(1)}) custom-call(f32[576,128]{1,0:T(8,128)S(1)} %get-tuple-element.26.own, f32[576,128]{1,0:T(8,128)S(1)} %collective-permute-done.5.from_m1, f32[576,128]{1,0:T(8,128)S(1)} %collective-permute-done.6.from_m2, f32[576,128]{1,0:T(8,128)S(1)} %collective-permute-done.7.from_p1, f32[8]{0:T(128)S(1)} %copy-done.1, ...), custom_call_target="tpu_custom_call" | custom-call | flops 100000000 | bytes 100000000 | tf_op jit(solution)/shard_map/expand/pallas_call | solution.py:351
  51.7 5.2 %all-to-all-done = f32[64,1,128]{2,1,0:T(1,128)S(1)} async-done(((f32[64,1,128]{2,1,0:T(1,128)}), f32[64,1,128]{2,1,0:T(1,128)S(1)}, u32[]{:S(2)}, u32[]{:S(2)}) %all-to-all-start) | async-done | bytes 32800 | tf_op jit(solution)/shard_map/all_to_all | solution.py:445
  56.9 2.5 %collective-permute-start.10 = (f32[8,128]{1,0:T(8,128)S(1)}, f32[8,128]{1,0:T(8,128)S(1)}, u32[]{:S(2)}, u32[]{:S(2)}) collective-permute-start(f32[8,128]{1,0:T(8,128)S(1)} %total.1.own), channel_id=1, source_target_pairs={{0,192},{64,0},{128,64},{192,128},{1,193},{65,1},{129,65},{193,129... | collective-permute-start | bytes 12296 | tf_op jit(solution)/shard_map/ppermute | solution.py:420
  59.4 0.7 %collective-permute-start.9 = (f32[8,128]{1,0:T(8,128)S(1)}, f32[8,128]{1,0:T(8,128)S(1)}, u32[]{:S(2)}, u32[]{:S(2)}) collective-permute-start(f32[8,128]{1,0:T(8,128)S(1)} %total.1.own), channel_id=1, source_target_pairs={{0,128},{64,192},{128,0},{192,64},{1,129},{65,193},{129,1},{193,65... | collective-permute-start | bytes 12296 | tf_op jit(solution)/shard_map/ppermute | solution.py:420
  60.1 0.0 collective-permute-start.8
  60.1 0.1 collective-permute-done.10.from_p1
  60.1 3.2 %collective-permute-done.9.from_m2 = f32[8,128]{1,0:T(8,128)S(1)} collective-permute-done((f32[8,128]{1,0:T(8,128)S(1)}, f32[8,128]{1,0:T(8,128)S(1)}, u32[]{:S(2)}, u32[]{:S(2)}) %collective-permute-start.9) | collective-permute-done | bytes 4128 | tf_op jit(solution)/shard_map/ppermute | solution.py:420
  63.3 0.4 collective-permute-done.8.from_m1
  63.7 1.2 %vegas.1 = f32[1,16]{1,0:T(1,128)} custom-call(f32[8,128]{1,0:T(8,128)S(1)} %total.1.own, f32[8,128]{1,0:T(8,128)S(1)} %collective-permute-done.8.from_m1, f32[8,128]{1,0:T(8,128)S(1)} %collective-permute-done.9.from_m2, f32[8,128]{1,0:T(8,128)S(1)} %collective-permute-done.10.from_p1, s32[16]{0:T(128)S(1)} %copy-done.2, f32[16]{0:T(128)S(1)} %get-tuple-element.31.rate), custom_call_target="tpu_custom_call" | custom-call | tf_op jit(solution)/shard_map/vegas/pallas_call | solution.py:405
  (1 shorter events, 0.0 us)
Async XLA Ops:
  1.5 5.7 %collective-permute-start = (f32[24,128]{1,0:T(8,128)S(1)}, f32[24,128]{1,0:T(8,128)S(1)}, u32[]{:S(2)}, u32[]{:S(2)}) collective-permute-start(f32[24,128]{1,0:T(8,128)S(1)} %get-tuple-element.18), channel_id=1, source_target_pairs={{0,1},{1,0},{2,3},{3,2},{4,5},{5,4},{6,7},{7,6},{8,9},{9,8},{10,11... | collective-permute-start | bytes 36872 | tf_op jit(solution)/shard_map/ppermute | solution.py:431
  4.9 4.6 %collective-permute-start.1 = (f32[24,128]{1,0:T(8,128)S(1)}, f32[24,128]{1,0:T(8,128)S(1)}, u32[]{:S(2)}, u32[]{:S(2)}) collective-permute-start(f32[24,128]{1,0:T(8,128)S(1)} %get-tuple-element.19), channel_id=1, source_target_pairs={{0,63},{1,2},{2,1},{3,4},{4,3},{5,6},{6,5},{7,8},{8,7},{9,10},{10,... | collective-permute-start | bytes 36872 | tf_op jit(solution)/shard_map/ppermute | solution.py:432
  5.9 20.3 %copy-start = (s32[8,128]{1,0:T(8,128)S(1)}, s32[8,128]{1,0:T(8,128)}, u32[]{:S(2)}) copy-start(s32[8,128]{1,0:T(8,128)} %offsets.3) | copy-start | bytes 12292
  5.9 20.3 %copy-start.1 = (f32[8]{0:T(128)S(1)}, f32[8]{0:T(128)}, u32[]{:S(2)}) copy-start(f32[8]{0:T(128)} %vol.3) | copy-start | bytes 100
  9.5 39.5 %copy-start.2 = (s32[16]{0:T(128)S(1)}, s32[16]{0:T(128)}, u32[]{:S(2)}) copy-start(s32[16]{0:T(128)} %bucket.3) | copy-start | bytes 196
  9.5 39.5 %copy-start.3 = (f32[16]{0:T(128)S(1)}, f32[16]{0:T(128)}, u32[]{:S(2)}) copy-start(f32[16]{0:T(128)} %bump.1) | copy-start | bytes 196
  9.6 10.6 %collective-permute-start.2 = (f32[664,128]{1,0:T(8,128)S(1)}, f32[664,128]{1,0:T(8,128)S(1)}, u32[]{:S(2)}, u32[]{:S(2)}) collective-permute-start(f32[664,128]{1,0:T(8,128)S(1)} %get-tuple-element.21), channel_id=1, source_target_pairs={{0,64},{64,128},{128,192},{192,0},{1,65},{65,129},{129,193},{193,1... | collective-permute-start | bytes 1019912 | tf_op jit(solution)/shard_map/ppermute | solution.py:437
  9.7 12.2 %collective-permute-start.3 = (f32[664,128]{1,0:T(8,128)S(1)}, f32[664,128]{1,0:T(8,128)S(1)}, u32[]{:S(2)}, u32[]{:S(2)}) collective-permute-start(f32[664,128]{1,0:T(8,128)S(1)} %get-tuple-element.22), channel_id=1, source_target_pairs={{0,128},{64,192},{128,0},{192,64},{1,129},{65,193},{129,1},{193,65... | collective-permute-start | bytes 1019912 | tf_op jit(solution)/shard_map/ppermute | solution.py:438
  11.9 14.3 %collective-permute-start.4 = (f32[664,128]{1,0:T(8,128)S(1)}, f32[664,128]{1,0:T(8,128)S(1)}, u32[]{:S(2)}, u32[]{:S(2)}) collective-permute-start(f32[664,128]{1,0:T(8,128)S(1)} %get-tuple-element.23), channel_id=1, source_target_pairs={{0,192},{64,0},{128,64},{192,128},{1,193},{65,1},{129,65},{193,129... | collective-permute-start | bytes 1019912 | tf_op jit(solution)/shard_map/ppermute | solution.py:439
  29.5 18.2 %collective-permute-start.7 = (f32[576,128]{1,0:T(8,128)S(1)}, f32[576,128]{1,0:T(8,128)S(1)}, u32[]{:S(2)}, u32[]{:S(2)}) collective-permute-start(f32[576,128]{1,0:T(8,128)S(1)} %get-tuple-element.26.own), channel_id=1, source_target_pairs={{0,192},{64,0},{128,64},{192,128},{1,193},{65,1},{129,65},{193,129... | collective-permute-start | bytes 884744 | tf_op jit(solution)/shard_map/ppermute | solution.py:420
  32.9 14.8 %collective-permute-start.6 = (f32[576,128]{1,0:T(8,128)S(1)}, f32[576,128]{1,0:T(8,128)S(1)}, u32[]{:S(2)}, u32[]{:S(2)}) collective-permute-start(f32[576,128]{1,0:T(8,128)S(1)} %get-tuple-element.26.own), channel_id=1, source_target_pairs={{0,128},{64,192},{128,0},{192,64},{1,129},{65,193},{129,1},{193,65... | collective-permute-start | bytes 884744 | tf_op jit(solution)/shard_map/ppermute | solution.py:420
  32.9 16.1 %collective-permute-start.5 = (f32[576,128]{1,0:T(8,128)S(1)}, f32[576,128]{1,0:T(8,128)S(1)}, u32[]{:S(2)}, u32[]{:S(2)}) collective-permute-start(f32[576,128]{1,0:T(8,128)S(1)} %get-tuple-element.26.own), channel_id=1, source_target_pairs={{0,64},{64,128},{128,192},{192,0},{1,65},{65,129},{129,193},{193,1... | collective-permute-start | bytes 884744 | tf_op jit(solution)/shard_map/ppermute | solution.py:420
  33.5 23.4 %all-to-all-start = ((f32[64,1,128]{2,1,0:T(1,128)}), f32[64,1,128]{2,1,0:T(1,128)S(1)}, u32[]{:S(2)}, u32[]{:S(2)}) async-start(f32[64,1,128]{2,1,0:T(1,128)} %bitcast.13), calls=%async_computation | async-start | bytes 65536 | tf_op jit(solution)/shard_map/all_to_all | solution.py:445
  56.9 3.2 %collective-permute-start.10 = (f32[8,128]{1,0:T(8,128)S(1)}, f32[8,128]{1,0:T(8,128)S(1)}, u32[]{:S(2)}, u32[]{:S(2)}) collective-permute-start(f32[8,128]{1,0:T(8,128)S(1)} %total.1.own), channel_id=1, source_target_pairs={{0,192},{64,0},{128,64},{192,128},{1,193},{65,1},{129,65},{193,129... | collective-permute-start | bytes 12296 | tf_op jit(solution)/shard_map/ppermute | solution.py:420
  59.4 4.0 %collective-permute-start.9 = (f32[8,128]{1,0:T(8,128)S(1)}, f32[8,128]{1,0:T(8,128)S(1)}, u32[]{:S(2)}, u32[]{:S(2)}) collective-permute-start(f32[8,128]{1,0:T(8,128)S(1)} %total.1.own), channel_id=1, source_target_pairs={{0,128},{64,192},{128,0},{192,64},{1,129},{65,193},{129,1},{193,65... | collective-permute-start | bytes 12296 | tf_op jit(solution)/shard_map/ppermute | solution.py:420
  60.1 3.7 %collective-permute-start.8 = (f32[8,128]{1,0:T(8,128)S(1)}, f32[8,128]{1,0:T(8,128)S(1)}, u32[]{:S(2)}, u32[]{:S(2)}) collective-permute-start(f32[8,128]{1,0:T(8,128)S(1)} %total.1.own), channel_id=1, source_target_pairs={{0,64},{64,128},{128,192},{192,0},{1,65},{65,129},{129,193},{193,1... | collective-permute-start | bytes 12296 | tf_op jit(solution)/shard_map/ppermute | solution.py:420

commit v3 on v2

--- a/solution.py
+++ b/solution.py
@@ -6,6 +6,7 @@
 from jax.sharding import PartitionSpec as P
 
 NODE_AXES = ("nx", "ny")
+ALL_AXES = ("bump", "nx", "ny")
 LANES = 128
 ROWS_PER_STEP = 5
 STEPS = 8
@@ -26,6 +27,7 @@
 MESSAGE = TABLE_ROWS + GHOST_ROWS
 HALO = 24
 VALUES = (STEPS + 1) * CHUNK
+HALF = VALUES // 2
 
 EXPAND_COST = pl.CostEstimate(flops=100_000_000, bytes_accessed=100_000_000, transcendentals=0)
 
@@ -288,22 +290,24 @@
         values = weigh(weights, reach)
     out[0:CHUNK, :] = values[0:CHUNK]
     weight = positions[pl.ds(start, CHUNK), :]
-    lane8 = lax.broadcasted_iota(jnp.int32, (8, LANES), 1)
-    held = jnp.zeros((8, LANES), jnp.float32)
+    lines = []
     for s in range(STEPS):
         slope = slopes[s][0:CHUNK]
         out[(s + 1) * CHUNK : (s + 2) * CHUNK, :] = slope
-        total = jnp.sum(jnp.sum(weight * slope, axis=0, keepdims=True), axis=1, keepdims=True)
-        held = jnp.where(lane8 == s, total, held)
-    sums[...] = jnp.broadcast_to(held[0:1, :], sums.shape)
-
-
-def roll_back(messages, payoff, positions, offsets, one, two, vol, groups):
+        lines.append(jnp.sum(weight * slope, axis=0, keepdims=True))
+    totals = jnp.sum(jnp.concatenate(lines), axis=1, keepdims=True)
+    step = lax.broadcasted_iota(jnp.int32, (STEPS, LANES), 0)
+    own_lane = lax.broadcasted_iota(jnp.int32, (STEPS, LANES), 1) == step
+    line = jnp.sum(jnp.where(own_lane, totals, 0.0), axis=0, keepdims=True)
+    sums[...] = jnp.broadcast_to(line, sums.shape)
+
+
+def roll_back(messages, payoff, positions, offsets, one, two, vol, peers):
     return pl.pallas_call(
         roll_kernel,
         out_shape=(
             jax.ShapeDtypeStruct((VALUES, LANES), jnp.float32),
-            jax.ShapeDtypeStruct((groups, LANES), jnp.float32),
+            jax.ShapeDtypeStruct((peers, LANES), jnp.float32),
         ),
         in_specs=[vmem()] * (WORKERS + 5) + [smem()],
         out_specs=(vmem(), vmem()),
@@ -334,90 +338,103 @@
     return stores
 
 
-def expand_kernel(own, from_m1, from_m2, from_p1, vol, bucket, bump, out, rate, built, done):
+def rates(vol, bucket, bump):
+    return [2.0 * vol[bucket[b]] + bump[b] for b in range(CURVES)]
+
+
+def expand_chunks(parts, vol, bucket, bump, out, built, done):
     me = lax.axis_index("bump")
-    for b in range(CURVES):
-        rate[b] = 2.0 * vol[bucket[b]] + bump[b]
+    rate = rates(vol, bucket, bump)
     stores = []
-    for k, (source, turn) in enumerate(((own, 0), (from_m1, 3), (from_m2, 2), (from_p1, 1))):
+    for k, (source, turn) in enumerate(parts):
         build(source, built.at[k], rate, bucket, bump)
         stores += write(built.at[k], out, lax.rem(me + turn, WORKERS), done.at[k])
     for store in stores:
         store.wait()
 
 
-def expand(parts, vol, bucket, bump):
+def expand_kernel(own, from_m1, from_p1, vol, bucket, bump, out, built, done):
+    parts = ((own, 0), (from_m1, WORKERS - 1), (from_p1, 1))
+    expand_chunks(parts, vol, bucket, bump, out, built, done)
+
+
+def scratch(chunks):
     tiles = CURVES // 8
-    laid, rate = pl.pallas_call(
+    return [
+        pltpu.VMEM((chunks, tiles, CHUNK * 8, LANES), jnp.float32),
+        pltpu.SemaphoreType.DMA((chunks, tiles)),
+    ]
+
+
+def expand(own, from_m1, from_p1, vol, bucket, bump):
+    return pl.pallas_call(
         expand_kernel,
-        out_shape=(
-            jax.ShapeDtypeStruct((tiles, ROWS * 8, LANES), jnp.float32),
-            jax.ShapeDtypeStruct((CURVES,), jnp.float32),
-        ),
-        in_specs=[vmem()] * WORKERS + [smem()] * 3,
-        out_specs=(anywhere(), smem()),
-        scratch_shapes=[
-            pltpu.VMEM((WORKERS, tiles, CHUNK * 8, LANES), jnp.float32),
-            pltpu.SemaphoreType.DMA((WORKERS, tiles)),
-        ],
+        out_shape=jax.ShapeDtypeStruct((CURVES // 8, ROWS * 8, LANES), jnp.float32),
+        in_specs=[vmem()] * 3 + [smem()] * 3,
+        out_specs=anywhere(),
+        scratch_shapes=scratch(3),
         compiler_params=params(),
         cost_estimate=EXPAND_COST,
         name="expand",
-    )(*parts, vol, bucket, bump)
+    )(own, from_m1, from_p1, vol, bucket, bump)
+
+
+def complete_kernel(low, high, vol, bucket, bump, started, out, picks, joined, built, done):
+    del started
+    rate = rates(vol, bucket, bump)
+    row = lax.broadcasted_iota(jnp.int32, (CURVES, LANES), 0)
+    lane = lax.broadcasted_iota(jnp.int32, (CURVES, LANES), 1)
+    pick = jnp.zeros((CURVES, LANES), jnp.float32)
+    for b in range(CURVES):
+        pick = jnp.where(jnp.logical_and(row == b, lane == bucket[b]), rate[b], pick)
+    picks[...] = pick
+    joined[0:HALF, :] = low[...]
+    joined[HALF:, :] = high[...]
+    expand_chunks(((joined, WORKERS - 2),), vol, bucket, bump, out, built, done)
+
+
+def complete(low, high, vol, bucket, bump, started):
+    tiles = CURVES // 8
+    laid, picks = pl.pallas_call(
+        complete_kernel,
+        out_shape=(
+            jax.ShapeDtypeStruct(started.shape, started.dtype),
+            jax.ShapeDtypeStruct((CURVES, LANES), jnp.float32),
+        ),
+        in_specs=[vmem()] * 2 + [smem()] * 3 + [anywhere()],
+        out_specs=(anywhere(), vmem()),
+        scratch_shapes=[pltpu.VMEM((VALUES, LANES), jnp.float32)] + scratch(1),
+        input_output_aliases={5: 0},
+        compiler_params=params(),
+        cost_estimate=EXPAND_COST,
+        name="complete",
+    )(low, high, vol, bucket, bump, started)
     curves = laid.reshape(tiles, ROWS, 8, LANES).transpose(0, 2, 1, 3)
-    return curves.reshape(CURVES, ROWS * LANES), rate
-
-
-def total_kernel(shared, out):
-    out[...] = jnp.broadcast_to(jnp.sum(shared[...], axis=0, keepdims=True), out.shape)
-
-
-def total(shared):
-    return pl.pallas_call(
-        total_kernel,
-        out_shape=jax.ShapeDtypeStruct((8, LANES), jnp.float32),
-        in_specs=[vmem()],
-        out_specs=vmem(),
-        compiler_params=params(),
-        name="total",
-    )(shared)
-
-
-def vega_kernel(own, from_m1, from_m2, from_p1, bucket, rate, vega):
-    totals = own[...] + from_m1[...] + from_m2[...] + from_p1[...]
-    lane = lax.broadcasted_iota(jnp.int32, (8, LANES), 1)
-    row = lax.broadcasted_iota(jnp.int32, (8, LANES), 0)
-    line = jnp.zeros((1, LANES), jnp.float32)
-    for tile in range(CURVES // 8):
-        picked = jnp.zeros((8, LANES), jnp.float32)
-        for r in range(8):
-            b = tile * 8 + r
-            hit = jnp.logical_and(row == r, lane == bucket[b])
-            picked = jnp.where(hit, rate[b] * totals, picked)
-        entry = jnp.sum(picked, axis=1, keepdims=True)
-        line += jnp.sum(
-            jnp.where(lane == row + tile * 8, entry, 0.0), axis=0, keepdims=True
-        )
+    return curves.reshape(CURVES, ROWS * LANES), picks
+
+
+def vega_kernel(shared, picks, vega):
+    totals = jnp.sum(shared[...], axis=0, keepdims=True)
+    entry = jnp.sum(picks[...] * totals, axis=1, keepdims=True)
+    row = lax.broadcasted_iota(jnp.int32, (CURVES, LANES), 0)
+    lane = lax.broadcasted_iota(jnp.int32, (CURVES, LANES), 1)
+    line = jnp.sum(jnp.where(lane == row, entry, 0.0), axis=0, keepdims=True)
     vega[...] = line[:, :CURVES]
 
 
-def vegas(parts, bucket, rate):
+def vegas(shared, picks):
     return pl.pallas_call(
         vega_kernel,
         out_shape=jax.ShapeDtypeStruct((1, CURVES), jnp.float32),
-        in_specs=[vmem()] * WORKERS + [smem(), smem()],
+        in_specs=[vmem(), vmem()],
         out_specs=vmem(),
         compiler_params=params(),
         name="vegas",
-    )(*parts, bucket, rate).reshape(CURVES)
+    )(shared, picks).reshape(CURVES)
 
 
 def rotated(by):
     return [(i, (i + by) % WORKERS) for i in range(WORKERS)]
-
-
-def exchanged(array, axis):
-    return (array,) + tuple(lax.ppermute(array, axis, rotated(by)) for by in (1, 2, -1))
 
 
 def on_device(payoff, positions, tables, offsets, vol_curve, bucket, bump_size):
@@ -438,16 +455,20 @@
         lax.ppermute(messages[2], "bump", rotated(2)),
         lax.ppermute(messages[3], "bump", rotated(-1)),
     )
+    peers = lax.axis_size(ALL_AXES)
     arrays, sums = roll_back(
-        received, payoff_rows, position_rows, offsets, one, two, vol_curve, groups
-    )
-    bumped_values, rate = expand(exchanged(arrays, "bump"), vol_curve, bucket, bump_size)
+        received, payoff_rows, position_rows, offsets, one, two, vol_curve, peers
+    )
+    from_m1 = lax.ppermute(arrays, "bump", rotated(1))
+    from_p1 = lax.ppermute(arrays, "bump", rotated(-1))
+    low = lax.ppermute(from_m1[:HALF], "bump", rotated(1))
+    high = lax.ppermute(from_p1[HALF:], "bump", rotated(-1))
+    started = expand(arrays, from_m1, from_p1, vol_curve, bucket, bump_size)
+    bumped_values, picks = complete(low, high, vol_curve, bucket, bump_size, started)
     shared = lax.all_to_all(
-        sums.reshape(groups, 1, LANES), NODE_AXES, split_axis=0, concat_axis=0, tiled=True
-    )
-    shared, rate = lax.optimization_barrier((shared, rate))
-    totals = exchanged(total(shared.reshape(groups, LANES)), "bump")
-    return (bumped_values, vegas(totals, bucket, rate))
+        sums.reshape(peers, 1, LANES), ALL_AXES, split_axis=0, concat_axis=0, tiled=True
+    )
+    return (bumped_values, vegas(shared.reshape(peers, LANES), picks))
 
 
 def solution(mesh):

time: 65.1 us -> 62.3 us (0.957)
  waiting for transfers between devices: 25.6 us -> 22 us
    all_to_all x1, waiting for transfers between devices: 5.2 us -> 1.7 us  [on_device(): lax.all_to_all(sums.reshape(peers, 1, LANES), ALL_AXES, split_axis=0, con...]
    all_to_all x1, starting transfers between devices: 14.2 us -> 15.6 us  [on_device(): lax.all_to_all(sums.reshape(peers, 1, LANES), ALL_AXES, split_axis=0, con...]
    ppermute x6 -> x4, starting transfers between devices: 7.13 us -> 6.22 us  [the longest x1 3.41 us: on_device(): from_p1 = lax.ppermute(arrays, 'bump', rotated(-1))]
    pallas_call x2, Pallas kernels: 2.68 us -> 3.42 us  [the longest x1 1.88 us: expand(): pl.pallas_call(expand_kernel, out_shape=jax.ShapeDtypeStruct((CURVES // 8...]
    ppermute x6 -> x4, waiting for transfers between devices: 4.94 us -> 4.84 us  [the longest x1 3.47 us: on_device(): low = lax.ppermute(from_m1[:HALF], 'bump', rotated(1))]
  transfers between devices with their start and end apart: 12 -> 10, of which waited for: 9 -> 7; matrix products, arithmetic and copies ran while one was open for 0% -> 0% of each run, Pallas kernels for 6% -> 8%
where the time goes in v3:
time: 62.3 us; the launch traced here: 62.1 us
  starting transfers between devices  29.4 us (47%)
  waiting for transfers between devices  22 us (35%)
  Pallas kernels  9.86 us (16%)
  between operations  0.77 us (1%)
    all_to_all x1, starting transfers between devices, on_device(): lax.all_to_all(sums.reshape(peers, 1, LANES), ALL_AXES, split_axis=0, con...  15.6 us
    ppermute x1, waiting for transfers between devices, on_device(): lax.ppermute(messages[1], 'bump', rotated(1))  7.23 us
    ppermute x1, waiting for transfers between devices, on_device(): lax.ppermute(messages[3], 'bump', rotated(-1))  4.18 us
    ppermute x1, waiting for transfers between devices, on_device(): low = lax.ppermute(from_m1[:HALF], 'bump', rotated(1))  3.47 us
    pallas_call x1, Pallas kernels, roll_back(): pl.pallas_call(roll_kernel, out_shape=(jax.ShapeDtypeStruct((VALUES, LANE...  3.43 us
    ppermute x1, starting transfers between devices, on_device(): from_p1 = lax.ppermute(arrays, 'bump', rotated(-1))  3.41 us
    ppermute x1, starting transfers between devices, on_device(): one = lax.ppermute(one, NODE_AXES, with_next)  3.33 us
    ppermute x1, starting transfers between devices, on_device(): high = lax.ppermute(from_p1[HALF:], 'bump', rotated(-1))  2.73 us
  transfers between devices with their start and end apart: 10, of which 7 were waited for; matrix products, arithmetic and copies ran while one was open for 0% of the time, Pallas kernels for 8%

profile of v3, /device:TPU:1, one launch (start us, length us, event | category | flops | bytes accessed | tf_op | source)
XLA Modules:
  0.0 62.1 jit_solution(8644081968843504448)
XLA Ops:
  0.6 0.0 copy-start
  0.6 0.0 copy-start.1
  0.6 0.9 %edges.1 = (f32[24,128]{1,0:T(8,128)S(1)}, f32[24,128]{1,0:T(8,128)S(1)}) custom-call(f32[5,512,128]{2,1,0:T(8,128)} %bitcast.21, f32[256,128]{1,0:T(8,128)} %bitcast.23, s32[8,128]{1,0:T(8,128)} %offsets.3), custom_call_target="tpu_custom_call" | custom-call | tf_op jit(solution)/shard_map/edges/pallas_call | solution.py:105
  1.6 3.3 %collective-permute-start = (f32[24,128]{1,0:T(8,128)S(1)}, f32[24,128]{1,0:T(8,128)S(1)}, u32[]{:S(2)}, u32[]{:S(2)}) collective-permute-start(f32[24,128]{1,0:T(8,128)S(1)} %get-tuple-element.16), channel_id=1, source_target_pairs={{0,1},{1,0},{2,3},{3,2},{4,5},{5,4},{6,7},{7,6},{8,9},{9,8},{10,11... | collective-permute-start | bytes 36872 | tf_op jit(solution)/shard_map/ppermute | solution.py:448
  4.9 1.0 %collective-permute-start.1 = (f32[24,128]{1,0:T(8,128)S(1)}, f32[24,128]{1,0:T(8,128)S(1)}, u32[]{:S(2)}, u32[]{:S(2)}) collective-permute-start(f32[24,128]{1,0:T(8,128)S(1)} %get-tuple-element.17), channel_id=1, source_target_pairs={{0,63},{1,2},{2,1},{3,4},{4,3},{5,6},{6,5},{7,8},{8,7},{9,10},{10,... | collective-permute-start | bytes 36872 | tf_op jit(solution)/shard_map/ppermute | solution.py:449
  5.9 1.4 %load.1 = (f32[5,512,128]{2,1,0:T(8,128)S(1)}, f32[256,128]{1,0:T(8,128)S(1)}, f32[256,128]{1,0:T(8,128)S(1)}) custom-call(f32[5,512,128]{2,1,0:T(8,128)} %bitcast.22, f32[256,128]{1,0:T(8,128)} %bitcast.24, f32[256,128]{1,0:T(8,128)} %bitcast.25), custom_call_target="tpu_custom_call" | custom-call | bytes 6000000 | tf_op jit(solution)/shard_map/load/pallas_call | solution.py:136
  7.3 0.0 copy-start.2
  7.3 0.0 copy-start.3
  7.3 0.0 collective-permute-done.one
  7.3 2.2 %collective-permute-done.1.two = f32[24,128]{1,0:T(8,128)S(1)} collective-permute-done((f32[24,128]{1,0:T(8,128)S(1)}, f32[24,128]{1,0:T(8,128)S(1)}, u32[]{:S(2)}, u32[]{:S(2)}) %collective-permute-start.1) | collective-permute-done | bytes 12320 | tf_op jit(solution)/shard_map/ppermute | solution.py:449
  9.5 0.1 pack.1
  9.6 0.1 collective-permute-start.2
  9.7 2.2 %collective-permute-start.3 = (f32[664,128]{1,0:T(8,128)S(1)}, f32[664,128]{1,0:T(8,128)S(1)}, u32[]{:S(2)}, u32[]{:S(2)}) collective-permute-start(f32[664,128]{1,0:T(8,128)S(1)} %get-tuple-element.20), channel_id=1, source_target_pairs={{0,128},{64,192},{128,0},{192,64},{1,129},{65,193},{129,1},{193,65... | collective-permute-start | bytes 1019912 | tf_op jit(solution)/shard_map/ppermute | solution.py:455
  11.9 1.1 %collective-permute-start.4 = (f32[664,128]{1,0:T(8,128)S(1)}, f32[664,128]{1,0:T(8,128)S(1)}, u32[]{:S(2)}, u32[]{:S(2)}) collective-permute-start(f32[664,128]{1,0:T(8,128)S(1)} %get-tuple-element.21), channel_id=1, source_target_pairs={{0,192},{64,0},{128,64},{192,128},{1,193},{65,1},{129,65},{193,129... | collective-permute-start | bytes 1019912 | tf_op jit(solution)/shard_map/ppermute | solution.py:456
  13.0 7.2 %collective-permute-done.2.from_m1 = f32[664,128]{1,0:T(8,128)S(1)} collective-permute-done((f32[664,128]{1,0:T(8,128)S(1)}, f32[664,128]{1,0:T(8,128)S(1)}, u32[]{:S(2)}, u32[]{:S(2)}) %collective-permute-start.2) | collective-permute-done | bytes 340000 | tf_op jit(solution)/shard_map/ppermute | solution.py:454
  20.2 1.8 %collective-permute-done.3.from_m2 = f32[664,128]{1,0:T(8,128)S(1)} collective-permute-done((f32[664,128]{1,0:T(8,128)S(1)}, f32[664,128]{1,0:T(8,128)S(1)}, u32[]{:S(2)}, u32[]{:S(2)}) %collective-permute-start.3) | collective-permute-done | bytes 340000 | tf_op jit(solution)/shard_map/ppermute | solution.py:455
  22.0 4.2 %collective-permute-done.4.from_p1 = f32[664,128]{1,0:T(8,128)S(1)} collective-permute-done((f32[664,128]{1,0:T(8,128)S(1)}, f32[664,128]{1,0:T(8,128)S(1)}, u32[]{:S(2)}, u32[]{:S(2)}) %collective-permute-start.4) | collective-permute-done | bytes 340000 | tf_op jit(solution)/shard_map/ppermute | solution.py:456
  26.2 0.0 copy-done
  26.2 0.0 copy-done.1
  26.2 3.4 %roll_back.1 = (f32[576,128]{1,0:T(8,128)S(1)}, f32[256,128]{1,0:T(8,128)}) custom-call(f32[664,128]{1,0:T(8,128)S(1)} %get-tuple-element.18.own, f32[664,128]{1,0:T(8,128)S(1)} %collective-permute-done.2.from_m1, f32[664,128]{1,0:T(8,128)S(1)} %collective-permute-done.3.from_m2, f32[664,128]{1,0:T(8,128)S(1)} %collective-permute-done.4.from_p1, ...), custom_call_target="tpu_custom_call" | custom-call | tf_op jit(solution)/shard_map/roll_back/pallas_call | solution.py:306
  29.6 3.4 %collective-permute-start.7 = (f32[576,128]{1,0:T(8,128)S(1)}, f32[576,128]{1,0:T(8,128)S(1)}, u32[]{:S(2)}, u32[]{:S(2)}) collective-permute-start(f32[576,128]{1,0:T(8,128)S(1)} %get-tuple-element.24.own), channel_id=1, source_target_pairs={{0,192},{64,0},{128,64},{192,128},{1,193},{65,1},{129,65},{193,129... | collective-permute-start | bytes 884744 | tf_op jit(solution)/shard_map/ppermute | solution.py:463
  33.0 0.0 collective-permute-start.5
  33.0 15.6 %all-to-all-start = ((f32[256,1,128]{2,1,0:T(1,128)}), f32[256,1,128]{2,1,0:T(1,128)S(1)}, u32[]{:S(2)}, u32[]{:S(2)}) async-start(f32[256,1,128]{2,1,0:T(1,128)} %bitcast.13), calls=%async_computation | async-start | bytes 262144 | tf_op jit(solution)/shard_map/all_to_all | solution.py:468
  48.6 0.0 collective-permute-done.7.from_p1
  48.6 2.7 %collective-permute-start.8 = (f32[288,128]{1,0:T(8,128)S(1)}, f32[288,128]{1,0:T(8,128)S(1)}, u32[]{:S(2)}, u32[]{:S(2)}) collective-permute-start(f32[288,128]{1,0:T(8,128)S(1)} %slice.9), channel_id=1, source_target_pairs={{0,192},{64,0},{128,64},{192,128},{1,193},{65,1},{129,65},{193,129... | collective-permute-start | bytes 442376 | tf_op jit(solution)/shard_map/ppermute | solution.py:465
  51.3 0.0 collective-permute-done.5.from_m1
  51.4 0.1 collective-permute-start.6
  51.5 0.0 copy-done.2
  51.5 0.0 copy-done.3
  51.5 1.9 %expand.1.started = f32[2,2048,128]{2,1,0:T(8,128)} custom-call(f32[576,128]{1,0:T(8,128)S(1)} %get-tuple-element.24.own, f32[576,128]{1,0:T(8,128)S(1)} %collective-permute-done.5.from_m1, f32[576,128]{1,0:T(8,128)S(1)} %collective-permute-done.7.from_p1, f32[8]{0:T(128)S(1)} %copy-done.1, s32[16]{0:T(128)S(1)} %copy-done.2, f32[16]{0:T(128)S(1)} %copy-done.3), custom_call_target="tpu_custom_call" | custom-call | flops 100000000 | bytes 100000000 | tf_op jit(solution)/shard_map/expand/pallas_call | solution.py:370
  53.4 1.4 %collective-permute-done.8.high = f32[288,128]{1,0:T(8,128)S(1)} collective-permute-done((f32[288,128]{1,0:T(8,128)S(1)}, f32[288,128]{1,0:T(8,128)S(1)}, u32[]{:S(2)}, u32[]{:S(2)}) %collective-permute-start.8) | collective-permute-done | bytes 147488 | tf_op jit(solution)/shard_map/ppermute | solution.py:465
  54.7 3.5 %collective-permute-done.6.low = f32[288,128]{1,0:T(8,128)S(1)} collective-permute-done((f32[288,128]{1,0:T(8,128)S(1)}, f32[288,128]{1,0:T(8,128)S(1)}, u32[]{:S(2)}, u32[]{:S(2)}) %collective-permute-start.6) | collective-permute-done | bytes 147488 | tf_op jit(solution)/shard_map/ppermute | solution.py:464
  58.2 1.5 %complete.1 = (f32[2,2048,128]{2,1,0:T(8,128)}, f32[16,128]{1,0:T(8,128)S(1)}) custom-call(f32[288,128]{1,0:T(8,128)S(1)} %collective-permute-done.6.low, f32[288,128]{1,0:T(8,128)S(1)} %collective-permute-done.8.high, f32[8]{0:T(128)S(1)} %copy-done.1, s32[16]{0:T(128)S(1)} %copy-done.2, f32[16]{0:T(128)S(1)} %copy-done.3, ...), custom_call_target="tpu_custom_call", output_to_operand_aliasing={{0}: (5, {})} | custom-call | flops 100000000 | bytes 100000000 | tf_op jit(solution)/shard_map/complete/pallas_call | solution.py:398
  59.7 1.7 %all-to-all-done = f32[256,1,128]{2,1,0:T(1,128)S(1)} async-done(((f32[256,1,128]{2,1,0:T(1,128)}), f32[256,1,128]{2,1,0:T(1,128)S(1)}, u32[]{:S(2)}, u32[]{:S(2)}) %all-to-all-start) | async-done | bytes 131104 | tf_op jit(solution)/shard_map/all_to_all | solution.py:468
  61.5 0.6 %vegas.1 = f32[1,16]{1,0:T(1,128)} custom-call(f32[256,128]{1,0:T(8,128)S(1)} %bitcast.19, f32[16,128]{1,0:T(8,128)S(1)} %get-tuple-element.27.picks), custom_call_target="tpu_custom_call" | custom-call | tf_op jit(solution)/shard_map/vegas/pallas_call | solution.py:426
  (2 shorter events, 0.0 us)
Async XLA Ops:
  0.6 25.5 %copy-start = (s32[8,128]{1,0:T(8,128)S(1)}, s32[8,128]{1,0:T(8,128)}, u32[]{:S(2)}) copy-start(s32[8,128]{1,0:T(8,128)} %offsets.3) | copy-start | bytes 12292
  0.6 25.5 %copy-start.1 = (f32[8]{0:T(128)S(1)}, f32[8]{0:T(128)}, u32[]{:S(2)}) copy-start(f32[8]{0:T(128)} %vol.5) | copy-start | bytes 100
  1.6 5.7 %collective-permute-start = (f32[24,128]{1,0:T(8,128)S(1)}, f32[24,128]{1,0:T(8,128)S(1)}, u32[]{:S(2)}, u32[]{:S(2)}) collective-permute-start(f32[24,128]{1,0:T(8,128)S(1)} %get-tuple-element.16), channel_id=1, source_target_pairs={{0,1},{1,0},{2,3},{3,2},{4,5},{5,4},{6,7},{7,6},{8,9},{9,8},{10,11... | collective-permute-start | bytes 36872 | tf_op jit(solution)/shard_map/ppermute | solution.py:448
  4.9 4.6 %collective-permute-start.1 = (f32[24,128]{1,0:T(8,128)S(1)}, f32[24,128]{1,0:T(8,128)S(1)}, u32[]{:S(2)}, u32[]{:S(2)}) collective-permute-start(f32[24,128]{1,0:T(8,128)S(1)} %get-tuple-element.17), channel_id=1, source_target_pairs={{0,63},{1,2},{2,1},{3,4},{4,3},{5,6},{6,5},{7,8},{8,7},{9,10},{10,... | collective-permute-start | bytes 36872 | tf_op jit(solution)/shard_map/ppermute | solution.py:449
  7.3 44.2 %copy-start.2 = (s32[16]{0:T(128)S(1)}, s32[16]{0:T(128)}, u32[]{:S(2)}) copy-start(s32[16]{0:T(128)} %bucket.3) | copy-start | bytes 196
  7.3 44.2 %copy-start.3 = (f32[16]{0:T(128)S(1)}, f32[16]{0:T(128)}, u32[]{:S(2)}) copy-start(f32[16]{0:T(128)} %bump.3) | copy-start | bytes 196
  9.6 10.6 %collective-permute-start.2 = (f32[664,128]{1,0:T(8,128)S(1)}, f32[664,128]{1,0:T(8,128)S(1)}, u32[]{:S(2)}, u32[]{:S(2)}) collective-permute-start(f32[664,128]{1,0:T(8,128)S(1)} %get-tuple-element.19), channel_id=1, source_target_pairs={{0,64},{64,128},{128,192},{192,0},{1,65},{65,129},{129,193},{193,1... | collective-permute-start | bytes 1019912 | tf_op jit(solution)/shard_map/ppermute | solution.py:454
  9.7 12.3 %collective-permute-start.3 = (f32[664,128]{1,0:T(8,128)S(1)}, f32[664,128]{1,0:T(8,128)S(1)}, u32[]{:S(2)}, u32[]{:S(2)}) collective-permute-start(f32[664,128]{1,0:T(8,128)S(1)} %get-tuple-element.20), channel_id=1, source_target_pairs={{0,128},{64,192},{128,0},{192,64},{1,129},{65,193},{129,1},{193,65... | collective-permute-start | bytes 1019912 | tf_op jit(solution)/shard_map/ppermute | solution.py:455
  11.9 14.3 %collective-permute-start.4 = (f32[664,128]{1,0:T(8,128)S(1)}, f32[664,128]{1,0:T(8,128)S(1)}, u32[]{:S(2)}, u32[]{:S(2)}) collective-permute-start(f32[664,128]{1,0:T(8,128)S(1)} %get-tuple-element.21), channel_id=1, source_target_pairs={{0,192},{64,0},{128,64},{192,128},{1,193},{65,1},{129,65},{193,129... | collective-permute-start | bytes 1019912 | tf_op jit(solution)/shard_map/ppermute | solution.py:456
  29.6 19.0 %collective-permute-start.7 = (f32[576,128]{1,0:T(8,128)S(1)}, f32[576,128]{1,0:T(8,128)S(1)}, u32[]{:S(2)}, u32[]{:S(2)}) collective-permute-start(f32[576,128]{1,0:T(8,128)S(1)} %get-tuple-element.24.own), channel_id=1, source_target_pairs={{0,192},{64,0},{128,64},{192,128},{1,193},{65,1},{129,65},{193,129... | collective-permute-start | bytes 884744 | tf_op jit(solution)/shard_map/ppermute | solution.py:463
  33.0 18.3 %collective-permute-start.5 = (f32[576,128]{1,0:T(8,128)S(1)}, f32[576,128]{1,0:T(8,128)S(1)}, u32[]{:S(2)}, u32[]{:S(2)}) collective-permute-start(f32[576,128]{1,0:T(8,128)S(1)} %get-tuple-element.24.own), channel_id=1, source_target_pairs={{0,64},{64,128},{128,192},{192,0},{1,65},{65,129},{129,193},{193,1... | collective-permute-start | bytes 884744 | tf_op jit(solution)/shard_map/ppermute | solution.py:462
  33.0 28.4 %all-to-all-start = ((f32[256,1,128]{2,1,0:T(1,128)}), f32[256,1,128]{2,1,0:T(1,128)S(1)}, u32[]{:S(2)}, u32[]{:S(2)}) async-start(f32[256,1,128]{2,1,0:T(1,128)} %bitcast.13), calls=%async_computation | async-start | bytes 262144 | tf_op jit(solution)/shard_map/all_to_all | solution.py:468
  48.6 6.1 %collective-permute-start.8 = (f32[288,128]{1,0:T(8,128)S(1)}, f32[288,128]{1,0:T(8,128)S(1)}, u32[]{:S(2)}, u32[]{:S(2)}) collective-permute-start(f32[288,128]{1,0:T(8,128)S(1)} %slice.9), channel_id=1, source_target_pairs={{0,192},{64,0},{128,64},{192,128},{1,193},{65,1},{129,65},{193,129... | collective-permute-start | bytes 442376 | tf_op jit(solution)/shard_map/ppermute | solution.py:465
  51.4 6.8 %collective-permute-start.6 = (f32[288,128]{1,0:T(8,128)S(1)}, f32[288,128]{1,0:T(8,128)S(1)}, u32[]{:S(2)}, u32[]{:S(2)}) collective-permute-start(f32[288,128]{1,0:T(8,128)S(1)} %slice.8), channel_id=1, source_target_pairs={{0,64},{64,128},{128,192},{192,0},{1,65},{65,129},{129,193},{193,1... | collective-permute-start | bytes 442376 | tf_op jit(solution)/shard_map/ppermute | solution.py:464

commit v4 on v3

--- a/solution.py
+++ b/solution.py
@@ -68,116 +68,103 @@
     return jnp.where(even, two[...], one[...]), jnp.where(even, one[...], two[...])
 
 
-def edges_kernel(tables, payoff, offsets, one, two, held, held_payoff, held_offsets, ends, sem):
-    copies = [pltpu.make_async_copy(offsets, held_offsets, sem.at[2, 0])]
-    for side, pair, row in ((0, 0, 0), (1, PAIRS - 8, ROWS - 8)):
-        copies.append(
-            pltpu.make_async_copy(tables.at[:, pl.ds(pair, 8), :], held.at[side], sem.at[0, side])
-        )
-        copies.append(
-            pltpu.make_async_copy(
-                payoff.at[pl.ds(row, 8), :], held_payoff.at[side], sem.at[1, side]
-            )
-        )
+def pack_one(tables, k, out, before, after):
+    chunk = lax.rem(lax.axis_index("bump") + k, WORKERS)
+    start = pl.multiple_of(chunk * CHUNK_PAIRS, CHUNK_PAIRS)
+    low = pl.multiple_of(lax.rem(start + PAIRS - 8, PAIRS), 8)
+    high = pl.multiple_of(lax.rem(start + CHUNK_PAIRS, PAIRS), CHUNK_PAIRS)
+    for i in range(ROWS_PER_STEP):
+        out[i * CHUNK_PAIRS : (i + 1) * CHUNK_PAIRS, :] = tables[i, pl.ds(start, CHUNK_PAIRS), :]
+        at = slice(i * LOCAL_STEPS, (i + 1) * LOCAL_STEPS)
+        beside = tables[i, pl.ds(low, 8), :][8 - LOCAL_STEPS :]
+        if before is not None:
+            beside = jnp.where(chunk == 0, before[at, :], beside)
+        row = TABLE_ROWS + i * LOCAL_STEPS
+        out[row : row + LOCAL_STEPS, :] = beside
+        beside = tables[i, pl.ds(high, 8), :][:LOCAL_STEPS]
+        if after is not None:
+            beside = jnp.where(chunk == WORKERS - 1, after[at, :], beside)
+        row += LOCAL_ROWS
+        out[row : row + LOCAL_STEPS, :] = beside
+    out[TABLE_ROWS + 2 * LOCAL_ROWS :, :] = jnp.zeros(
+        (GHOST_ROWS - 2 * LOCAL_ROWS, LANES), jnp.float32
+    )
+
+
+def first_kernel(
+    tables,
+    payoff,
+    positions,
+    offsets,
+    held_tables,
+    held_payoff,
+    held_positions,
+    held_offsets,
+    plus2,
+    one,
+    two,
+    far,
+    ends,
+    sem,
+):
+    held = (held_tables, held_payoff, held_positions, held_offsets)
+    copies = [
+        pltpu.make_async_copy(source, target, sem.at[i])
+        for i, (source, target) in enumerate(zip((tables, payoff, positions, offsets), held))
+    ]
     for copy in copies:
         copy.start()
     for copy in copies:
         copy.wait()
-    for side, row, lane in ((0, 0, 0), (1, 7, LANES - 1)):
+    pack_one(held_tables, 2, plus2, None, None)
+    for side, pair, row, lane in ((0, 0, 0, 0), (1, PAIRS - LOCAL_STEPS, ROWS - 1, LANES - 1)):
         out = ends.at[side]
-        pair = row * (8 - LOCAL_STEPS) // 7
         for i in range(ROWS_PER_STEP):
-            out[i * LOCAL_STEPS : (i + 1) * LOCAL_STEPS, :] = held[
-                side, i, pair : pair + LOCAL_STEPS, :
+            out[i * LOCAL_STEPS : (i + 1) * LOCAL_STEPS, :] = held_tables[
+                i, pair : pair + LOCAL_STEPS, :
             ]
         out[LOCAL_ROWS : 2 * STEPS, :] = jnp.broadcast_to(
-            held_payoff[side, row : row + 1, :], (2 * STEPS - LOCAL_ROWS, LANES)
+            held_payoff[row : row + 1, :], (2 * STEPS - LOCAL_ROWS, LANES)
         )
         out[2 * STEPS : HALO, :] = jnp.broadcast_to(
             held_offsets[:, lane : lane + 1].astype(jnp.float32), (STEPS, LANES)
         )
     one[...] = jnp.where(on_even_group(), ends[1], ends[0])
     two[...] = jnp.where(on_even_group(), ends[0], ends[1])
-
-
-def edges(tables, payoff_rows, offsets):
-    shape = jax.ShapeDtypeStruct((HALO, LANES), jnp.float32)
+    far[...] = jnp.where(lax.axis_index("bump") == WORKERS // 2, ends[1], ends[0])
+
+
+def first(*arrays):
+    same = tuple(jax.ShapeDtypeStruct(array.shape, array.dtype) for array in arrays)
+    message = jax.ShapeDtypeStruct((MESSAGE, LANES), jnp.float32)
+    halo = jax.ShapeDtypeStruct((HALO, LANES), jnp.float32)
     return pl.pallas_call(
-        edges_kernel,
-        out_shape=(shape, shape),
-        in_specs=[hbm(), hbm(), hbm()],
-        out_specs=(vmem(), vmem()),
+        first_kernel,
+        out_shape=same + (message, halo, halo, halo),
+        in_specs=[hbm()] * len(arrays),
+        out_specs=(vmem(),) * (len(arrays) + 4),
         scratch_shapes=[
-            pltpu.VMEM((2, ROWS_PER_STEP, 8, LANES), jnp.float32),
-            pltpu.VMEM((2, 8, LANES), jnp.float32),
-            pltpu.VMEM((STEPS, LANES), jnp.int32),
             pltpu.VMEM((2, HALO, LANES), jnp.float32),
-            pltpu.SemaphoreType.DMA((3, 2)),
+            pltpu.SemaphoreType.DMA((len(arrays),)),
         ],
         compiler_params=params(),
-        name="edges",
-    )(*(in_hbm(array) for array in (tables, payoff_rows, offsets)))
-
-
-def load_kernel(tables, payoff, positions, held, held_payoff, held_positions, sem):
-    copies = [
-        pltpu.make_async_copy(source, target, sem.at[i])
-        for i, (source, target) in enumerate(
-            ((tables, held), (payoff, held_payoff), (positions, held_positions))
-        )
-    ]
-    for copy in copies:
-        copy.start()
-    for copy in copies:
-        copy.wait()
-
-
-def load(*arrays):
-    return pl.pallas_call(
-        load_kernel,
-        out_shape=tuple(jax.ShapeDtypeStruct(array.shape, array.dtype) for array in arrays),
-        in_specs=[hbm()] * len(arrays),
-        out_specs=(vmem(),) * len(arrays),
-        scratch_shapes=[pltpu.SemaphoreType.DMA((len(arrays),))],
-        compiler_params=params(),
-        cost_estimate=pl.CostEstimate(flops=0, bytes_accessed=6_000_000, transcendentals=0),
-        name="load",
+        name="first",
     )(*(in_hbm(array) for array in arrays))
 
 
-def pack_kernel(tables, one, two, own, plus1, plus2, plus3):
-    me = lax.axis_index("bump")
+def pack_near_kernel(tables, one, two, own, plus1, plus3):
     before, after = halos(one, two)
-    for k, out in ((1, plus1), (3, plus3), (2, plus2), (0, own)):
-        chunk = lax.rem(me + k, WORKERS)
-        below = lax.rem(chunk + WORKERS - 1, WORKERS)
-        above = lax.rem(chunk + 1, WORKERS)
-        start = pl.multiple_of(chunk * CHUNK_PAIRS, CHUNK_PAIRS)
-        low = pl.multiple_of(below * CHUNK_PAIRS + CHUNK_PAIRS - 8, 8)
-        high = pl.multiple_of(above * CHUNK_PAIRS, CHUNK_PAIRS)
-        for i in range(ROWS_PER_STEP):
-            out[i * CHUNK_PAIRS : (i + 1) * CHUNK_PAIRS, :] = tables[i, pl.ds(start, CHUNK_PAIRS), :]
-            at = slice(i * LOCAL_STEPS, (i + 1) * LOCAL_STEPS)
-            row = TABLE_ROWS + i * LOCAL_STEPS
-            out[row : row + LOCAL_STEPS, :] = jnp.where(
-                chunk == 0, before[at, :], tables[i, pl.ds(low, 8), :][8 - LOCAL_STEPS :]
-            )
-            row += LOCAL_ROWS
-            out[row : row + LOCAL_STEPS, :] = jnp.where(
-                chunk == WORKERS - 1, after[at, :], tables[i, pl.ds(high, 8), :][:LOCAL_STEPS]
-            )
-        out[TABLE_ROWS + 2 * LOCAL_ROWS :, :] = jnp.zeros(
-            (GHOST_ROWS - 2 * LOCAL_ROWS, LANES), jnp.float32
-        )
-
-
-def pack(tables, one, two):
+    for k, out in ((1, plus1), (3, plus3), (0, own)):
+        pack_one(tables, k, out, before, after)
+
+
+def pack_near(tables, one, two):
     shape = jax.ShapeDtypeStruct((MESSAGE, LANES), jnp.float32)
     return pl.pallas_call(
-        pack_kernel,
-        out_shape=(shape,) * WORKERS,
+        pack_near_kernel,
+        out_shape=(shape,) * 3,
         in_specs=[vmem()] * 3,
-        out_specs=(vmem(),) * WORKERS,
+        out_specs=(vmem(),) * 3,
         compiler_params=params(),
         name="pack",
     )(tables, one, two)
@@ -220,6 +207,7 @@
     offsets,
     one,
     two,
+    far,
     vol,
     out,
     sums,
@@ -261,11 +249,15 @@
         source = sources[k]
         for i in range(ROWS_PER_STEP):
             table[owner, i, :CHUNK_PAIRS, :] = source[i * CHUNK_PAIRS : (i + 1) * CHUNK_PAIRS, :]
+            at = slice(i * LOCAL_STEPS, (i + 1) * LOCAL_STEPS)
             low = TABLE_ROWS + i * LOCAL_STEPS
             high = low + LOCAL_ROWS
-            table[owner, i, CHUNK_PAIRS:, :] = jnp.concatenate(
-                [source[high : high + LOCAL_STEPS, :], gap, source[low : low + LOCAL_STEPS, :]]
-            )
+            ahead = source[low : low + LOCAL_STEPS, :]
+            behind = source[high : high + LOCAL_STEPS, :]
+            if k == 2:
+                ahead = jnp.where(me == 0, far[at, :], ahead)
+                behind = jnp.where(me == WORKERS - 1, far[at, :], behind)
+            table[owner, i, CHUNK_PAIRS:, :] = jnp.concatenate([behind, gap, ahead])
 
     def rows(s, i):
         return table[s // LOCAL_STEPS, i, pl.ds(s % LOCAL_STEPS, PADDED, stride=LOCAL_STEPS), :]
@@ -302,14 +294,14 @@
     sums[...] = jnp.broadcast_to(line, sums.shape)
 
 
-def roll_back(messages, payoff, positions, offsets, one, two, vol, peers):
+def roll_back(messages, payoff, positions, offsets, one, two, far, vol, peers):
     return pl.pallas_call(
         roll_kernel,
         out_shape=(
             jax.ShapeDtypeStruct((VALUES, LANES), jnp.float32),
             jax.ShapeDtypeStruct((peers, LANES), jnp.float32),
         ),
-        in_specs=[vmem()] * (WORKERS + 5) + [smem()],
+        in_specs=[vmem()] * (WORKERS + 6) + [smem()],
         out_specs=(vmem(), vmem()),
         scratch_shapes=[
             pltpu.VMEM((WORKERS, ROWS_PER_STEP, PADDED_PAIRS, LANES), jnp.float32),
@@ -318,7 +310,7 @@
         ],
         compiler_params=params(),
         name="roll_back",
-    )(*messages, payoff, positions, offsets, one, two, vol)
+    )(*messages, payoff, positions, offsets, one, two, far, vol)
 
 
 def build(source, tile_rows, rate, bucket, bump):
@@ -444,20 +436,25 @@
     payoff_rows = payoff.reshape(ROWS, LANES)
     tables = tables.transpose(1, 0, 2).reshape(ROWS_PER_STEP, LOCAL_STEPS, ROWS, LANES)
     tables = tables.transpose(0, 2, 1, 3).reshape(ROWS_PER_STEP, PAIRS, LANES)
-    one, two = edges(tables, payoff_rows, offsets)
+    to_ends = [(2 * groups + i, (i + 1) % groups) for i in range(groups)]
+    to_ends += [(groups + i, 3 * groups + (i + groups - 1) % groups) for i in range(groups)]
+    held, payoff_rows, position_rows, offsets, plus2, one, two, far = first(
+        tables, payoff_rows, positions.reshape(ROWS, LANES), offsets
+    )
+    far = lax.ppermute(far, ALL_AXES, to_ends)
+    from_m2 = lax.ppermute(plus2, "bump", rotated(2))
     one = lax.ppermute(one, NODE_AXES, with_next)
     two = lax.ppermute(two, NODE_AXES, with_last)
-    held, payoff_rows, position_rows = load(tables, payoff_rows, positions.reshape(ROWS, LANES))
-    messages = pack(held, one, two)
+    own, plus1, plus3 = pack_near(held, one, two)
     received = (
-        messages[0],
-        lax.ppermute(messages[1], "bump", rotated(1)),
-        lax.ppermute(messages[2], "bump", rotated(2)),
-        lax.ppermute(messages[3], "bump", rotated(-1)),
+        own,
+        lax.ppermute(plus1, "bump", rotated(1)),
+        from_m2,
+        lax.ppermute(plus3, "bump", rotated(-1)),
     )
     peers = lax.axis_size(ALL_AXES)
     arrays, sums = roll_back(
-        received, payoff_rows, position_rows, offsets, one, two, vol_curve, peers
+        received, payoff_rows, position_rows, offsets, one, two, far, vol_curve, peers
     )
     from_m1 = lax.ppermute(arrays, "bump", rotated(1))
     from_p1 = lax.ppermute(arrays, "bump", rotated(-1))

time: 62.3 us -> 58.7 us (0.942)
  waiting for transfers between devices: 22 us -> 18.2 us
  starting transfers between devices: 29.4 us -> 30.6 us
  Pallas kernels: 9.86 us -> 9.03 us
    ppermute x3 -> x4, starting transfers between devices: 3.32 us -> 6.94 us  [the longest x1 2.91 us: on_device(): from_m2 = lax.ppermute(plus2, 'bump', rotated(2))]
    ppermute x1, starting transfers between devices: 3.41 us -> 0.01 us  [on_device(): from_p1 = lax.ppermute(arrays, 'bump', rotated(-1))]
    ppermute x3 -> x4, waiting for transfers between devices: 13.2 us -> 10.9 us  [the longest x1 10.9 us: on_device(): far = lax.ppermute(far, ALL_AXES, to_ends)]
    ppermute x1, waiting for transfers between devices: 2.23 us -> 0.71 us  [on_device(): two = lax.ppermute(two, NODE_AXES, with_last)]
    ppermute x1, starting transfers between devices: 0.01 us -> 1.46 us  [on_device(): from_m1 = lax.ppermute(arrays, 'bump', rotated(1))]
    pallas_call x3 -> x2, Pallas kernels: 2.38 us -> 1.53 us  [the longest x1 1.45 us: first(): pl.pallas_call(first_kernel, out_shape=same + (message, halo, halo, halo)...]
  transfers between devices with their start and end apart: 10 -> 11, of which waited for: 7 -> 5; matrix products, arithmetic and copies ran while one was open for 0% -> 0% of each run, Pallas kernels for 8% -> 6%
where the time goes in v4:
time: 58.7 us; the launch traced here: 58.6 us
  starting transfers between devices  30.6 us (52%)
  waiting for transfers between devices  18.2 us (31%)
  Pallas kernels  9.03 us (15%)
  between operations  0.77 us (1%)
    all_to_all x1, starting transfers between devices, on_device(): lax.all_to_all(sums.reshape(peers, 1, LANES), ALL_AXES, split_axis=0, con...  15.1 us
    ppermute x1, waiting for transfers between devices, on_device(): far = lax.ppermute(far, ALL_AXES, to_ends)  10.9 us
    ppermute x1, waiting for transfers between devices, on_device(): low = lax.ppermute(from_m1[:HALF], 'bump', rotated(1))  3.48 us
    pallas_call x1, Pallas kernels, roll_back(): pl.pallas_call(roll_kernel, out_shape=(jax.ShapeDtypeStruct((VALUES, LANE...  3.44 us
    ppermute x1, starting transfers between devices, on_device(): one = lax.ppermute(one, NODE_AXES, with_next)  3.33 us
    ppermute x1, starting transfers between devices, on_device(): from_m2 = lax.ppermute(plus2, 'bump', rotated(2))  2.91 us
    ppermute x1, starting transfers between devices, on_device(): high = lax.ppermute(from_p1[HALF:], 'bump', rotated(-1))  2.73 us
    ppermute x1, starting transfers between devices, on_device(): lax.ppermute(plus3, 'bump', rotated(-1))  2.66 us
  transfers between devices with their start and end apart: 11, of which 5 were waited for; matrix products, arithmetic and copies ran while one was open for 0% of the time, Pallas kernels for 6%

profile of v4, /device:TPU:1, one launch (start us, length us, event | category | flops | bytes accessed | tf_op | source)
XLA Modules:
  0.0 58.6 jit_solution(9188225254041130933)
XLA Ops:
  0.6 0.0 copy-start
  0.6 1.5 %first.1 = (f32[5,512,128]{2,1,0:T(8,128)S(1)}, f32[256,128]{1,0:T(8,128)S(1)}, f32[256,128]{1,0:T(8,128)S(1)}, s32[8,128]{1,0:T(8,128)S(1)}, f32[664,128]{1,0:T...) custom-call(f32[5,512,128]{2,1,0:T(8,128)} %bitcast.21, f32[256,128]{1,0:T(8,128)} %bitcast.22, ...), custom_call_target="tpu_custom_call" | custom-call | tf_op jit(solution)/shard_map/first/pallas_call | solution.py:141
  2.1 0.0 copy-start.1
  2.1 0.0 copy-start.2
  2.1 3.3 %collective-permute-start = (f32[24,128]{1,0:T(8,128)S(1)}, f32[24,128]{1,0:T(8,128)S(1)}, u32[]{:S(2)}, u32[]{:S(2)}) collective-permute-start(f32[24,128]{1,0:T(8,128)S(1)} %get-tuple-element.18), channel_id=1, source_target_pairs={{0,1},{1,0},{2,3},{3,2},{4,5},{5,4},{6,7},{7,6},{8,9},{9,8},{10,11... | collective-permute-start | bytes 36872 | tf_op jit(solution)/shard_map/ppermute | solution.py:446
  5.5 1.0 %collective-permute-start.1 = (f32[24,128]{1,0:T(8,128)S(1)}, f32[24,128]{1,0:T(8,128)S(1)}, u32[]{:S(2)}, u32[]{:S(2)}) collective-permute-start(f32[24,128]{1,0:T(8,128)S(1)} %get-tuple-element.19), channel_id=1, source_target_pairs={{0,63},{1,2},{2,1},{3,4},{4,3},{5,6},{6,5},{7,8},{8,7},{9,10},{10,... | collective-permute-start | bytes 36872 | tf_op jit(solution)/shard_map/ppermute | solution.py:447
  6.4 2.9 %collective-permute-start.3 = (f32[664,128]{1,0:T(8,128)S(1)}, f32[664,128]{1,0:T(8,128)S(1)}, u32[]{:S(2)}, u32[]{:S(2)}) collective-permute-start(f32[664,128]{1,0:T(8,128)S(1)} %get-tuple-element.22), channel_id=1, source_target_pairs={{0,128},{64,192},{128,0},{192,64},{1,129},{65,193},{129,1},{193,65... | collective-permute-start | bytes 1019912 | tf_op jit(solution)/shard_map/ppermute | solution.py:445
  9.4 0.0 collective-permute-done.one
  9.4 0.7 %collective-permute-done.1.two = f32[24,128]{1,0:T(8,128)S(1)} collective-permute-done((f32[24,128]{1,0:T(8,128)S(1)}, f32[24,128]{1,0:T(8,128)S(1)}, u32[]{:S(2)}, u32[]{:S(2)}) %collective-permute-start.1) | collective-permute-done | bytes 12320 | tf_op jit(solution)/shard_map/ppermute | solution.py:447
  10.1 0.1 pack.1
  10.2 0.1 collective-permute-start.2
  10.3 2.7 %collective-permute-start.4 = (f32[664,128]{1,0:T(8,128)S(1)}, f32[664,128]{1,0:T(8,128)S(1)}, u32[]{:S(2)}, u32[]{:S(2)}) collective-permute-start(f32[664,128]{1,0:T(8,128)S(1)} %get-tuple-element.23), channel_id=1, source_target_pairs={{0,192},{64,0},{128,64},{192,128},{1,193},{65,1},{129,65},{193,129... | collective-permute-start | bytes 1019912 | tf_op jit(solution)/shard_map/ppermute | solution.py:453
  12.9 1.3 %collective-permute-start.5 = (f32[24,128]{1,0:T(8,128)S(1)}, f32[24,128]{1,0:T(8,128)S(1)}, u32[]{:S(2)}, u32[]{:S(2)}) collective-permute-start(f32[24,128]{1,0:T(8,128)S(1)} %get-tuple-element.27), channel_id=1, source_target_pairs={{128,1},{129,2},{130,3},{131,4},{132,5},{133,6},{134,7},{135,8},{1... | collective-permute-start | bytes 36872 | tf_op jit(solution)/shard_map/ppermute | solution.py:444
  14.2 10.9 %collective-permute-done.5.far = f32[24,128]{1,0:T(8,128)S(1)} collective-permute-done((f32[24,128]{1,0:T(8,128)S(1)}, f32[24,128]{1,0:T(8,128)S(1)}, u32[]{:S(2)}, u32[]{:S(2)}) %collective-permute-start.5) | collective-permute-done | bytes 12320 | tf_op jit(solution)/shard_map/ppermute | solution.py:444
  25.1 0.0 collective-permute-done.3.from_m2
  25.1 0.0 collective-permute-done.2.from_m1
  25.1 0.0 collective-permute-done.4.from_p1
  25.1 0.0 copy-done
  25.1 3.4 %roll_back.1 = (f32[576,128]{1,0:T(8,128)S(1)}, f32[256,128]{1,0:T(8,128)}) custom-call(f32[664,128]{1,0:T(8,128)S(1)} %get-tuple-element.20.own, f32[664,128]{1,0:T(8,128)S(1)} %collective-permute-done.2.from_m1, f32[664,128]{1,0:T(8,128)S(1)} %collective-permute-done.3.from_m2, f32[664,128]{1,0:T(8,128)S(1)} %collective-permute-done.4.from_p1, ...), custom_call_target="tpu_custom_call" | custom-call | tf_op jit(solution)/shard_map/roll_back/pallas_call | solution.py:298
  28.6 0.0 collective-permute-start.8
  28.6 1.5 %collective-permute-start.6 = (f32[576,128]{1,0:T(8,128)S(1)}, f32[576,128]{1,0:T(8,128)S(1)}, u32[]{:S(2)}, u32[]{:S(2)}) collective-permute-start(f32[576,128]{1,0:T(8,128)S(1)} %get-tuple-element.28.own), channel_id=1, source_target_pairs={{0,64},{64,128},{128,192},{192,0},{1,65},{65,129},{129,193},{193,1... | collective-permute-start | bytes 884744 | tf_op jit(solution)/shard_map/ppermute | solution.py:459
  30.0 15.1 %all-to-all-start = ((f32[256,1,128]{2,1,0:T(1,128)}), f32[256,1,128]{2,1,0:T(1,128)S(1)}, u32[]{:S(2)}, u32[]{:S(2)}) async-start(f32[256,1,128]{2,1,0:T(1,128)} %bitcast.10), calls=%async_computation | async-start | bytes 262144 | tf_op jit(solution)/shard_map/all_to_all | solution.py:465
  45.1 0.0 collective-permute-done.8.from_p1
  45.1 2.7 %collective-permute-start.9 = (f32[288,128]{1,0:T(8,128)S(1)}, f32[288,128]{1,0:T(8,128)S(1)}, u32[]{:S(2)}, u32[]{:S(2)}) collective-permute-start(f32[288,128]{1,0:T(8,128)S(1)} %slice.9), channel_id=1, source_target_pairs={{0,192},{64,0},{128,64},{192,128},{1,193},{65,1},{129,65},{193,129... | collective-permute-start | bytes 442376 | tf_op jit(solution)/shard_map/ppermute | solution.py:462
  47.9 0.0 collective-permute-done.6.from_m1
  47.9 0.1 collective-permute-start.7
  48.0 0.0 copy-done.1
  48.0 0.0 copy-done.2
  48.0 1.9 %expand.1.started = f32[2,2048,128]{2,1,0:T(8,128)} custom-call(f32[576,128]{1,0:T(8,128)S(1)} %get-tuple-element.28.own, f32[576,128]{1,0:T(8,128)S(1)} %collective-permute-done.6.from_m1, f32[576,128]{1,0:T(8,128)S(1)} %collective-permute-done.8.from_p1, f32[8]{0:T(128)S(1)} %copy-done, s32[16]{0:T(128)S(1)} %copy-done.1, f32[16]{0:T(128)S(1)} %copy-done.2), custom_call_target="tpu_custom_call" | custom-call | flops 100000000 | bytes 100000000 | tf_op jit(solution)/shard_map/expand/pallas_call | solution.py:362
  49.9 1.3 %collective-permute-done.9.high = f32[288,128]{1,0:T(8,128)S(1)} collective-permute-done((f32[288,128]{1,0:T(8,128)S(1)}, f32[288,128]{1,0:T(8,128)S(1)}, u32[]{:S(2)}, u32[]{:S(2)}) %collective-permute-start.9) | collective-permute-done | bytes 147488 | tf_op jit(solution)/shard_map/ppermute | solution.py:462
  51.2 3.5 %collective-permute-done.7.low = f32[288,128]{1,0:T(8,128)S(1)} collective-permute-done((f32[288,128]{1,0:T(8,128)S(1)}, f32[288,128]{1,0:T(8,128)S(1)}, u32[]{:S(2)}, u32[]{:S(2)}) %collective-permute-start.7) | collective-permute-done | bytes 147488 | tf_op jit(solution)/shard_map/ppermute | solution.py:461
  54.7 1.5 %complete.1 = (f32[2,2048,128]{2,1,0:T(8,128)}, f32[16,128]{1,0:T(8,128)S(1)}) custom-call(f32[288,128]{1,0:T(8,128)S(1)} %collective-permute-done.7.low, f32[288,128]{1,0:T(8,128)S(1)} %collective-permute-done.9.high, f32[8]{0:T(128)S(1)} %copy-done, s32[16]{0:T(128)S(1)} %copy-done.1, f32[16]{0:T(128)S(1)} %copy-done.2, ...), custom_call_target="tpu_custom_call", output_to_operand_aliasing={{0}: (5, {})} | custom-call | flops 100000000 | bytes 100000000 | tf_op jit(solution)/shard_map/complete/pallas_call | solution.py:390
  56.3 1.7 %all-to-all-done = f32[256,1,128]{2,1,0:T(1,128)S(1)} async-done(((f32[256,1,128]{2,1,0:T(1,128)}), f32[256,1,128]{2,1,0:T(1,128)S(1)}, u32[]{:S(2)}, u32[]{:S(2)}) %all-to-all-start) | async-done | bytes 131104 | tf_op jit(solution)/shard_map/all_to_all | solution.py:465
  57.9 0.6 %vegas.1 = f32[1,16]{1,0:T(1,128)} custom-call(f32[256,128]{1,0:T(8,128)S(1)} %bitcast.19, f32[16,128]{1,0:T(8,128)S(1)} %get-tuple-element.31.picks), custom_call_target="tpu_custom_call" | custom-call | tf_op jit(solution)/shard_map/vegas/pallas_call | solution.py:418
  (2 shorter events, 0.0 us)
Async XLA Ops:
  0.6 24.5 %copy-start = (f32[8]{0:T(128)S(1)}, f32[8]{0:T(128)}, u32[]{:S(2)}) copy-start(f32[8]{0:T(128)} %vol.5) | copy-start | bytes 100
  2.1 45.9 %copy-start.1 = (s32[16]{0:T(128)S(1)}, s32[16]{0:T(128)}, u32[]{:S(2)}) copy-start(s32[16]{0:T(128)} %bucket.3) | copy-start | bytes 196
  2.1 45.9 %copy-start.2 = (f32[16]{0:T(128)S(1)}, f32[16]{0:T(128)}, u32[]{:S(2)}) copy-start(f32[16]{0:T(128)} %bump.3) | copy-start | bytes 196
  2.1 7.2 %collective-permute-start = (f32[24,128]{1,0:T(8,128)S(1)}, f32[24,128]{1,0:T(8,128)S(1)}, u32[]{:S(2)}, u32[]{:S(2)}) collective-permute-start(f32[24,128]{1,0:T(8,128)S(1)} %get-tuple-element.18), channel_id=1, source_target_pairs={{0,1},{1,0},{2,3},{3,2},{4,5},{5,4},{6,7},{7,6},{8,9},{9,8},{10,11... | collective-permute-start | bytes 36872 | tf_op jit(solution)/shard_map/ppermute | solution.py:446
  5.5 4.6 %collective-permute-start.1 = (f32[24,128]{1,0:T(8,128)S(1)}, f32[24,128]{1,0:T(8,128)S(1)}, u32[]{:S(2)}, u32[]{:S(2)}) collective-permute-start(f32[24,128]{1,0:T(8,128)S(1)} %get-tuple-element.19), channel_id=1, source_target_pairs={{0,63},{1,2},{2,1},{3,4},{4,3},{5,6},{6,5},{7,8},{8,7},{9,10},{10,... | collective-permute-start | bytes 36872 | tf_op jit(solution)/shard_map/ppermute | solution.py:447
  6.4 18.7 %collective-permute-start.3 = (f32[664,128]{1,0:T(8,128)S(1)}, f32[664,128]{1,0:T(8,128)S(1)}, u32[]{:S(2)}, u32[]{:S(2)}) collective-permute-start(f32[664,128]{1,0:T(8,128)S(1)} %get-tuple-element.22), channel_id=1, source_target_pairs={{0,128},{64,192},{128,0},{192,64},{1,129},{65,193},{129,1},{193,65... | collective-permute-start | bytes 1019912 | tf_op jit(solution)/shard_map/ppermute | solution.py:445
  10.2 15.0 %collective-permute-start.2 = (f32[664,128]{1,0:T(8,128)S(1)}, f32[664,128]{1,0:T(8,128)S(1)}, u32[]{:S(2)}, u32[]{:S(2)}) collective-permute-start(f32[664,128]{1,0:T(8,128)S(1)} %get-tuple-element.21), channel_id=1, source_target_pairs={{0,64},{64,128},{128,192},{192,0},{1,65},{65,129},{129,193},{193,1... | collective-permute-start | bytes 1019912 | tf_op jit(solution)/shard_map/ppermute | solution.py:451
  10.3 14.9 %collective-permute-start.4 = (f32[664,128]{1,0:T(8,128)S(1)}, f32[664,128]{1,0:T(8,128)S(1)}, u32[]{:S(2)}, u32[]{:S(2)}) collective-permute-start(f32[664,128]{1,0:T(8,128)S(1)} %get-tuple-element.23), channel_id=1, source_target_pairs={{0,192},{64,0},{128,64},{192,128},{1,193},{65,1},{129,65},{193,129... | collective-permute-start | bytes 1019912 | tf_op jit(solution)/shard_map/ppermute | solution.py:453
  12.9 12.2 %collective-permute-start.5 = (f32[24,128]{1,0:T(8,128)S(1)}, f32[24,128]{1,0:T(8,128)S(1)}, u32[]{:S(2)}, u32[]{:S(2)}) collective-permute-start(f32[24,128]{1,0:T(8,128)S(1)} %get-tuple-element.27), channel_id=1, source_target_pairs={{128,1},{129,2},{130,3},{131,4},{132,5},{133,6},{134,7},{135,8},{1... | collective-permute-start | bytes 36872 | tf_op jit(solution)/shard_map/ppermute | solution.py:444
  28.6 16.5 %collective-permute-start.8 = (f32[576,128]{1,0:T(8,128)S(1)}, f32[576,128]{1,0:T(8,128)S(1)}, u32[]{:S(2)}, u32[]{:S(2)}) collective-permute-start(f32[576,128]{1,0:T(8,128)S(1)} %get-tuple-element.28.own), channel_id=1, source_target_pairs={{0,192},{64,0},{128,64},{192,128},{1,193},{65,1},{129,65},{193,129... | collective-permute-start | bytes 884744 | tf_op jit(solution)/shard_map/ppermute | solution.py:460
  28.6 19.3 %collective-permute-start.6 = (f32[576,128]{1,0:T(8,128)S(1)}, f32[576,128]{1,0:T(8,128)S(1)}, u32[]{:S(2)}, u32[]{:S(2)}) collective-permute-start(f32[576,128]{1,0:T(8,128)S(1)} %get-tuple-element.28.own), channel_id=1, source_target_pairs={{0,64},{64,128},{128,192},{192,0},{1,65},{65,129},{129,193},{193,1... | collective-permute-start | bytes 884744 | tf_op jit(solution)/shard_map/ppermute | solution.py:459
  30.0 27.9 %all-to-all-start = ((f32[256,1,128]{2,1,0:T(1,128)}), f32[256,1,128]{2,1,0:T(1,128)S(1)}, u32[]{:S(2)}, u32[]{:S(2)}) async-start(f32[256,1,128]{2,1,0:T(1,128)} %bitcast.10), calls=%async_computation | async-start | bytes 262144 | tf_op jit(solution)/shard_map/all_to_all | solution.py:465
  45.1 6.1 %collective-permute-start.9 = (f32[288,128]{1,0:T(8,128)S(1)}, f32[288,128]{1,0:T(8,128)S(1)}, u32[]{:S(2)}, u32[]{:S(2)}) collective-permute-start(f32[288,128]{1,0:T(8,128)S(1)} %slice.9), channel_id=1, source_target_pairs={{0,192},{64,0},{128,64},{192,128},{1,193},{65,1},{129,65},{193,129... | collective-permute-start | bytes 442376 | tf_op jit(solution)/shard_map/ppermute | solution.py:462
  47.9 6.8 %collective-permute-start.7 = (f32[288,128]{1,0:T(8,128)S(1)}, f32[288,128]{1,0:T(8,128)S(1)}, u32[]{:S(2)}, u32[]{:S(2)}) collective-permute-start(f32[288,128]{1,0:T(8,128)S(1)} %slice.8), channel_id=1, source_target_pairs={{0,64},{64,128},{128,192},{192,0},{1,65},{65,129},{129,193},{193,1... | collective-permute-start | bytes 442376 | tf_op jit(solution)/shard_map/ppermute | solution.py:461

commit v5 on v4

--- a/solution.py
+++ b/solution.py
@@ -197,28 +197,9 @@
     return total
 
 
-def roll_kernel(
-    own,
-    from_m1,
-    from_m2,
-    from_p1,
-    payoff,
-    positions,
-    offsets,
-    one,
-    two,
-    far,
-    vol,
-    out,
-    sums,
-    table,
-    steps_k,
-    nodes_k,
-):
+def prepare_kernel(payoff, offsets, one, two, out, nodes_k, steps_k):
     me = lax.axis_index("bump")
     before, after = halos(one, two)
-    sources = (own, from_m1, from_m2, from_p1)
-    turns = (0, WORKERS - 1, WORKERS - 2, 1)
     turned = jnp.transpose(offsets[...].astype(jnp.float32))
     steps_k[8 : 8 + ROWS, :] = jnp.repeat(turned, ROWS // LANES, axis=0)
     steps_k[0:8, :] = jnp.transpose(before[2 * STEPS : HALO, 0:8])
@@ -235,7 +216,7 @@
         nodes_k[s] = jnp.broadcast_to(part[:, s : s + 1], (PADDED, LANES))
     above = payoff[pl.ds(pl.multiple_of(jnp.minimum(start + CHUNK, ROWS - 8), 8), 8), :]
     below = payoff[pl.ds(pl.multiple_of(jnp.maximum(start - 8, 0), 8), 8), :]
-    values = jnp.concatenate(
+    out[...] = jnp.concatenate(
         [
             payoff[pl.ds(start, CHUNK), :],
             jnp.where(me == WORKERS - 1, after[LOCAL_ROWS : LOCAL_ROWS + 1, :], above[0:1, :]),
@@ -243,6 +224,41 @@
             jnp.where(me == 0, before[LOCAL_ROWS : LOCAL_ROWS + 1, :], below[7:8, :]),
         ]
     )
+
+
+def prepare(payoff, offsets, one, two):
+    return pl.pallas_call(
+        prepare_kernel,
+        out_shape=(
+            jax.ShapeDtypeStruct((PADDED, LANES), jnp.float32),
+            jax.ShapeDtypeStruct((STEPS, PADDED, LANES), jnp.float32),
+        ),
+        in_specs=[vmem()] * 4,
+        out_specs=(vmem(), vmem()),
+        scratch_shapes=[pltpu.VMEM((ROWS + 16, STEPS), jnp.float32)],
+        compiler_params=params(),
+        name="prepare",
+    )(payoff, offsets, one, two)
+
+
+def roll_kernel(
+    own,
+    from_m1,
+    from_m2,
+    from_p1,
+    payoff,
+    nodes_k,
+    positions,
+    far,
+    vol,
+    out,
+    sums,
+    table,
+):
+    me = lax.axis_index("bump")
+    sources = (own, from_m1, from_m2, from_p1)
+    turns = (0, WORKERS - 1, WORKERS - 2, 1)
+    start = pl.multiple_of(me * CHUNK, CHUNK)
     gap = jnp.zeros((PADDED_PAIRS - CHUNK_PAIRS - 2 * LOCAL_STEPS, LANES), jnp.float32)
     for k in range(WORKERS):
         owner = lax.rem(me + turns[k], WORKERS)
@@ -263,6 +279,7 @@
         return table[s // LOCAL_STEPS, i, pl.ds(s % LOCAL_STEPS, PADDED, stride=LOCAL_STEPS), :]
 
     lane = lax.broadcasted_iota(jnp.int32, (PADDED, LANES), 1)
+    values = payoff[...]
     slopes = {}
     for s in reversed(range(STEPS)):
         variance = vol[s] * vol[s]
@@ -294,37 +311,33 @@
     sums[...] = jnp.broadcast_to(line, sums.shape)
 
 
-def roll_back(messages, payoff, positions, offsets, one, two, far, vol, peers):
+def roll_back(messages, payoff, nodes_k, positions, far, vol, peers):
     return pl.pallas_call(
         roll_kernel,
         out_shape=(
             jax.ShapeDtypeStruct((VALUES, LANES), jnp.float32),
             jax.ShapeDtypeStruct((peers, LANES), jnp.float32),
         ),
-        in_specs=[vmem()] * (WORKERS + 6) + [smem()],
+        in_specs=[vmem()] * (WORKERS + 4) + [smem()],
         out_specs=(vmem(), vmem()),
         scratch_shapes=[
             pltpu.VMEM((WORKERS, ROWS_PER_STEP, PADDED_PAIRS, LANES), jnp.float32),
-            pltpu.VMEM((ROWS + 16, STEPS), jnp.float32),
-            pltpu.VMEM((STEPS, PADDED, LANES), jnp.float32),
         ],
         compiler_params=params(),
         name="roll_back",
-    )(*messages, payoff, positions, offsets, one, two, far, vol)
-
-
-def build(source, tile_rows, rate, bucket, bump):
+    )(*messages, payoff, nodes_k, positions, far, vol)
+
+
+def build(source, built, out, chunk, rate, bucket, bump, sems):
     base = source[0:CHUNK, :]
-    for b in range(CURVES):
-        gain = bump[b] * rate[b]
-        slope = source[pl.ds(pl.multiple_of((bucket[b] + 1) * CHUNK, CHUNK), CHUNK), :]
-        tile_rows[b // 8, pl.ds(b % 8, CHUNK, stride=8), :] = base + gain * slope
-
-
-def write(built, out, chunk, sems):
+    rows = pl.ds(pl.multiple_of(chunk * CHUNK * 8, CHUNK * 8), CHUNK * 8)
     stores = []
     for tile in range(CURVES // 8):
-        rows = pl.ds(pl.multiple_of(chunk * CHUNK * 8, CHUNK * 8), CHUNK * 8)
+        for r in range(8):
+            b = tile * 8 + r
+            gain = bump[b] * rate[b]
+            slope = source[pl.ds(pl.multiple_of((bucket[b] + 1) * CHUNK, CHUNK), CHUNK), :]
+            built[tile, pl.ds(r, CHUNK, stride=8), :] = base + gain * slope
         stores.append(pltpu.make_async_copy(built.at[tile], out.at[tile, rows, :], sems.at[tile]))
         stores[-1].start()
     return stores
@@ -339,8 +352,8 @@
     rate = rates(vol, bucket, bump)
     stores = []
     for k, (source, turn) in enumerate(parts):
-        build(source, built.at[k], rate, bucket, bump)
-        stores += write(built.at[k], out, lax.rem(me + turn, WORKERS), done.at[k])
+        chunk = lax.rem(me + turn, WORKERS)
+        stores += build(source, built.at[k], out, chunk, rate, bucket, bump, done.at[k])
     for store in stores:
         store.wait()
 
@@ -453,8 +466,9 @@
         lax.ppermute(plus3, "bump", rotated(-1)),
     )
     peers = lax.axis_size(ALL_AXES)
+    payoff_part, nodes_k = prepare(payoff_rows, offsets, one, two)
     arrays, sums = roll_back(
-        received, payoff_rows, position_rows, offsets, one, two, far, vol_curve, peers
+        received, payoff_part, nodes_k, position_rows, far, vol_curve, peers
     )
     from_m1 = lax.ppermute(arrays, "bump", rotated(1))
     from_p1 = lax.ppermute(arrays, "bump", rotated(-1))

time: 58.7 us -> 58.6 us (level)
  no operation moved by 1% of the time
where the time goes in v5:
time: 58.6 us; the launch traced here: 58.4 us
  starting transfers between devices  30.6 us (52%)
  waiting for transfers between devices  18 us (31%)
  Pallas kernels  9.04 us (15%)
  between operations  0.75 us (1%)
    all_to_all x1, starting transfers between devices, on_device(): lax.all_to_all(sums.reshape(peers, 1, LANES), ALL_AXES, split_axis=0, con...  15.1 us
    ppermute x1, waiting for transfers between devices, on_device(): far = lax.ppermute(far, ALL_AXES, to_ends)  10.6 us
    ppermute x1, waiting for transfers between devices, on_device(): low = lax.ppermute(from_m1[:HALF], 'bump', rotated(1))  3.47 us
    ppermute x1, starting transfers between devices, on_device(): one = lax.ppermute(one, NODE_AXES, with_next)  3.33 us
    pallas_call x1, Pallas kernels, roll_back(): pl.pallas_call(roll_kernel, out_shape=(jax.ShapeDtypeStruct((VALUES, LANE...  3.26 us
    ppermute x1, starting transfers between devices, on_device(): from_m2 = lax.ppermute(plus2, 'bump', rotated(2))  2.91 us
    ppermute x1, starting transfers between devices, on_device(): high = lax.ppermute(from_p1[HALF:], 'bump', rotated(-1))  2.73 us
    ppermute x1, starting transfers between devices, on_device(): lax.ppermute(plus3, 'bump', rotated(-1))  2.66 us
  transfers between devices with their start and end apart: 11, of which 5 were waited for; matrix products, arithmetic and copies ran while one was open for 0% of the time, Pallas kernels for 6%

profile of v5, /device:TPU:1, one launch (start us, length us, event | category | flops | bytes accessed | tf_op | source)
XLA Modules:
  0.0 58.4 jit_solution(2203322579520198792)
XLA Ops:
  0.6 0.0 copy-start
  0.6 1.5 %first.1 = (f32[5,512,128]{2,1,0:T(8,128)S(1)}, f32[256,128]{1,0:T(8,128)S(1)}, f32[256,128]{1,0:T(8,128)S(1)}, s32[8,128]{1,0:T(8,128)S(1)}, f32[664,128]{1,0:T...) custom-call(f32[5,512,128]{2,1,0:T(8,128)} %bitcast.21, f32[256,128]{1,0:T(8,128)} %bitcast.22, ...), custom_call_target="tpu_custom_call" | custom-call | tf_op jit(solution)/shard_map/first/pallas_call | solution.py:141
  2.1 3.3 %collective-permute-start = (f32[24,128]{1,0:T(8,128)S(1)}, f32[24,128]{1,0:T(8,128)S(1)}, u32[]{:S(2)}, u32[]{:S(2)}) collective-permute-start(f32[24,128]{1,0:T(8,128)S(1)} %get-tuple-element.20), channel_id=1, source_target_pairs={{0,1},{1,0},{2,3},{3,2},{4,5},{5,4},{6,7},{7,6},{8,9},{9,8},{10,11... | collective-permute-start | bytes 36872 | tf_op jit(solution)/shard_map/ppermute | solution.py:459
  5.4 1.0 %collective-permute-start.1 = (f32[24,128]{1,0:T(8,128)S(1)}, f32[24,128]{1,0:T(8,128)S(1)}, u32[]{:S(2)}, u32[]{:S(2)}) collective-permute-start(f32[24,128]{1,0:T(8,128)S(1)} %get-tuple-element.21), channel_id=1, source_target_pairs={{0,63},{1,2},{2,1},{3,4},{4,3},{5,6},{6,5},{7,8},{8,7},{9,10},{10,... | collective-permute-start | bytes 36872 | tf_op jit(solution)/shard_map/ppermute | solution.py:460
  6.4 2.9 %collective-permute-start.3 = (f32[664,128]{1,0:T(8,128)S(1)}, f32[664,128]{1,0:T(8,128)S(1)}, u32[]{:S(2)}, u32[]{:S(2)}) collective-permute-start(f32[664,128]{1,0:T(8,128)S(1)} %get-tuple-element.24), channel_id=1, source_target_pairs={{0,128},{64,192},{128,0},{192,64},{1,129},{65,193},{129,1},{193,65... | collective-permute-start | bytes 1019912 | tf_op jit(solution)/shard_map/ppermute | solution.py:458
  9.3 0.0 collective-permute-done.one
  9.3 0.7 %collective-permute-done.1.two = f32[24,128]{1,0:T(8,128)S(1)} collective-permute-done((f32[24,128]{1,0:T(8,128)S(1)}, f32[24,128]{1,0:T(8,128)S(1)}, u32[]{:S(2)}, u32[]{:S(2)}) %collective-permute-start.1) | collective-permute-done | bytes 12320 | tf_op jit(solution)/shard_map/ppermute | solution.py:460
  10.1 0.0 copy-start.1
  10.1 0.0 copy-start.2
  10.1 0.1 pack.1
  10.1 0.1 collective-permute-start.2
  10.2 2.7 %collective-permute-start.4 = (f32[664,128]{1,0:T(8,128)S(1)}, f32[664,128]{1,0:T(8,128)S(1)}, u32[]{:S(2)}, u32[]{:S(2)}) collective-permute-start(f32[664,128]{1,0:T(8,128)S(1)} %get-tuple-element.25), channel_id=1, source_target_pairs={{0,192},{64,0},{128,64},{192,128},{1,193},{65,1},{129,65},{193,129... | collective-permute-start | bytes 1019912 | tf_op jit(solution)/shard_map/ppermute | solution.py:466
  12.9 1.3 %collective-permute-start.5 = (f32[24,128]{1,0:T(8,128)S(1)}, f32[24,128]{1,0:T(8,128)S(1)}, u32[]{:S(2)}, u32[]{:S(2)}) collective-permute-start(f32[24,128]{1,0:T(8,128)S(1)} %get-tuple-element.31), channel_id=1, source_target_pairs={{128,1},{129,2},{130,3},{131,4},{132,5},{133,6},{134,7},{135,8},{1... | collective-permute-start | bytes 36872 | tf_op jit(solution)/shard_map/ppermute | solution.py:457
  14.2 0.3 prepare.1
  14.5 10.6 %collective-permute-done.5.far = f32[24,128]{1,0:T(8,128)S(1)} collective-permute-done((f32[24,128]{1,0:T(8,128)S(1)}, f32[24,128]{1,0:T(8,128)S(1)}, u32[]{:S(2)}, u32[]{:S(2)}) %collective-permute-start.5) | collective-permute-done | bytes 12320 | tf_op jit(solution)/shard_map/ppermute | solution.py:457
  25.1 0.0 collective-permute-done.3.from_m2
  25.1 0.0 collective-permute-done.2.from_m1
  25.1 0.0 collective-permute-done.4.from_p1
  25.1 0.0 copy-done
  25.1 3.3 %roll_back.1 = (f32[576,128]{1,0:T(8,128)S(1)}, f32[256,128]{1,0:T(8,128)}) custom-call(f32[664,128]{1,0:T(8,128)S(1)} %get-tuple-element.22.own, f32[664,128]{1,0:T(8,128)S(1)} %collective-permute-done.2.from_m1, f32[664,128]{1,0:T(8,128)S(1)} %collective-permute-done.3.from_m2, f32[664,128]{1,0:T(8,128)S(1)} %collective-permute-done.4.from_p1, ...), custom_call_target="tpu_custom_call" | custom-call | tf_op jit(solution)/shard_map/roll_back/pallas_call | solution.py:315
  28.4 0.0 collective-permute-start.8
  28.4 1.5 %collective-permute-start.6 = (f32[576,128]{1,0:T(8,128)S(1)}, f32[576,128]{1,0:T(8,128)S(1)}, u32[]{:S(2)}, u32[]{:S(2)}) collective-permute-start(f32[576,128]{1,0:T(8,128)S(1)} %get-tuple-element.32.own), channel_id=1, source_target_pairs={{0,64},{64,128},{128,192},{192,0},{1,65},{65,129},{129,193},{193,1... | collective-permute-start | bytes 884744 | tf_op jit(solution)/shard_map/ppermute | solution.py:473
  29.8 15.1 %all-to-all-start = ((f32[256,1,128]{2,1,0:T(1,128)}), f32[256,1,128]{2,1,0:T(1,128)S(1)}, u32[]{:S(2)}, u32[]{:S(2)}) async-start(f32[256,1,128]{2,1,0:T(1,128)} %bitcast.10), calls=%async_computation | async-start | bytes 262144 | tf_op jit(solution)/shard_map/all_to_all | solution.py:479
  44.9 0.0 collective-permute-done.8.from_p1
  44.9 2.7 %collective-permute-start.9 = (f32[288,128]{1,0:T(8,128)S(1)}, f32[288,128]{1,0:T(8,128)S(1)}, u32[]{:S(2)}, u32[]{:S(2)}) collective-permute-start(f32[288,128]{1,0:T(8,128)S(1)} %slice.9), channel_id=1, source_target_pairs={{0,192},{64,0},{128,64},{192,128},{1,193},{65,1},{129,65},{193,129... | collective-permute-start | bytes 442376 | tf_op jit(solution)/shard_map/ppermute | solution.py:476
  47.7 0.0 collective-permute-done.6.from_m1
  47.7 0.1 collective-permute-start.7
  47.8 0.0 copy-done.1
  47.8 0.0 copy-done.2
  47.8 1.8 %expand.1.started = f32[2,2048,128]{2,1,0:T(8,128)} custom-call(f32[576,128]{1,0:T(8,128)S(1)} %get-tuple-element.32.own, f32[576,128]{1,0:T(8,128)S(1)} %collective-permute-done.6.from_m1, f32[576,128]{1,0:T(8,128)S(1)} %collective-permute-done.8.from_p1, f32[8]{0:T(128)S(1)} %copy-done, s32[16]{0:T(128)S(1)} %copy-done.1, f32[16]{0:T(128)S(1)} %copy-done.2), custom_call_target="tpu_custom_call" | custom-call | flops 100000000 | bytes 100000000 | tf_op jit(solution)/shard_map/expand/pallas_call | solution.py:375
  49.6 1.4 %collective-permute-done.9.high = f32[288,128]{1,0:T(8,128)S(1)} collective-permute-done((f32[288,128]{1,0:T(8,128)S(1)}, f32[288,128]{1,0:T(8,128)S(1)}, u32[]{:S(2)}, u32[]{:S(2)}) %collective-permute-start.9) | collective-permute-done | bytes 147488 | tf_op jit(solution)/shard_map/ppermute | solution.py:476
  51.0 3.5 %collective-permute-done.7.low = f32[288,128]{1,0:T(8,128)S(1)} collective-permute-done((f32[288,128]{1,0:T(8,128)S(1)}, f32[288,128]{1,0:T(8,128)S(1)}, u32[]{:S(2)}, u32[]{:S(2)}) %collective-permute-start.7) | collective-permute-done | bytes 147488 | tf_op jit(solution)/shard_map/ppermute | solution.py:475
  54.5 1.5 %complete.1 = (f32[2,2048,128]{2,1,0:T(8,128)}, f32[16,128]{1,0:T(8,128)S(1)}) custom-call(f32[288,128]{1,0:T(8,128)S(1)} %collective-permute-done.7.low, f32[288,128]{1,0:T(8,128)S(1)} %collective-permute-done.9.high, f32[8]{0:T(128)S(1)} %copy-done, s32[16]{0:T(128)S(1)} %copy-done.1, f32[16]{0:T(128)S(1)} %copy-done.2, ...), custom_call_target="tpu_custom_call", output_to_operand_aliasing={{0}: (5, {})} | custom-call | flops 100000000 | bytes 100000000 | tf_op jit(solution)/shard_map/complete/pallas_call | solution.py:403
  56.0 1.8 %all-to-all-done = f32[256,1,128]{2,1,0:T(1,128)S(1)} async-done(((f32[256,1,128]{2,1,0:T(1,128)}), f32[256,1,128]{2,1,0:T(1,128)S(1)}, u32[]{:S(2)}, u32[]{:S(2)}) %all-to-all-start) | async-done | bytes 131104 | tf_op jit(solution)/shard_map/all_to_all | solution.py:479
  57.8 0.6 %vegas.1 = f32[1,16]{1,0:T(1,128)} custom-call(f32[256,128]{1,0:T(8,128)S(1)} %bitcast.19, f32[16,128]{1,0:T(8,128)S(1)} %get-tuple-element.35.picks), custom_call_target="tpu_custom_call" | custom-call | tf_op jit(solution)/shard_map/vegas/pallas_call | solution.py:431
  (2 shorter events, 0.0 us)
Async XLA Ops:
  0.6 24.5 %copy-start = (f32[8]{0:T(128)S(1)}, f32[8]{0:T(128)}, u32[]{:S(2)}) copy-start(f32[8]{0:T(128)} %vol.5) | copy-start | bytes 100
  2.1 7.2 %collective-permute-start = (f32[24,128]{1,0:T(8,128)S(1)}, f32[24,128]{1,0:T(8,128)S(1)}, u32[]{:S(2)}, u32[]{:S(2)}) collective-permute-start(f32[24,128]{1,0:T(8,128)S(1)} %get-tuple-element.20), channel_id=1, source_target_pairs={{0,1},{1,0},{2,3},{3,2},{4,5},{5,4},{6,7},{7,6},{8,9},{9,8},{10,11... | collective-permute-start | bytes 36872 | tf_op jit(solution)/shard_map/ppermute | solution.py:459
  5.4 4.6 %collective-permute-start.1 = (f32[24,128]{1,0:T(8,128)S(1)}, f32[24,128]{1,0:T(8,128)S(1)}, u32[]{:S(2)}, u32[]{:S(2)}) collective-permute-start(f32[24,128]{1,0:T(8,128)S(1)} %get-tuple-element.21), channel_id=1, source_target_pairs={{0,63},{1,2},{2,1},{3,4},{4,3},{5,6},{6,5},{7,8},{8,7},{9,10},{10,... | collective-permute-start | bytes 36872 | tf_op jit(solution)/shard_map/ppermute | solution.py:460
  6.4 18.7 %collective-permute-start.3 = (f32[664,128]{1,0:T(8,128)S(1)}, f32[664,128]{1,0:T(8,128)S(1)}, u32[]{:S(2)}, u32[]{:S(2)}) collective-permute-start(f32[664,128]{1,0:T(8,128)S(1)} %get-tuple-element.24), channel_id=1, source_target_pairs={{0,128},{64,192},{128,0},{192,64},{1,129},{65,193},{129,1},{193,65... | collective-permute-start | bytes 1019912 | tf_op jit(solution)/shard_map/ppermute | solution.py:458
  10.1 37.7 %copy-start.1 = (s32[16]{0:T(128)S(1)}, s32[16]{0:T(128)}, u32[]{:S(2)}) copy-start(s32[16]{0:T(128)} %bucket.3) | copy-start | bytes 196
  10.1 37.7 %copy-start.2 = (f32[16]{0:T(128)S(1)}, f32[16]{0:T(128)}, u32[]{:S(2)}) copy-start(f32[16]{0:T(128)} %bump.3) | copy-start | bytes 196
  10.1 15.0 %collective-permute-start.2 = (f32[664,128]{1,0:T(8,128)S(1)}, f32[664,128]{1,0:T(8,128)S(1)}, u32[]{:S(2)}, u32[]{:S(2)}) collective-permute-start(f32[664,128]{1,0:T(8,128)S(1)} %get-tuple-element.23), channel_id=1, source_target_pairs={{0,64},{64,128},{128,192},{192,0},{1,65},{65,129},{129,193},{193,1... | collective-permute-start | bytes 1019912 | tf_op jit(solution)/shard_map/ppermute | solution.py:464
  10.2 14.9 %collective-permute-start.4 = (f32[664,128]{1,0:T(8,128)S(1)}, f32[664,128]{1,0:T(8,128)S(1)}, u32[]{:S(2)}, u32[]{:S(2)}) collective-permute-start(f32[664,128]{1,0:T(8,128)S(1)} %get-tuple-element.25), channel_id=1, source_target_pairs={{0,192},{64,0},{128,64},{192,128},{1,193},{65,1},{129,65},{193,129... | collective-permute-start | bytes 1019912 | tf_op jit(solution)/shard_map/ppermute | solution.py:466
  12.9 12.2 %collective-permute-start.5 = (f32[24,128]{1,0:T(8,128)S(1)}, f32[24,128]{1,0:T(8,128)S(1)}, u32[]{:S(2)}, u32[]{:S(2)}) collective-permute-start(f32[24,128]{1,0:T(8,128)S(1)} %get-tuple-element.31), channel_id=1, source_target_pairs={{128,1},{129,2},{130,3},{131,4},{132,5},{133,6},{134,7},{135,8},{1... | collective-permute-start | bytes 36872 | tf_op jit(solution)/shard_map/ppermute | solution.py:457
  28.4 16.5 %collective-permute-start.8 = (f32[576,128]{1,0:T(8,128)S(1)}, f32[576,128]{1,0:T(8,128)S(1)}, u32[]{:S(2)}, u32[]{:S(2)}) collective-permute-start(f32[576,128]{1,0:T(8,128)S(1)} %get-tuple-element.32.own), channel_id=1, source_target_pairs={{0,192},{64,0},{128,64},{192,128},{1,193},{65,1},{129,65},{193,129... | collective-permute-start | bytes 884744 | tf_op jit(solution)/shard_map/ppermute | solution.py:474
  28.4 19.3 %collective-permute-start.6 = (f32[576,128]{1,0:T(8,128)S(1)}, f32[576,128]{1,0:T(8,128)S(1)}, u32[]{:S(2)}, u32[]{:S(2)}) collective-permute-start(f32[576,128]{1,0:T(8,128)S(1)} %get-tuple-element.32.own), channel_id=1, source_target_pairs={{0,64},{64,128},{128,192},{192,0},{1,65},{65,129},{129,193},{193,1... | collective-permute-start | bytes 884744 | tf_op jit(solution)/shard_map/ppermute | solution.py:473
  29.8 27.9 %all-to-all-start = ((f32[256,1,128]{2,1,0:T(1,128)}), f32[256,1,128]{2,1,0:T(1,128)S(1)}, u32[]{:S(2)}, u32[]{:S(2)}) async-start(f32[256,1,128]{2,1,0:T(1,128)} %bitcast.10), calls=%async_computation | async-start | bytes 262144 | tf_op jit(solution)/shard_map/all_to_all | solution.py:479
  44.9 6.1 %collective-permute-start.9 = (f32[288,128]{1,0:T(8,128)S(1)}, f32[288,128]{1,0:T(8,128)S(1)}, u32[]{:S(2)}, u32[]{:S(2)}) collective-permute-start(f32[288,128]{1,0:T(8,128)S(1)} %slice.9), channel_id=1, source_target_pairs={{0,192},{64,0},{128,64},{192,128},{1,193},{65,1},{129,65},{193,129... | collective-permute-start | bytes 442376 | tf_op jit(solution)/shard_map/ppermute | solution.py:476
  47.7 6.8 %collective-permute-start.7 = (f32[288,128]{1,0:T(8,128)S(1)}, f32[288,128]{1,0:T(8,128)S(1)}, u32[]{:S(2)}, u32[]{:S(2)}) collective-permute-start(f32[288,128]{1,0:T(8,128)S(1)} %slice.8), channel_id=1, source_target_pairs={{0,64},{64,128},{128,192},{192,0},{1,65},{65,129},{129,193},{193,1... | collective-permute-start | bytes 442376 | tf_op jit(solution)/shard_map/ppermute | solution.py:475

commit v6 on v4

--- a/solution.py
+++ b/solution.py
@@ -338,15 +338,15 @@
     me = lax.axis_index("bump")
     rate = rates(vol, bucket, bump)
     stores = []
-    for k, (source, turn) in enumerate(parts):
+    for k, (source, flip) in enumerate(parts):
         build(source, built.at[k], rate, bucket, bump)
-        stores += write(built.at[k], out, lax.rem(me + turn, WORKERS), done.at[k])
+        stores += write(built.at[k], out, lax.bitwise_xor(me, flip), done.at[k])
     for store in stores:
         store.wait()
 
 
-def expand_kernel(own, from_m1, from_p1, vol, bucket, bump, out, built, done):
-    parts = ((own, 0), (from_m1, WORKERS - 1), (from_p1, 1))
+def expand_kernel(own, from_1, from_3, vol, bucket, bump, out, built, done):
+    parts = ((own, 0), (from_1, 1), (from_3, 3))
     expand_chunks(parts, vol, bucket, bump, out, built, done)
 
 
@@ -358,7 +358,7 @@
     ]
 
 
-def expand(own, from_m1, from_p1, vol, bucket, bump):
+def expand(own, from_1, from_3, vol, bucket, bump):
     return pl.pallas_call(
         expand_kernel,
         out_shape=jax.ShapeDtypeStruct((CURVES // 8, ROWS * 8, LANES), jnp.float32),
@@ -368,7 +368,7 @@
         compiler_params=params(),
         cost_estimate=EXPAND_COST,
         name="expand",
-    )(own, from_m1, from_p1, vol, bucket, bump)
+    )(own, from_1, from_3, vol, bucket, bump)
 
 
 def complete_kernel(low, high, vol, bucket, bump, started, out, picks, joined, built, done):
@@ -382,7 +382,7 @@
     picks[...] = pick
     joined[0:HALF, :] = low[...]
     joined[HALF:, :] = high[...]
-    expand_chunks(((joined, WORKERS - 2),), vol, bucket, bump, out, built, done)
+    expand_chunks(((joined, 2),), vol, bucket, bump, out, built, done)
 
 
 def complete(low, high, vol, bucket, bump, started):
@@ -456,11 +456,12 @@
     arrays, sums = roll_back(
         received, payoff_rows, position_rows, offsets, one, two, far, vol_curve, peers
     )
-    from_m1 = lax.ppermute(arrays, "bump", rotated(1))
-    from_p1 = lax.ppermute(arrays, "bump", rotated(-1))
-    low = lax.ppermute(from_m1[:HALF], "bump", rotated(1))
-    high = lax.ppermute(from_p1[HALF:], "bump", rotated(-1))
-    started = expand(arrays, from_m1, from_p1, vol_curve, bucket, bump_size)
+    pairs = {flip: [(i, i ^ flip) for i in range(WORKERS)] for flip in (1, 3)}
+    from_1 = lax.ppermute(arrays, "bump", pairs[1])
+    from_3 = lax.ppermute(arrays, "bump", pairs[3])
+    low = lax.ppermute(from_3[:HALF], "bump", pairs[1])
+    high = lax.ppermute(from_1[HALF:], "bump", pairs[3])
+    started = expand(arrays, from_1, from_3, vol_curve, bucket, bump_size)
     bumped_values, picks = complete(low, high, vol_curve, bucket, bump_size, started)
     shared = lax.all_to_all(
         sums.reshape(peers, 1, LANES), ALL_AXES, split_axis=0, concat_axis=0, tiled=True

time: 58.7 us -> 57.2 us (0.974)
  starting transfers between devices: 30.6 us -> 29.1 us
    ppermute x4, waiting for transfers between devices: 4.83 us -> 3.63 us  [the longest x1 2.29 us: on_device(): low = lax.ppermute(from_3[:HALF], 'bump', pairs[1])]
    all_to_all x1, waiting for transfers between devices: 1.69 us -> 2.88 us  [on_device(): lax.all_to_all(sums.reshape(peers, 1, LANES), ALL_AXES, split_axis=0, con...]
    all_to_all x1, starting transfers between devices: 15.1 us -> 14.1 us  [on_device(): lax.all_to_all(sums.reshape(peers, 1, LANES), ALL_AXES, split_axis=0, con...]
where the time goes in v6:
time: 57.2 us; the launch traced here: 57.1 us
  starting transfers between devices  29.1 us (51%)
  waiting for transfers between devices  18.1 us (32%)
  Pallas kernels  9.03 us (16%)
  between operations  0.77 us (1%)
    all_to_all x1, starting transfers between devices, on_device(): lax.all_to_all(sums.reshape(peers, 1, LANES), ALL_AXES, split_axis=0, con...  14.1 us
    ppermute x1, waiting for transfers between devices, on_device(): far = lax.ppermute(far, ALL_AXES, to_ends)  10.9 us
    pallas_call x1, Pallas kernels, roll_back(): pl.pallas_call(roll_kernel, out_shape=(jax.ShapeDtypeStruct((VALUES, LANE...  3.44 us
    ppermute x1, starting transfers between devices, on_device(): one = lax.ppermute(one, NODE_AXES, with_next)  3.33 us
    ppermute x1, starting transfers between devices, on_device(): from_m2 = lax.ppermute(plus2, 'bump', rotated(2))  2.91 us
    all_to_all x1, waiting for transfers between devices, on_device(): lax.all_to_all(sums.reshape(peers, 1, LANES), ALL_AXES, split_axis=0, con...  2.88 us
    ppermute x1, starting transfers between devices, on_device(): high = lax.ppermute(from_1[HALF:], 'bump', pairs[3])  2.74 us
    ppermute x1, starting transfers between devices, on_device(): lax.ppermute(plus3, 'bump', rotated(-1))  2.66 us
  transfers between devices with their start and end apart: 11, of which 5 were waited for; matrix products, arithmetic and copies ran while one was open for 0% of the time, Pallas kernels for 6%

profile of v6, /device:TPU:1, one launch (start us, length us, event | category | flops | bytes accessed | tf_op | source)
XLA Modules:
  0.0 57.1 jit_solution(17460283867671640553)
XLA Ops:
  0.6 0.0 copy-start
  0.6 1.5 %first.1 = (f32[5,512,128]{2,1,0:T(8,128)S(1)}, f32[256,128]{1,0:T(8,128)S(1)}, f32[256,128]{1,0:T(8,128)S(1)}, s32[8,128]{1,0:T(8,128)S(1)}, f32[664,128]{1,0:T...) custom-call(f32[5,512,128]{2,1,0:T(8,128)} %bitcast.21, f32[256,128]{1,0:T(8,128)} %bitcast.22, ...), custom_call_target="tpu_custom_call" | custom-call | tf_op jit(solution)/shard_map/first/pallas_call | solution.py:141
  2.1 0.0 copy-start.1
  2.1 0.0 copy-start.2
  2.1 3.3 %collective-permute-start = (f32[24,128]{1,0:T(8,128)S(1)}, f32[24,128]{1,0:T(8,128)S(1)}, u32[]{:S(2)}, u32[]{:S(2)}) collective-permute-start(f32[24,128]{1,0:T(8,128)S(1)} %get-tuple-element.18), channel_id=1, source_target_pairs={{0,1},{1,0},{2,3},{3,2},{4,5},{5,4},{6,7},{7,6},{8,9},{9,8},{10,11... | collective-permute-start | bytes 36872 | tf_op jit(solution)/shard_map/ppermute | solution.py:446
  5.5 1.0 %collective-permute-start.1 = (f32[24,128]{1,0:T(8,128)S(1)}, f32[24,128]{1,0:T(8,128)S(1)}, u32[]{:S(2)}, u32[]{:S(2)}) collective-permute-start(f32[24,128]{1,0:T(8,128)S(1)} %get-tuple-element.19), channel_id=1, source_target_pairs={{0,63},{1,2},{2,1},{3,4},{4,3},{5,6},{6,5},{7,8},{8,7},{9,10},{10,... | collective-permute-start | bytes 36872 | tf_op jit(solution)/shard_map/ppermute | solution.py:447
  6.4 2.9 %collective-permute-start.3 = (f32[664,128]{1,0:T(8,128)S(1)}, f32[664,128]{1,0:T(8,128)S(1)}, u32[]{:S(2)}, u32[]{:S(2)}) collective-permute-start(f32[664,128]{1,0:T(8,128)S(1)} %get-tuple-element.22), channel_id=1, source_target_pairs={{0,128},{64,192},{128,0},{192,64},{1,129},{65,193},{129,1},{193,65... | collective-permute-start | bytes 1019912 | tf_op jit(solution)/shard_map/ppermute | solution.py:445
  9.4 0.0 collective-permute-done.one
  9.4 0.7 %collective-permute-done.1.two = f32[24,128]{1,0:T(8,128)S(1)} collective-permute-done((f32[24,128]{1,0:T(8,128)S(1)}, f32[24,128]{1,0:T(8,128)S(1)}, u32[]{:S(2)}, u32[]{:S(2)}) %collective-permute-start.1) | collective-permute-done | bytes 12320 | tf_op jit(solution)/shard_map/ppermute | solution.py:447
  10.1 0.1 pack.1
  10.2 0.1 collective-permute-start.2
  10.3 2.7 %collective-permute-start.4 = (f32[664,128]{1,0:T(8,128)S(1)}, f32[664,128]{1,0:T(8,128)S(1)}, u32[]{:S(2)}, u32[]{:S(2)}) collective-permute-start(f32[664,128]{1,0:T(8,128)S(1)} %get-tuple-element.23), channel_id=1, source_target_pairs={{0,192},{64,0},{128,64},{192,128},{1,193},{65,1},{129,65},{193,129... | collective-permute-start | bytes 1019912 | tf_op jit(solution)/shard_map/ppermute | solution.py:453
  12.9 1.3 %collective-permute-start.5 = (f32[24,128]{1,0:T(8,128)S(1)}, f32[24,128]{1,0:T(8,128)S(1)}, u32[]{:S(2)}, u32[]{:S(2)}) collective-permute-start(f32[24,128]{1,0:T(8,128)S(1)} %get-tuple-element.27), channel_id=1, source_target_pairs={{128,1},{129,2},{130,3},{131,4},{132,5},{133,6},{134,7},{135,8},{1... | collective-permute-start | bytes 36872 | tf_op jit(solution)/shard_map/ppermute | solution.py:444
  14.2 10.9 %collective-permute-done.5.far = f32[24,128]{1,0:T(8,128)S(1)} collective-permute-done((f32[24,128]{1,0:T(8,128)S(1)}, f32[24,128]{1,0:T(8,128)S(1)}, u32[]{:S(2)}, u32[]{:S(2)}) %collective-permute-start.5) | collective-permute-done | bytes 12320 | tf_op jit(solution)/shard_map/ppermute | solution.py:444
  25.1 0.0 collective-permute-done.3.from_m2
  25.1 0.0 collective-permute-done.2.from_m1
  25.1 0.0 collective-permute-done.4.from_p1
  25.1 0.0 copy-done
  25.1 3.4 %roll_back.1 = (f32[576,128]{1,0:T(8,128)S(1)}, f32[256,128]{1,0:T(8,128)}) custom-call(f32[664,128]{1,0:T(8,128)S(1)} %get-tuple-element.20.own, f32[664,128]{1,0:T(8,128)S(1)} %collective-permute-done.2.from_m1, f32[664,128]{1,0:T(8,128)S(1)} %collective-permute-done.3.from_m2, f32[664,128]{1,0:T(8,128)S(1)} %collective-permute-done.4.from_p1, ...), custom_call_target="tpu_custom_call" | custom-call | tf_op jit(solution)/shard_map/roll_back/pallas_call | solution.py:298
  28.6 0.0 collective-permute-start.8
  28.6 0.9 %collective-permute-start.6 = (f32[576,128]{1,0:T(8,128)S(1)}, f32[576,128]{1,0:T(8,128)S(1)}, u32[]{:S(2)}, u32[]{:S(2)}) collective-permute-start(f32[576,128]{1,0:T(8,128)S(1)} %get-tuple-element.28.own), channel_id=1, source_target_pairs={{0,192},{64,128},{128,64},{192,0},{1,193},{65,129},{129,65},{193,1... | collective-permute-start | bytes 884744 | tf_op jit(solution)/shard_map/ppermute | solution.py:461
  29.5 14.1 %all-to-all-start = ((f32[256,1,128]{2,1,0:T(1,128)}), f32[256,1,128]{2,1,0:T(1,128)S(1)}, u32[]{:S(2)}, u32[]{:S(2)}) async-start(f32[256,1,128]{2,1,0:T(1,128)} %bitcast.10), calls=%async_computation | async-start | bytes 262144 | tf_op jit(solution)/shard_map/all_to_all | solution.py:466
  43.6 0.0 collective-permute-done.8.from_1
  43.6 2.7 %collective-permute-start.9 = (f32[288,128]{1,0:T(8,128)S(1)}, f32[288,128]{1,0:T(8,128)S(1)}, u32[]{:S(2)}, u32[]{:S(2)}) collective-permute-start(f32[288,128]{1,0:T(8,128)S(1)} %slice.9), channel_id=1, source_target_pairs={{0,192},{64,128},{128,64},{192,0},{1,193},{65,129},{129,65},{193,1... | collective-permute-start | bytes 442376 | tf_op jit(solution)/shard_map/ppermute | solution.py:463
  46.3 0.0 collective-permute-done.6.from_3
  46.4 0.1 collective-permute-start.7
  46.5 0.0 copy-done.1
  46.5 0.0 copy-done.2
  46.5 1.9 %expand.1.started = f32[2,2048,128]{2,1,0:T(8,128)} custom-call(f32[576,128]{1,0:T(8,128)S(1)} %get-tuple-element.28.own, f32[576,128]{1,0:T(8,128)S(1)} %collective-permute-done.8.from_1, f32[576,128]{1,0:T(8,128)S(1)} %collective-permute-done.6.from_3, f32[8]{0:T(128)S(1)} %copy-done, s32[16]{0:T(128)S(1)} %copy-done.1, f32[16]{0:T(128)S(1)} %copy-done.2), custom_call_target="tpu_custom_call" | custom-call | flops 100000000 | bytes 100000000 | tf_op jit(solution)/shard_map/expand/pallas_call | solution.py:362
  48.4 1.3 %collective-permute-done.9.high = f32[288,128]{1,0:T(8,128)S(1)} collective-permute-done((f32[288,128]{1,0:T(8,128)S(1)}, f32[288,128]{1,0:T(8,128)S(1)}, u32[]{:S(2)}, u32[]{:S(2)}) %collective-permute-start.9) | collective-permute-done | bytes 147488 | tf_op jit(solution)/shard_map/ppermute | solution.py:463
  49.7 2.3 %collective-permute-done.7.low = f32[288,128]{1,0:T(8,128)S(1)} collective-permute-done((f32[288,128]{1,0:T(8,128)S(1)}, f32[288,128]{1,0:T(8,128)S(1)}, u32[]{:S(2)}, u32[]{:S(2)}) %collective-permute-start.7) | collective-permute-done | bytes 147488 | tf_op jit(solution)/shard_map/ppermute | solution.py:462
  52.0 1.5 %complete.1 = (f32[2,2048,128]{2,1,0:T(8,128)}, f32[16,128]{1,0:T(8,128)S(1)}) custom-call(f32[288,128]{1,0:T(8,128)S(1)} %collective-permute-done.7.low, f32[288,128]{1,0:T(8,128)S(1)} %collective-permute-done.9.high, f32[8]{0:T(128)S(1)} %copy-done, s32[16]{0:T(128)S(1)} %copy-done.1, f32[16]{0:T(128)S(1)} %copy-done.2, ...), custom_call_target="tpu_custom_call", output_to_operand_aliasing={{0}: (5, {})} | custom-call | flops 100000000 | bytes 100000000 | tf_op jit(solution)/shard_map/complete/pallas_call | solution.py:390
  53.5 2.9 %all-to-all-done = f32[256,1,128]{2,1,0:T(1,128)S(1)} async-done(((f32[256,1,128]{2,1,0:T(1,128)}), f32[256,1,128]{2,1,0:T(1,128)S(1)}, u32[]{:S(2)}, u32[]{:S(2)}) %all-to-all-start) | async-done | bytes 131104 | tf_op jit(solution)/shard_map/all_to_all | solution.py:466
  56.4 0.6 %vegas.1 = f32[1,16]{1,0:T(1,128)} custom-call(f32[256,128]{1,0:T(8,128)S(1)} %bitcast.19, f32[16,128]{1,0:T(8,128)S(1)} %get-tuple-element.31.picks), custom_call_target="tpu_custom_call" | custom-call | tf_op jit(solution)/shard_map/vegas/pallas_call | solution.py:418
  (2 shorter events, 0.0 us)
Async XLA Ops:
  0.6 24.5 %copy-start = (f32[8]{0:T(128)S(1)}, f32[8]{0:T(128)}, u32[]{:S(2)}) copy-start(f32[8]{0:T(128)} %vol.5) | copy-start | bytes 100
  2.1 44.4 %copy-start.1 = (s32[16]{0:T(128)S(1)}, s32[16]{0:T(128)}, u32[]{:S(2)}) copy-start(s32[16]{0:T(128)} %bucket.3) | copy-start | bytes 196
  2.1 44.4 %copy-start.2 = (f32[16]{0:T(128)S(1)}, f32[16]{0:T(128)}, u32[]{:S(2)}) copy-start(f32[16]{0:T(128)} %bump.3) | copy-start | bytes 196
  2.1 7.2 %collective-permute-start = (f32[24,128]{1,0:T(8,128)S(1)}, f32[24,128]{1,0:T(8,128)S(1)}, u32[]{:S(2)}, u32[]{:S(2)}) collective-permute-start(f32[24,128]{1,0:T(8,128)S(1)} %get-tuple-element.18), channel_id=1, source_target_pairs={{0,1},{1,0},{2,3},{3,2},{4,5},{5,4},{6,7},{7,6},{8,9},{9,8},{10,11... | collective-permute-start | bytes 36872 | tf_op jit(solution)/shard_map/ppermute | solution.py:446
  5.5 4.6 %collective-permute-start.1 = (f32[24,128]{1,0:T(8,128)S(1)}, f32[24,128]{1,0:T(8,128)S(1)}, u32[]{:S(2)}, u32[]{:S(2)}) collective-permute-start(f32[24,128]{1,0:T(8,128)S(1)} %get-tuple-element.19), channel_id=1, source_target_pairs={{0,63},{1,2},{2,1},{3,4},{4,3},{5,6},{6,5},{7,8},{8,7},{9,10},{10,... | collective-permute-start | bytes 36872 | tf_op jit(solution)/shard_map/ppermute | solution.py:447
  6.4 18.7 %collective-permute-start.3 = (f32[664,128]{1,0:T(8,128)S(1)}, f32[664,128]{1,0:T(8,128)S(1)}, u32[]{:S(2)}, u32[]{:S(2)}) collective-permute-start(f32[664,128]{1,0:T(8,128)S(1)} %get-tuple-element.22), channel_id=1, source_target_pairs={{0,128},{64,192},{128,0},{192,64},{1,129},{65,193},{129,1},{193,65... | collective-permute-start | bytes 1019912 | tf_op jit(solution)/shard_map/ppermute | solution.py:445
  10.2 15.0 %collective-permute-start.2 = (f32[664,128]{1,0:T(8,128)S(1)}, f32[664,128]{1,0:T(8,128)S(1)}, u32[]{:S(2)}, u32[]{:S(2)}) collective-permute-start(f32[664,128]{1,0:T(8,128)S(1)} %get-tuple-element.21), channel_id=1, source_target_pairs={{0,64},{64,128},{128,192},{192,0},{1,65},{65,129},{129,193},{193,1... | collective-permute-start | bytes 1019912 | tf_op jit(solution)/shard_map/ppermute | solution.py:451
  10.3 14.9 %collective-permute-start.4 = (f32[664,128]{1,0:T(8,128)S(1)}, f32[664,128]{1,0:T(8,128)S(1)}, u32[]{:S(2)}, u32[]{:S(2)}) collective-permute-start(f32[664,128]{1,0:T(8,128)S(1)} %get-tuple-element.23), channel_id=1, source_target_pairs={{0,192},{64,0},{128,64},{192,128},{1,193},{65,1},{129,65},{193,129... | collective-permute-start | bytes 1019912 | tf_op jit(solution)/shard_map/ppermute | solution.py:453
  12.9 12.2 %collective-permute-start.5 = (f32[24,128]{1,0:T(8,128)S(1)}, f32[24,128]{1,0:T(8,128)S(1)}, u32[]{:S(2)}, u32[]{:S(2)}) collective-permute-start(f32[24,128]{1,0:T(8,128)S(1)} %get-tuple-element.27), channel_id=1, source_target_pairs={{128,1},{129,2},{130,3},{131,4},{132,5},{133,6},{134,7},{135,8},{1... | collective-permute-start | bytes 36872 | tf_op jit(solution)/shard_map/ppermute | solution.py:444
  28.6 15.0 %collective-permute-start.8 = (f32[576,128]{1,0:T(8,128)S(1)}, f32[576,128]{1,0:T(8,128)S(1)}, u32[]{:S(2)}, u32[]{:S(2)}) collective-permute-start(f32[576,128]{1,0:T(8,128)S(1)} %get-tuple-element.28.own), channel_id=1, source_target_pairs={{0,64},{64,0},{128,192},{192,128},{1,65},{65,1},{129,193},{193,129... | collective-permute-start | bytes 884744 | tf_op jit(solution)/shard_map/ppermute | solution.py:460
  28.6 17.8 %collective-permute-start.6 = (f32[576,128]{1,0:T(8,128)S(1)}, f32[576,128]{1,0:T(8,128)S(1)}, u32[]{:S(2)}, u32[]{:S(2)}) collective-permute-start(f32[576,128]{1,0:T(8,128)S(1)} %get-tuple-element.28.own), channel_id=1, source_target_pairs={{0,192},{64,128},{128,64},{192,0},{1,193},{65,129},{129,65},{193,1... | collective-permute-start | bytes 884744 | tf_op jit(solution)/shard_map/ppermute | solution.py:461
  29.5 26.9 %all-to-all-start = ((f32[256,1,128]{2,1,0:T(1,128)}), f32[256,1,128]{2,1,0:T(1,128)S(1)}, u32[]{:S(2)}, u32[]{:S(2)}) async-start(f32[256,1,128]{2,1,0:T(1,128)} %bitcast.10), calls=%async_computation | async-start | bytes 262144 | tf_op jit(solution)/shard_map/all_to_all | solution.py:466
  43.6 6.1 %collective-permute-start.9 = (f32[288,128]{1,0:T(8,128)S(1)}, f32[288,128]{1,0:T(8,128)S(1)}, u32[]{:S(2)}, u32[]{:S(2)}) collective-permute-start(f32[288,128]{1,0:T(8,128)S(1)} %slice.9), channel_id=1, source_target_pairs={{0,192},{64,128},{128,64},{192,0},{1,193},{65,129},{129,65},{193,1... | collective-permute-start | bytes 442376 | tf_op jit(solution)/shard_map/ppermute | solution.py:463
  46.4 5.6 %collective-permute-start.7 = (f32[288,128]{1,0:T(8,128)S(1)}, f32[288,128]{1,0:T(8,128)S(1)}, u32[]{:S(2)}, u32[]{:S(2)}) collective-permute-start(f32[288,128]{1,0:T(8,128)S(1)} %slice.8), channel_id=1, source_target_pairs={{0,64},{64,0},{128,192},{192,128},{1,65},{65,1},{129,193},{193,129... | collective-permute-start | bytes 442376 | tf_op jit(solution)/shard_map/ppermute | solution.py:462

commit v7 on v6

--- a/solution.py
+++ b/solution.py
@@ -69,7 +69,7 @@
 
 
 def pack_one(tables, k, out, before, after):
-    chunk = lax.rem(lax.axis_index("bump") + k, WORKERS)
+    chunk = lax.bitwise_xor(lax.axis_index("bump"), k)
     start = pl.multiple_of(chunk * CHUNK_PAIRS, CHUNK_PAIRS)
     low = pl.multiple_of(lax.rem(start + PAIRS - 8, PAIRS), 8)
     high = pl.multiple_of(lax.rem(start + CHUNK_PAIRS, PAIRS), CHUNK_PAIRS)
@@ -218,7 +218,6 @@
     me = lax.axis_index("bump")
     before, after = halos(one, two)
     sources = (own, from_m1, from_m2, from_p1)
-    turns = (0, WORKERS - 1, WORKERS - 2, 1)
     turned = jnp.transpose(offsets[...].astype(jnp.float32))
     steps_k[8 : 8 + ROWS, :] = jnp.repeat(turned, ROWS // LANES, axis=0)
     steps_k[0:8, :] = jnp.transpose(before[2 * STEPS : HALO, 0:8])
@@ -245,7 +244,7 @@
     )
     gap = jnp.zeros((PADDED_PAIRS - CHUNK_PAIRS - 2 * LOCAL_STEPS, LANES), jnp.float32)
     for k in range(WORKERS):
-        owner = lax.rem(me + turns[k], WORKERS)
+        owner = lax.bitwise_xor(me, k)
         source = sources[k]
         for i in range(ROWS_PER_STEP):
             table[owner, i, :CHUNK_PAIRS, :] = source[i * CHUNK_PAIRS : (i + 1) * CHUNK_PAIRS, :]
@@ -448,9 +447,9 @@
     own, plus1, plus3 = pack_near(held, one, two)
     received = (
         own,
-        lax.ppermute(plus1, "bump", rotated(1)),
+        lax.ppermute(plus1, "bump", [(i, i ^ 1) for i in range(WORKERS)]),
         from_m2,
-        lax.ppermute(plus3, "bump", rotated(-1)),
+        lax.ppermute(plus3, "bump", [(i, i ^ 3) for i in range(WORKERS)]),
     )
     peers = lax.axis_size(ALL_AXES)
     arrays, sums = roll_back(

time: 57.2 us -> 57.2 us (level)
  starting transfers between devices: 29.1 us -> 27.9 us
  waiting for transfers between devices: 18.1 us -> 19.3 us
    ppermute x2, starting transfers between devices: 2.75 us -> 1.54 us  [the longest x1 1.45 us: on_device(): lax.ppermute(plus3, 'bump', [(i, i ^ 3) for i in range(WORKERS)])]
    ppermute x1, waiting for transfers between devices: 10.9 us -> 12.1 us  [on_device(): far = lax.ppermute(far, ALL_AXES, to_ends)]
    all_to_all x1, starting transfers between devices: 14.1 us -> 14.7 us  [on_device(): lax.all_to_all(sums.reshape(peers, 1, LANES), ALL_AXES, split_axis=0, con...]
    ppermute x1, starting transfers between devices: 0.91 us -> 0.31 us  [on_device(): from_3 = lax.ppermute(arrays, 'bump', pairs[3])]
where the time goes in v7:
time: 57.2 us; the launch traced here: 57.1 us
  starting transfers between devices  27.9 us (49%)
  waiting for transfers between devices  19.3 us (34%)
  Pallas kernels  9.04 us (16%)
  between operations  0.77 us (1%)
    all_to_all x1, starting transfers between devices, on_device(): lax.all_to_all(sums.reshape(peers, 1, LANES), ALL_AXES, split_axis=0, con...  14.7 us
    ppermute x1, waiting for transfers between devices, on_device(): far = lax.ppermute(far, ALL_AXES, to_ends)  12.1 us
    pallas_call x1, Pallas kernels, roll_back(): pl.pallas_call(roll_kernel, out_shape=(jax.ShapeDtypeStruct((VALUES, LANE...  3.45 us
    ppermute x1, starting transfers between devices, on_device(): one = lax.ppermute(one, NODE_AXES, with_next)  3.33 us
    ppermute x1, starting transfers between devices, on_device(): from_m2 = lax.ppermute(plus2, 'bump', rotated(2))  2.91 us
    all_to_all x1, waiting for transfers between devices, on_device(): lax.all_to_all(sums.reshape(peers, 1, LANES), ALL_AXES, split_axis=0, con...  2.88 us
    ppermute x1, starting transfers between devices, on_device(): high = lax.ppermute(from_1[HALF:], 'bump', pairs[3])  2.74 us
    ppermute x1, waiting for transfers between devices, on_device(): low = lax.ppermute(from_3[:HALF], 'bump', pairs[1])  2.29 us
  transfers between devices with their start and end apart: 11, of which 5 were waited for; matrix products, arithmetic and copies ran while one was open for 0% of the time, Pallas kernels for 6%

profile of v7, /device:TPU:1, one launch (start us, length us, event | category | flops | bytes accessed | tf_op | source)
XLA Modules:
  0.0 57.1 jit_solution(11427406088251787292)
XLA Ops:
  0.6 0.0 copy-start
  0.6 1.5 %first.1 = (f32[5,512,128]{2,1,0:T(8,128)S(1)}, f32[256,128]{1,0:T(8,128)S(1)}, f32[256,128]{1,0:T(8,128)S(1)}, s32[8,128]{1,0:T(8,128)S(1)}, f32[664,128]{1,0:T...) custom-call(f32[5,512,128]{2,1,0:T(8,128)} %bitcast.21, f32[256,128]{1,0:T(8,128)} %bitcast.22, ...), custom_call_target="tpu_custom_call" | custom-call | tf_op jit(solution)/shard_map/first/pallas_call | solution.py:141
  2.1 0.0 copy-start.1
  2.1 0.0 copy-start.2
  2.1 3.3 %collective-permute-start = (f32[24,128]{1,0:T(8,128)S(1)}, f32[24,128]{1,0:T(8,128)S(1)}, u32[]{:S(2)}, u32[]{:S(2)}) collective-permute-start(f32[24,128]{1,0:T(8,128)S(1)} %get-tuple-element.18), channel_id=1, source_target_pairs={{0,1},{1,0},{2,3},{3,2},{4,5},{5,4},{6,7},{7,6},{8,9},{9,8},{10,11... | collective-permute-start | bytes 36872 | tf_op jit(solution)/shard_map/ppermute | solution.py:445
  5.5 1.0 %collective-permute-start.1 = (f32[24,128]{1,0:T(8,128)S(1)}, f32[24,128]{1,0:T(8,128)S(1)}, u32[]{:S(2)}, u32[]{:S(2)}) collective-permute-start(f32[24,128]{1,0:T(8,128)S(1)} %get-tuple-element.19), channel_id=1, source_target_pairs={{0,63},{1,2},{2,1},{3,4},{4,3},{5,6},{6,5},{7,8},{8,7},{9,10},{10,... | collective-permute-start | bytes 36872 | tf_op jit(solution)/shard_map/ppermute | solution.py:446
  6.4 2.9 %collective-permute-start.3 = (f32[664,128]{1,0:T(8,128)S(1)}, f32[664,128]{1,0:T(8,128)S(1)}, u32[]{:S(2)}, u32[]{:S(2)}) collective-permute-start(f32[664,128]{1,0:T(8,128)S(1)} %get-tuple-element.22), channel_id=1, source_target_pairs={{0,128},{64,192},{128,0},{192,64},{1,129},{65,193},{129,1},{193,65... | collective-permute-start | bytes 1019912 | tf_op jit(solution)/shard_map/ppermute | solution.py:444
  9.4 0.0 collective-permute-done.one
  9.4 0.7 %collective-permute-done.1.two = f32[24,128]{1,0:T(8,128)S(1)} collective-permute-done((f32[24,128]{1,0:T(8,128)S(1)}, f32[24,128]{1,0:T(8,128)S(1)}, u32[]{:S(2)}, u32[]{:S(2)}) %collective-permute-start.1) | collective-permute-done | bytes 12320 | tf_op jit(solution)/shard_map/ppermute | solution.py:446
  10.1 0.1 pack.1
  10.2 0.1 collective-permute-start.2
  10.3 1.4 %collective-permute-start.4 = (f32[664,128]{1,0:T(8,128)S(1)}, f32[664,128]{1,0:T(8,128)S(1)}, u32[]{:S(2)}, u32[]{:S(2)}) collective-permute-start(f32[664,128]{1,0:T(8,128)S(1)} %get-tuple-element.23), channel_id=1, source_target_pairs={{0,192},{64,128},{128,64},{192,0},{1,193},{65,129},{129,65},{193,1... | collective-permute-start | bytes 1019912 | tf_op jit(solution)/shard_map/ppermute | solution.py:452
  11.7 1.3 %collective-permute-start.5 = (f32[24,128]{1,0:T(8,128)S(1)}, f32[24,128]{1,0:T(8,128)S(1)}, u32[]{:S(2)}, u32[]{:S(2)}) collective-permute-start(f32[24,128]{1,0:T(8,128)S(1)} %get-tuple-element.27), channel_id=1, source_target_pairs={{128,1},{129,2},{130,3},{131,4},{132,5},{133,6},{134,7},{135,8},{1... | collective-permute-start | bytes 36872 | tf_op jit(solution)/shard_map/ppermute | solution.py:443
  13.0 12.1 %collective-permute-done.5.far = f32[24,128]{1,0:T(8,128)S(1)} collective-permute-done((f32[24,128]{1,0:T(8,128)S(1)}, f32[24,128]{1,0:T(8,128)S(1)}, u32[]{:S(2)}, u32[]{:S(2)}) %collective-permute-start.5) | collective-permute-done | bytes 12320 | tf_op jit(solution)/shard_map/ppermute | solution.py:443
  25.1 0.0 collective-permute-done.3.from_m2
  25.1 0.0 collective-permute-done.2.from_m1
  25.1 0.0 collective-permute-done.4.from_p1
  25.1 0.0 copy-done
  25.1 3.5 %roll_back.1 = (f32[576,128]{1,0:T(8,128)S(1)}, f32[256,128]{1,0:T(8,128)}) custom-call(f32[664,128]{1,0:T(8,128)S(1)} %get-tuple-element.20.own, f32[664,128]{1,0:T(8,128)S(1)} %collective-permute-done.2.from_m1, f32[664,128]{1,0:T(8,128)S(1)} %collective-permute-done.3.from_m2, f32[664,128]{1,0:T(8,128)S(1)} %collective-permute-done.4.from_p1, ...), custom_call_target="tpu_custom_call" | custom-call | tf_op jit(solution)/shard_map/roll_back/pallas_call | solution.py:297
  28.5 0.0 collective-permute-start.8
  28.5 0.3 collective-permute-start.6
  28.9 14.7 %all-to-all-start = ((f32[256,1,128]{2,1,0:T(1,128)}), f32[256,1,128]{2,1,0:T(1,128)S(1)}, u32[]{:S(2)}, u32[]{:S(2)}) async-start(f32[256,1,128]{2,1,0:T(1,128)} %bitcast.10), calls=%async_computation | async-start | bytes 262144 | tf_op jit(solution)/shard_map/all_to_all | solution.py:465
  43.6 0.0 collective-permute-done.8.from_1
  43.6 2.7 %collective-permute-start.9 = (f32[288,128]{1,0:T(8,128)S(1)}, f32[288,128]{1,0:T(8,128)S(1)}, u32[]{:S(2)}, u32[]{:S(2)}) collective-permute-start(f32[288,128]{1,0:T(8,128)S(1)} %slice.9), channel_id=1, source_target_pairs={{0,192},{64,128},{128,64},{192,0},{1,193},{65,129},{129,65},{193,1... | collective-permute-start | bytes 442376 | tf_op jit(solution)/shard_map/ppermute | solution.py:462
  46.4 0.0 collective-permute-done.6.from_3
  46.4 0.1 collective-permute-start.7
  46.5 0.0 copy-done.1
  46.5 0.0 copy-done.2
  46.5 1.9 %expand.1.started = f32[2,2048,128]{2,1,0:T(8,128)} custom-call(f32[576,128]{1,0:T(8,128)S(1)} %get-tuple-element.28.own, f32[576,128]{1,0:T(8,128)S(1)} %collective-permute-done.8.from_1, f32[576,128]{1,0:T(8,128)S(1)} %collective-permute-done.6.from_3, f32[8]{0:T(128)S(1)} %copy-done, s32[16]{0:T(128)S(1)} %copy-done.1, f32[16]{0:T(128)S(1)} %copy-done.2), custom_call_target="tpu_custom_call" | custom-call | flops 100000000 | bytes 100000000 | tf_op jit(solution)/shard_map/expand/pallas_call | solution.py:361
  48.4 1.3 %collective-permute-done.9.high = f32[288,128]{1,0:T(8,128)S(1)} collective-permute-done((f32[288,128]{1,0:T(8,128)S(1)}, f32[288,128]{1,0:T(8,128)S(1)}, u32[]{:S(2)}, u32[]{:S(2)}) %collective-permute-start.9) | collective-permute-done | bytes 147488 | tf_op jit(solution)/shard_map/ppermute | solution.py:462
  49.7 2.3 %collective-permute-done.7.low = f32[288,128]{1,0:T(8,128)S(1)} collective-permute-done((f32[288,128]{1,0:T(8,128)S(1)}, f32[288,128]{1,0:T(8,128)S(1)}, u32[]{:S(2)}, u32[]{:S(2)}) %collective-permute-start.7) | collective-permute-done | bytes 147488 | tf_op jit(solution)/shard_map/ppermute | solution.py:461
  52.0 1.5 %complete.1 = (f32[2,2048,128]{2,1,0:T(8,128)}, f32[16,128]{1,0:T(8,128)S(1)}) custom-call(f32[288,128]{1,0:T(8,128)S(1)} %collective-permute-done.7.low, f32[288,128]{1,0:T(8,128)S(1)} %collective-permute-done.9.high, f32[8]{0:T(128)S(1)} %copy-done, s32[16]{0:T(128)S(1)} %copy-done.1, f32[16]{0:T(128)S(1)} %copy-done.2, ...), custom_call_target="tpu_custom_call", output_to_operand_aliasing={{0}: (5, {})} | custom-call | flops 100000000 | bytes 100000000 | tf_op jit(solution)/shard_map/complete/pallas_call | solution.py:389
  53.6 2.9 %all-to-all-done = f32[256,1,128]{2,1,0:T(1,128)S(1)} async-done(((f32[256,1,128]{2,1,0:T(1,128)}), f32[256,1,128]{2,1,0:T(1,128)S(1)}, u32[]{:S(2)}, u32[]{:S(2)}) %all-to-all-start) | async-done | bytes 131104 | tf_op jit(solution)/shard_map/all_to_all | solution.py:465
  56.4 0.6 %vegas.1 = f32[1,16]{1,0:T(1,128)} custom-call(f32[256,128]{1,0:T(8,128)S(1)} %bitcast.19, f32[16,128]{1,0:T(8,128)S(1)} %get-tuple-element.31.picks), custom_call_target="tpu_custom_call" | custom-call | tf_op jit(solution)/shard_map/vegas/pallas_call | solution.py:417
  (2 shorter events, 0.0 us)
Async XLA Ops:
  0.6 24.5 %copy-start = (f32[8]{0:T(128)S(1)}, f32[8]{0:T(128)}, u32[]{:S(2)}) copy-start(f32[8]{0:T(128)} %vol.5) | copy-start | bytes 100
  2.1 44.4 %copy-start.1 = (s32[16]{0:T(128)S(1)}, s32[16]{0:T(128)}, u32[]{:S(2)}) copy-start(s32[16]{0:T(128)} %bucket.3) | copy-start | bytes 196
  2.1 44.4 %copy-start.2 = (f32[16]{0:T(128)S(1)}, f32[16]{0:T(128)}, u32[]{:S(2)}) copy-start(f32[16]{0:T(128)} %bump.3) | copy-start | bytes 196
  2.1 7.2 %collective-permute-start = (f32[24,128]{1,0:T(8,128)S(1)}, f32[24,128]{1,0:T(8,128)S(1)}, u32[]{:S(2)}, u32[]{:S(2)}) collective-permute-start(f32[24,128]{1,0:T(8,128)S(1)} %get-tuple-element.18), channel_id=1, source_target_pairs={{0,1},{1,0},{2,3},{3,2},{4,5},{5,4},{6,7},{7,6},{8,9},{9,8},{10,11... | collective-permute-start | bytes 36872 | tf_op jit(solution)/shard_map/ppermute | solution.py:445
  5.5 4.6 %collective-permute-start.1 = (f32[24,128]{1,0:T(8,128)S(1)}, f32[24,128]{1,0:T(8,128)S(1)}, u32[]{:S(2)}, u32[]{:S(2)}) collective-permute-start(f32[24,128]{1,0:T(8,128)S(1)} %get-tuple-element.19), channel_id=1, source_target_pairs={{0,63},{1,2},{2,1},{3,4},{4,3},{5,6},{6,5},{7,8},{8,7},{9,10},{10,... | collective-permute-start | bytes 36872 | tf_op jit(solution)/shard_map/ppermute | solution.py:446
  6.4 18.6 %collective-permute-start.3 = (f32[664,128]{1,0:T(8,128)S(1)}, f32[664,128]{1,0:T(8,128)S(1)}, u32[]{:S(2)}, u32[]{:S(2)}) collective-permute-start(f32[664,128]{1,0:T(8,128)S(1)} %get-tuple-element.22), channel_id=1, source_target_pairs={{0,128},{64,192},{128,0},{192,64},{1,129},{65,193},{129,1},{193,65... | collective-permute-start | bytes 1019912 | tf_op jit(solution)/shard_map/ppermute | solution.py:444
  10.2 14.9 %collective-permute-start.2 = (f32[664,128]{1,0:T(8,128)S(1)}, f32[664,128]{1,0:T(8,128)S(1)}, u32[]{:S(2)}, u32[]{:S(2)}) collective-permute-start(f32[664,128]{1,0:T(8,128)S(1)} %get-tuple-element.21), channel_id=1, source_target_pairs={{0,64},{64,0},{128,192},{192,128},{1,65},{65,1},{129,193},{193,129... | collective-permute-start | bytes 1019912 | tf_op jit(solution)/shard_map/ppermute | solution.py:450
  10.3 14.8 %collective-permute-start.4 = (f32[664,128]{1,0:T(8,128)S(1)}, f32[664,128]{1,0:T(8,128)S(1)}, u32[]{:S(2)}, u32[]{:S(2)}) collective-permute-start(f32[664,128]{1,0:T(8,128)S(1)} %get-tuple-element.23), channel_id=1, source_target_pairs={{0,192},{64,128},{128,64},{192,0},{1,193},{65,129},{129,65},{193,1... | collective-permute-start | bytes 1019912 | tf_op jit(solution)/shard_map/ppermute | solution.py:452
  11.7 13.4 %collective-permute-start.5 = (f32[24,128]{1,0:T(8,128)S(1)}, f32[24,128]{1,0:T(8,128)S(1)}, u32[]{:S(2)}, u32[]{:S(2)}) collective-permute-start(f32[24,128]{1,0:T(8,128)S(1)} %get-tuple-element.27), channel_id=1, source_target_pairs={{128,1},{129,2},{130,3},{131,4},{132,5},{133,6},{134,7},{135,8},{1... | collective-permute-start | bytes 36872 | tf_op jit(solution)/shard_map/ppermute | solution.py:443
  28.5 15.1 %collective-permute-start.8 = (f32[576,128]{1,0:T(8,128)S(1)}, f32[576,128]{1,0:T(8,128)S(1)}, u32[]{:S(2)}, u32[]{:S(2)}) collective-permute-start(f32[576,128]{1,0:T(8,128)S(1)} %get-tuple-element.28.own), channel_id=1, source_target_pairs={{0,64},{64,0},{128,192},{192,128},{1,65},{65,1},{129,193},{193,129... | collective-permute-start | bytes 884744 | tf_op jit(solution)/shard_map/ppermute | solution.py:459
  28.5 17.8 %collective-permute-start.6 = (f32[576,128]{1,0:T(8,128)S(1)}, f32[576,128]{1,0:T(8,128)S(1)}, u32[]{:S(2)}, u32[]{:S(2)}) collective-permute-start(f32[576,128]{1,0:T(8,128)S(1)} %get-tuple-element.28.own), channel_id=1, source_target_pairs={{0,192},{64,128},{128,64},{192,0},{1,193},{65,129},{129,65},{193,1... | collective-permute-start | bytes 884744 | tf_op jit(solution)/shard_map/ppermute | solution.py:460
  28.9 27.6 %all-to-all-start = ((f32[256,1,128]{2,1,0:T(1,128)}), f32[256,1,128]{2,1,0:T(1,128)S(1)}, u32[]{:S(2)}, u32[]{:S(2)}) async-start(f32[256,1,128]{2,1,0:T(1,128)} %bitcast.10), calls=%async_computation | async-start | bytes 262144 | tf_op jit(solution)/shard_map/all_to_all | solution.py:465
  43.6 6.1 %collective-permute-start.9 = (f32[288,128]{1,0:T(8,128)S(1)}, f32[288,128]{1,0:T(8,128)S(1)}, u32[]{:S(2)}, u32[]{:S(2)}) collective-permute-start(f32[288,128]{1,0:T(8,128)S(1)} %slice.9), channel_id=1, source_target_pairs={{0,192},{64,128},{128,64},{192,0},{1,193},{65,129},{129,65},{193,1... | collective-permute-start | bytes 442376 | tf_op jit(solution)/shard_map/ppermute | solution.py:462
  46.4 5.6 %collective-permute-start.7 = (f32[288,128]{1,0:T(8,128)S(1)}, f32[288,128]{1,0:T(8,128)S(1)}, u32[]{:S(2)}, u32[]{:S(2)}) collective-permute-start(f32[288,128]{1,0:T(8,128)S(1)} %slice.8), channel_id=1, source_target_pairs={{0,64},{64,0},{128,192},{192,128},{1,65},{65,1},{129,193},{193,129... | collective-permute-start | bytes 442376 | tf_op jit(solution)/shard_map/ppermute | solution.py:461
